TPU v7x, 32 devices: a whole 2x2x4 slice. The times are simulated.
32 devices in a mesh: seq: 8 (over y, x, core), fsdp: 4 (over z).
Axes of the slice: x: 2, y: 2, z: 4, core: 2. Of those that a mesh axis runs over, the one named last changes fastest.
Arguments:
- tokens: bfloat16 [4096, 4096], P('seq'), may hold values from -6 to 6
- w_in: bfloat16 [4096, 3072], P('seq', 'fsdp'), may hold values from -0.09375 to 0.09375
- step_logit: float32 [4096, 16], P('seq', 'fsdp'), may hold values from -7 to -5.5
- decay_logit: float32 [4096, 16], P('seq', 'fsdp'), may hold values from -20 to 1
- cotangent: bfloat16 [4096, 2048], P('seq', 'fsdp'), may hold values from -0.375 to 0.375
Outputs:
- layer_out: float32 [4096, 2048], P('seq', 'fsdp')
- input_grad: bfloat16 [4096, 4096], P('fsdp', 'seq')
- w_in_grad: float32 [4096, 3072], P('seq', 'fsdp')
All inputs are finite; a program needn't handle non-finite values.
Results may differ from a plain program's by a relative error of at most 0.017.
Values may be sent and summed in bfloat16 or wider, within the bound.
No kernel may reach another device: no remote copies, remote signals or barrier semaphores. Data moves between devices by JAX's collectives and lax.ppermute only.
A program may use at most 128 MiB of HBM per device.

v0:
```python
import jax
import jax.numpy as jnp
from jax import lax
from jax.sharding import PartitionSpec as P

HEAD_DIM = 128
STATE = 128
HEADS_DEV = 4
BLOCK = 128


def entering(shard, axis, combine, identity, reverse):
    devices, index = (lax.axis_size(axis), lax.axis_index(axis))
    everything = jax.tree.map(
        lambda part, kind: lax.all_gather(part.astype(kind), axis),
        shard,
        (jnp.bfloat16, jnp.bfloat16),
    )
    start = jax.tree.map(
        lambda part, zero: jnp.broadcast_to(jnp.asarray(zero, part.dtype), part.shape),
        shard,
        identity,
    )

    def step(k, before):
        at = devices - 1 - k if reverse else k
        reached = at > index if reverse else at < index
        new = combine(
            before, jax.tree.map(lambda part, own: part[at].astype(own.dtype), everything, shard)
        )
        return jax.tree.map(lambda a, b: jnp.where(reached, a, b), new, before)

    return lax.fori_loop(0, devices, step, start)


def block_step(memory, inputs):
    values, in_map, out_map, step_size, log_decay = inputs
    cum_decay = jnp.cumsum(log_decay, axis=0)
    scores = jnp.einsum("tgn,sgn->gts", out_map, in_map, preferred_element_type=jnp.float32)
    along = jnp.moveaxis(cum_decay, 0, -1)
    steps_along = jnp.moveaxis(step_size, 0, -1)
    span = along.shape[-1]
    causal = lax.broadcasted_iota(jnp.int32, (span, span), 0) >= lax.broadcasted_iota(
        jnp.int32, (span, span), 1
    )
    decays = jnp.exp(jnp.where(causal, along[..., :, None] - along[..., None, :], -1e30))
    mixing = (scores[:, None] * decays * steps_along[..., None, :]).astype(jnp.bfloat16)
    local_out = jnp.einsum("ghts,sghp->tghp", mixing, values, preferred_element_type=jnp.float32)
    carried = jnp.einsum(
        "tgn,ghnp->tghp", out_map.astype(jnp.float32), memory, precision=lax.Precision.HIGHEST
    )
    outputs = local_out + jnp.exp(cum_decay)[..., None] * carried
    block_total = cum_decay[-1]
    weight_end = jnp.exp(block_total[None] - cum_decay) * step_size
    scaled_in = (in_map.astype(jnp.float32)[:, :, None, :] * weight_end[..., None]).astype(
        jnp.bfloat16
    )
    written = jnp.einsum("sghn,sghp->ghnp", scaled_in, values, preferred_element_type=jnp.float32)
    return (jnp.exp(block_total)[..., None, None] * memory + written, outputs)


def run_blocks(projected, step_size, log_decay, groups):
    rows = projected.shape[0]
    block_count = rows // BLOCK
    width = HEADS_DEV * HEAD_DIM
    grouped = projected.reshape(rows, groups, width + 2 * STATE)
    values = grouped[:, :, :width].reshape(block_count, BLOCK, groups, HEADS_DEV, HEAD_DIM)
    in_map = grouped[:, :, width : width + STATE].reshape(block_count, BLOCK, groups, STATE)
    out_map = grouped[:, :, width + STATE :].reshape(block_count, BLOCK, groups, STATE)
    steps_blocked = step_size.reshape(block_count, BLOCK, groups, HEADS_DEV)
    decay_blocked = log_decay.reshape(block_count, BLOCK, groups, HEADS_DEV)
    empty_state = jnp.zeros((groups, HEADS_DEV, STATE, HEAD_DIM), jnp.float32)
    final_state, outputs = lax.scan(
        block_step, empty_state, (values, in_map, out_map, steps_blocked, decay_blocked)
    )
    return (outputs.reshape(rows, groups * width), final_state)


def combine(earlier, latter):
    return (earlier[0] + latter[0], jnp.exp(latter[0])[:, None, None] * earlier[1] + latter[1])


def shards(tokens, w_in, step_logit, decay_logit, cotangent):
    width = HEADS_DEV * HEAD_DIM
    gathered = lax.all_gather(w_in, "seq", axis=0, tiled=True)
    projected = jnp.dot(tokens, gathered, preferred_element_type=jnp.float32).astype(jnp.bfloat16)
    step_size = jax.nn.softplus(step_logit)
    log_decay = -jax.nn.softplus(decay_logit)
    cum_decay = jnp.cumsum(log_decay, axis=0)
    log_total = cum_decay[-1]

    def mixer(proj_in):
        return run_blocks(proj_in, step_size, log_decay, 1)

    (zero_out, zero_end), pullback = jax.vjp(mixer, projected)
    end_local = zero_end[0]
    identity = (jnp.zeros_like(log_total), jnp.zeros_like(end_local))
    _, incoming = entering((log_total, end_local), "seq", combine, identity, False)
    out_map = projected[:, width + STATE :].astype(jnp.float32)
    growth = jnp.exp(cum_decay)
    carried = jnp.einsum("tn,hnp->thp", out_map, incoming, precision=lax.Precision.HIGHEST)
    layer_out = zero_out + (growth[..., None] * carried).reshape(zero_out.shape)
    out_grad = cotangent.astype(jnp.float32)
    scaled_grad = growth[..., None] * out_grad.reshape(out_grad.shape[0], HEADS_DEV, HEAD_DIM)
    state_grad = jnp.einsum("tn,thp->hnp", out_map, scaled_grad, precision=lax.Precision.HIGHEST)
    _, outgoing = entering((log_total, state_grad), "seq", combine, identity, True)
    (zero_grad,) = pullback((out_grad, outgoing[None]))
    extra_grad = jnp.einsum("thp,hnp->tn", scaled_grad, incoming, precision=lax.Precision.HIGHEST)
    zero_grad = zero_grad.astype(jnp.float32)
    proj_grad = jnp.concatenate(
        [zero_grad[:, : width + STATE], zero_grad[:, width + STATE :] + extra_grad], axis=1
    ).astype(jnp.bfloat16)
    input_grad = lax.psum_scatter(
        lax.dot_general(
            gathered, proj_grad, (((1,), (1,)), ((), ())), preferred_element_type=jnp.float32
        ).astype(jnp.bfloat16),
        "fsdp",
        scatter_dimension=0,
        tiled=True,
    )
    w_in_grad = lax.psum_scatter(
        lax.dot_general(
            tokens, proj_grad, (((0,), (0,)), ((), ())), preferred_element_type=jnp.float32
        ).astype(jnp.bfloat16),
        "seq",
        scatter_dimension=0,
        tiled=True,
    ).astype(jnp.float32)
    return (layer_out, input_grad, w_in_grad)


def solution(mesh):
    in_specs = (
        P("seq", None),
        P("seq", "fsdp"),
        P("seq", "fsdp"),
        P("seq", "fsdp"),
        P("seq", "fsdp"),
    )
    out_specs = (P("seq", "fsdp"), P("fsdp", "seq"), P("seq", "fsdp"))
    return jax.shard_map(shards, mesh=mesh, in_specs=in_specs, out_specs=out_specs, check_vma=False)
```

profile of v0, /device:TPU:0, one launch (start us, length us, event | category | flops | bytes accessed | tf_op | source)
XLA Modules:
  0.0 335.2 jit_solution(9455065704548673268)
XLA Ops:
  10.6 10.2 %all-gather.1 = bf16[8,1,4]{2,1,0:T(2,128)(2,1)S(1)} all-gather(bf16[1,1,4]{2,1,0:T(2,128)(2,1)S(1)} %slice_bitcast_fusion.1), channel_id=1, replica_groups=mesh['seq'=8,'fsdp'=4] {'seq'}, dimensions={0}, use_global_device_ids=true | all-gather | bytes 72 | tf_op jit(solution)/shard_map/all_gather | solution.py:15
  20.8 1.3 copy.121
  22.2 2.4 reshape.638
  26.5 31.6 %all-gather.6.cloned.1.call-done = bf16[4096,768]{1,0:T(8,128)(2,1)} async-done(((bf16[512,768]{1,0:T(8,128)(2,1)}), bf16[4096,768]{1,0:T(8,128)(2,1)}) %all-gather.6.cloned.1.call-update) | async-done | bytes 6291472 | tf_op jit(solution)/shard_map/all_gather | solution.py:85
  58.2 7.5 %convolution_convert_fusion.8 = bf16[512,768]{1,0:T(8,128)(2,1)S(1)} fusion(bf16[512,4096]{1,0:T(8,128)(2,1)} %param.13, bf16[4096,768]{1,0:T(8,128)(2,1)} %all-gather.6.cloned.1.call-done), kind=kOutput, calls=%fused_computation.138 | convolution fusion | flops 3221618688 | bytes 11272192 | tf_op jit(solution)/shard_map/dot_general | solution.py:86
  66.8 1.5 fusion.98
  69.2 37.1 %while.86 = (s32[]{:T(128)}, f32[1,4,128,128]{3,2,1,0:T(8,128)S(1)}, f32[4,128,1,4,128]{4,3,1,0,2:T(4,128)}, f32[4,1,4,128,128]{4,3,2,1,0:T(8,128)}, f32[4,1,4,1...) while((s32[]{:T(128)}, ...), condition=%wide.region_2.3_spmd.clone.clone, body=%wide.region_0.0_spmd.clone.clone.sunk | while | flops 140019200 | bytes 4827465 | solution.py:73
  107.2 8.5 %while.85 = (s32[]{:T(128)}, f32[4,128,128]{2,1,0:T(8,128)S(1)}, s32[]{:T(128)}, bf16[8,4]{1,0:T(8,128)(2,1)S(1)}, bf16[8,4,128,128]{3,2,1,0:T(8,128)(2,1)}, /*index=5*/s32[]{:T(128)}, s32[]{:T(128)}, s32[]{:T(128)}, s32[]{:T(128)}) while((s32[]{:T(128)}, f32[4,128,128]{2,1,0:T(8,128)S(1)}, s32[]{:T(128)}, ...), condition=%wide.region_8.9_spmd.clone, body=%wide.region_7.8_spmd.clone.sunk | while | flops 327692 | bytes 655567 | solution.py:33
  117.1 42.4 %while.83 = (s32[]{:T(128)}, f32[1,4,128,128]{2,3,1,0:T(8,128)S(1)}, bf16[4,128,1,4,128]{4,1,3,2,0:T(8,128)(2,1)S(1)}, bf16[4,128,1,128]{3,1,2,0:T(8,128)(2,1)S(...) while((s32[]{:T(128)}, ...), condition=%wide.region_12.13_spmd, body=%wide.region_9.12_spmd.sunk | while | flops 277921792 | bytes 5299481 | solution.py:73
  121.2 1.5 fusion.209
  126.1 1.3 fusion.203
  131.8 1.5 fusion.209
  142.4 1.5 fusion.209
  147.3 1.3 fusion.203
  153.0 1.5 fusion.209
  158.0 1.3 fusion.203
  161.3 13.3 %while.84 = (s32[]{:T(128)}, f32[4,128,128]{2,1,0:T(8,128)S(1)}, s32[]{:T(128)}, bf16[8,4]{1,0:T(8,128)(2,1)}, bf16[8,4,128,128]{3,2,1,0:T(8,128)(2,1)}, /*index=5*/s32[]{:T(128)}, s32[]{:T(128)}) while((s32[]{:T(128)}, f32[4,128,128]{2,1,0:T(8,128)S(1)}, s32[]{:T(128)}, bf16[8,4]{1,0:T(8,128)(2,1)}, ...), condition=%wide.region_6.7_spmd.clone, body=%wide.region_5.6_spmd.clone.sunk | while | flops 327688 | bytes 655505 | solution.py:33
  175.4 7.9 %fusion.95 = bf16[4096,512]{0,1:T(8,128)(2,1)} fusion(bf16[4096,768]{1,0:T(8,128)(2,1)} %all-gather.6.cloned.1.call-done, bf16[512,128]{0,1:T(8,128)(2,1)S(1)} %fusion.97, bf16[512,640]{0,1:T(8,128)(2,1)S(1)} %slice.56), kind=kOutput, calls=%fused_computation.137 | convolution fusion | flops 3224895488 | bytes 11272192 | tf_op jit(solution)/shard_map/dot_general | solution.py:114
  183.3 7.8 %fusion.94 = bf16[4096,768]{0,1:T(8,128)(2,1)} fusion(bf16[512,4096]{1,0:T(8,128)(2,1)} %param.13, bf16[512,128]{0,1:T(8,128)(2,1)S(1)} %fusion.97, bf16[512,640]{0,1:T(8,128)(2,1)S(1)} %slice.56), kind=kOutput, calls=%fused_computation.135 | convolution fusion | flops 3225944064 | bytes 11272192 | tf_op jit(solution)/shard_map/dot_general | solution.py:122
  191.3 1.6 fusion.105
  194.6 65.6 %reduce-scatter.3.cloned.1.call-done = bf16[1024,512]{0,1:T(8,128)(2,1)} async-done(((bf16[4096,512]{0,1:T(8,128)(2,1)}), bf16[1024,512]{0,1:T(8,128)(2,1)}) %reduce-scatter.3.cloned.1.call-update) | async-done | bytes 1048592 | tf_op jit(solution)/shard_map/reduce_scatter | solution.py:113
  260.2 2.3 copy.137
  262.5 63.7 %reduce-scatter.5.cloned.1.call-done = bf16[512,768]{0,1:T(8,128)(2,1)} async-done(((bf16[4096,768]{0,1:T(8,128)(2,1)}), bf16[512,768]{0,1:T(8,128)(2,1)}) %reduce-scatter.5.cloned.1.call-update) | async-done | bytes 786448 | tf_op jit(solution)/shard_map/reduce_scatter | solution.py:121
  326.1 2.5 copy.138
  (261 shorter events, 104.1 us)
Async XLA Ops:
  7.2 17.4 %copy-start.2 = (f32[512,4]{0,1:T(4,128)S(1)}, f32[512,4]{0,1:T(4,128)}, u32[]{:S(2)}) copy-start(f32[512,4]{0,1:T(4,128)} %param.16) | copy-start | bytes 24580
  7.2 18.3 %copy-start.3 = (f32[512,4]{0,1:T(4,128)S(1)}, f32[512,4]{0,1:T(4,128)}, u32[]{:S(2)}) copy-start(f32[512,4]{0,1:T(4,128)} %param.15) | copy-start | bytes 24580
  7.2 51.0 %all-gather.6.cloned.1.call-start = ((), (), s32[]{:S(2)}) async-start(), calls=%async_computation.2 | async-start | bytes 7077888 | tf_op jit(solution)/shard_map/all_gather | solution.py:85
  7.9 99.3 %all-gather.10.cloned.1.call-start = ((), (), s32[]{:S(2)}) async-start(), calls=%async_computation.6 | async-start | bytes 1179648 | tf_op jit(solution)/shard_map/all_gather | solution.py:15
  65.6 0.9 copy-start
  69.1 92.2 %all-gather.8.cloned.1.call-start = ((), (), s32[]{:S(2)}) async-start(), calls=%async_computation.3 | async-start | bytes 1179648 | tf_op jit(solution)/shard_map/all_gather | solution.py:15
  107.0 153.2 %reduce-scatter.3.cloned.1.call-start = ((), (), s32[]{:S(2)}) async-start(), calls=%async_computation.4 | async-start | bytes 5242880 | tf_op jit(solution)/shard_map/reduce_scatter | solution.py:113
  115.8 0.5 copy-start.4
  183.3 142.8 %reduce-scatter.5.cloned.1.call-start = ((), (), s32[]{:S(2)}) async-start(), calls=%async_computation.5 | async-start | bytes 7077888 | tf_op jit(solution)/shard_map/reduce_scatter | solution.py:121
  191.2 2.2 copy-start.1
Sparse Core Ops, SparseCore 0:
  9.9 48.2 all-gather.5
  69.3 23.5 all-gather.9
  107.1 23.5 all-gather.7
  183.4 76.7 reduce-scatter.2
  263.8 62.2 reduce-scatter.4
where the time goes:
time: 337 us; the launch traced here: 335 us
  waiting for transfers between devices  162 us (48%)
  matrix products  57.6 us (17%)
  local copies, waits for them, and re-layouts  47.7 us (14%)
  other arithmetic  42.5 us (13%)
  between operations  14.1 us (4%)
  blocking collectives  10.2 us (3%)
    reduce_scatter x1, waiting for transfers between devices, shards(): lax.psum_scatter(lax.dot_general(gathered, proj_grad, (((1,), (1,)), ((),...  65.6 us
    reduce_scatter x1, waiting for transfers between devices, shards(): lax.psum_scatter(lax.dot_general(tokens, proj_grad, (((0,), (0,)), ((), (...  63.7 us
    all_gather x1, waiting for transfers between devices, shards(): gathered = lax.all_gather(w_in, 'seq', axis=0, tiled=True)  31.6 us
    select_n x16, other arithmetic, step(): return jax.tree.map(lambda a, b: jnp.where(reached, a, b), new, before)  16.2 us
    dot_general x12, matrix products, block_step(): jnp.einsum('tgn,ghnp->tghp', out_map.astype(jnp.float32), memory, precisi...  13.1 us
    dynamic_update_slice x16, other arithmetic, run_blocks(): lax.scan(block_step, empty_state, (values, in_map, out_map, steps_blocked...  12.7 us
    dynamic_slice x20, local copies, waits for them, and re-layouts, run_blocks(): lax.scan(block_step, empty_state, (values, in_map, out_map, steps_blocked...  11.9 us
    dynamic_update_slice x28, local copies, waits for them, and re-layouts, run_blocks(): lax.scan(block_step, empty_state, (values, in_map, out_map, steps_blocked...  10.7 us
  transfers between devices with their start and end apart: 5, of which 3 were waited for; matrix products, arithmetic and copies ran while one was open for 33% of the time, Pallas kernels for 0%

commit v1 on v0

v1 whole, which is shorter than its diff:
```python
import functools

import jax
import jax.numpy as jnp
from jax import lax
from jax.experimental import pallas as pl
from jax.experimental.pallas import tpu as pltpu
from jax.sharding import PartitionSpec as P

HEAD_DIM = 128
STATE = 128
HEADS = 4
WIDTH = HEADS * HEAD_DIM
STRIP = 128

F32 = jnp.float32
BF16 = jnp.bfloat16
NN = (((1,), (0,)), ((), ()))
NT = (((1,), (1,)), ((), ()))
TN = (((0,), (0,)), ((), ()))


def mm(a, b, dims=NN):
    return lax.dot_general(a, b, dims, preferred_element_type=F32)


def call(kernel, outs, args, flops):
    moved = sum(a.size * a.dtype.itemsize for a in (*args, *outs))
    return pl.pallas_call(
        kernel,
        out_shape=outs,
        in_specs=[pl.BlockSpec(memory_space=pltpu.VMEM)] * len(args),
        out_specs=[pl.BlockSpec(memory_space=pltpu.VMEM)] * len(outs),
        compiler_params=pltpu.CompilerParams(vmem_limit_bytes=40 * 2**20),
        cost_estimate=pl.CostEstimate(flops=flops, bytes_accessed=moved, transcendentals=0),
    )(*args)


def head(h):
    return slice(h * HEAD_DIM, (h + 1) * HEAD_DIM)


def ends_kernel(proj, cot, to_end, growth, ends):
    in_map = proj[:, WIDTH : WIDTH + STATE]
    out_map = proj[:, WIDTH + STATE :]
    fed = [
        (proj[:, head(h)].astype(F32) * to_end[:, h : h + 1]).astype(BF16) for h in range(HEADS)
    ]
    grown = [
        (cot[:, head(h)].astype(F32) * growth[:, h : h + 1]).astype(BF16) for h in range(HEADS)
    ]
    ends[:STATE, :] = mm(in_map, jnp.concatenate(fed, axis=1), TN).astype(BF16)
    ends[STATE:, :] = mm(out_map, jnp.concatenate(grown, axis=1), TN).astype(BF16)


def local_kernel(
    proj, cot, cum, cum_rows, step_rows, to_end, growth, y, dx, db, dc, fed, grown
):
    rows = proj.shape[0]
    for h in range(HEADS):
        fed[:, head(h)] = (proj[:, head(h)].astype(F32) * to_end[:, h : h + 1]).astype(BF16)
        grown[:, head(h)] = (cot[:, head(h)].astype(F32) * growth[:, h : h + 1]).astype(BF16)
    dx[...] = jnp.zeros_like(dx)
    db[...] = jnp.zeros_like(db)
    for at in range(0, rows, STRIP):
        upto = at + STRIP
        here = slice(at, upto)
        in_map = proj[:upto, WIDTH : WIDTH + STATE]
        out_map = proj[here, WIDTH + STATE :]
        scores = mm(out_map, in_map, NT)
        t = lax.broadcasted_iota(jnp.int32, (STRIP, upto), 0) + at
        s = lax.broadcasted_iota(jnp.int32, (STRIP, upto), 1)
        causal = t >= s
        dscores = jnp.zeros_like(scores)
        for h in range(HEADS):
            span = cum[here, h : h + 1] - cum_rows[h : h + 1, :upto]
            factor = jnp.exp(jnp.where(causal, span, -1e30)) * step_rows[h : h + 1, :upto]
            mixing = (scores * factor).astype(BF16)
            values = proj[:upto, head(h)]
            grad = cot[here, head(h)]
            y[here, head(h)] = mm(mixing, values)
            dx[:upto, head(h)] += mm(mixing, grad, TN)
            dscores = dscores + mm(grad, values, NT) * factor
        dscores = dscores.astype(BF16)
        dc[here, :] = mm(dscores, in_map)
        db[:upto, :] += mm(dscores, out_map, TN)


def join_kernel(
    count, proj, to_end, dx, db, dc, fed, grown, weights, near, *rest
):
    far, (proj_grad, entering) = rest[:count], rest[count:]
    before = near[:STATE, :].astype(F32) * weights[0:1, :]
    after = near[STATE:, :].astype(F32) * weights[1:2, :]
    for j, part in enumerate(far):
        value = part[...].astype(F32)
        before = before + value * weights[2 * j + 2 : 2 * j + 3, :]
        after = after + value * weights[2 * j + 3 : 2 * j + 4, :]
    before = before.astype(BF16)
    after = after.astype(BF16)
    entering[...] = before
    carried = mm(proj[:, WIDTH : WIDTH + STATE], after)
    for h in range(HEADS):
        proj_grad[:, head(h)] = (dx[:, head(h)] + carried[:, head(h)] * to_end[:, h : h + 1]).astype(BF16)
    proj_grad[:, WIDTH : WIDTH + STATE] = (db[...] + mm(fed[...], after, NT)).astype(BF16)
    proj_grad[:, WIDTH + STATE :] = (dc[...] + mm(grown[...], before, NT)).astype(BF16)


def output_kernel(proj, entering, growth, y, out):
    carried = mm(proj[:, WIDTH + STATE :], entering[...])
    for h in range(HEADS):
        out[:, head(h)] = y[:, head(h)] + carried[:, head(h)] * growth[:, h : h + 1]


def swap(value, size, bit):
    return lax.ppermute(value, "seq", [(i, i ^ bit) for i in range(size)])


def spread(row):
    return jnp.repeat(row, HEAD_DIM, axis=-1)


def shards(tokens, w_in, step_logit, decay_logit, cotangent):
    size = lax.axis_size("seq")
    me = lax.axis_index("seq")
    core, chip = me % 2, me // 2
    square = size == 8
    rows, columns = tokens.shape[0], w_in.shape[1]
    part = w_in.shape[0]
    half = part // 2
    state = jax.ShapeDtypeStruct

    def token_columns(bit):
        return lax.dynamic_slice_in_dim(tokens, (me ^ bit) * part, part, axis=1)

    if square:
        from_x, from_y = swap(w_in, size, 2), swap(w_in, size, 4)
        near = swap(w_in, size, 1)
        corner0 = swap(from_x[:half], size, 4)
        corner1 = swap(from_y[half:], size, 2)
        near_x, near_y = swap(from_x, size, 1), swap(from_y, size, 1)
        near0, near1 = swap(corner0, size, 1), swap(corner1, size, 1)
        pieces = [(0, 0, w_in), (1, 0, near), (2, 0, from_x), (4, 0, from_y), (3, 0, near_x), (5, 0, near_y)]
        pieces += [(6, 0, corner0), (6, half, corner1), (7, 0, near0), (7, half, near1)]
        total = 0.0
        for bit, first, piece in pieces:
            total = total + mm(token_columns(bit)[:, first : first + piece.shape[0]], piece)
        projected = total.astype(BF16)
        gathered = jnp.zeros((part * size, columns), BF16)
        for bit, first, piece in pieces:
            gathered = lax.dynamic_update_slice_in_dim(gathered, piece, (me ^ bit) * part + first, axis=0)
    else:
        gathered = lax.all_gather(w_in, "seq", axis=0, tiled=True)
        projected = mm(tokens, gathered).astype(BF16)

    step_size = jax.nn.softplus(step_logit)
    log_decay = -jax.nn.softplus(decay_logit)
    lower = (
        lax.broadcasted_iota(jnp.int32, (rows, rows), 0) >= lax.broadcasted_iota(jnp.int32, (rows, rows), 1)
    ).astype(F32)
    cum = lax.dot_general(lower, log_decay, NN, precision=lax.Precision.HIGHEST, preferred_element_type=F32)
    log_total = cum[-1]
    growth = jnp.exp(cum)
    to_end = jnp.exp(log_total[None] - cum) * step_size
    cum_rows, step_rows = cum.T, step_size.T
    totals = lax.all_gather(log_total, "seq")

    (ends,) = call(
        ends_kernel,
        [state((2 * STATE, WIDTH), BF16)],
        [projected, cotangent, to_end, growth],
        4 * rows * STATE * WIDTH,
    )
    if square:
        other = swap(ends, size, 1)
        pair = totals.reshape(size // 2, 2, HEADS)
        of_chip = pair.sum(1)
        until = jnp.stack(
            [sum([of_chip[j] for j in range(k)], jnp.zeros((HEADS,), F32)) for k in range(size // 2 + 1)]
        )
        mine = pair[chip]
        first, second = jnp.exp(mine[0]), jnp.exp(mine[1])
        one = jnp.ones_like(first)
        own_ends = jnp.concatenate(
            [
                jnp.broadcast_to(spread(jnp.where(core == 0, second, one)), (STATE, WIDTH)),
                jnp.broadcast_to(spread(jnp.where(core == 0, one, first)), (STATE, WIDTH)),
            ]
        )
        other_ends = jnp.concatenate(
            [
                jnp.broadcast_to(spread(jnp.where(core == 0, one, second)), (STATE, WIDTH)),
                jnp.broadcast_to(spread(jnp.where(core == 0, first, one)), (STATE, WIDTH)),
            ]
        )
        both = (ends.astype(F32) * own_ends + other.astype(F32) * other_ends).astype(BF16)
        forward, backward = both[:STATE], both[STATE:]
        for_x = jnp.where(chip % 2 == 0, forward, backward)
        for_y = jnp.where(chip < 2, forward, backward)
        far = [swap(for_x, size, 2), swap(for_y, size, 4), swap(for_y, size, 6)]
        weights = [
            jnp.where(core == 1, one, 0.0),
            jnp.where(core == 0, one, 0.0),
        ]
        for bit in (1, 2, 3):
            there = chip ^ bit
            reach = jnp.where(there < chip, until[chip] - until[there + 1], -1e30)
            weights.append(jnp.exp(reach) * jnp.where(core == 1, first, one))
            reach = jnp.where(there > chip, until[there] - until[chip + 1], -1e30)
            weights.append(jnp.exp(reach) * jnp.where(core == 0, second, one))
        weights = spread(jnp.stack(weights))
    else:
        everything = lax.all_gather(ends, "seq")
        places = jnp.arange(size)
        until = jnp.stack([jnp.sum(jnp.where((places < k)[:, None], totals, 0.0), axis=0) for k in range(size + 1)])
        reach = jnp.where((places < me)[:, None], until[me][None] - until[1:], -1e30)
        before = jnp.einsum("jnk,jk->nk", everything[:, :STATE].astype(F32), spread(jnp.exp(reach)))
        reach = jnp.where((places > me)[:, None], until[:-1] - until[me + 1][None], -1e30)
        after = jnp.einsum("jnk,jk->nk", everything[:, STATE:].astype(F32), spread(jnp.exp(reach)))
        other = jnp.concatenate([before, after]).astype(BF16)
        far = []
        weights = jnp.ones((2, WIDTH), F32)

    y, dx, db, dc, fed, grown = call(
        local_kernel,
        [
            state((rows, WIDTH), F32),
            state((rows, WIDTH), F32),
            state((rows, STATE), F32),
            state((rows, STATE), F32),
            state((rows, WIDTH), BF16),
            state((rows, WIDTH), BF16),
        ],
        [projected, cotangent, cum, cum_rows, step_rows, to_end, growth],
        20 * rows * rows * STATE,
    )
    proj_grad, entering = call(
        functools.partial(join_kernel, len(far)),
        [state((rows, columns), BF16), state((STATE, WIDTH), BF16)],
        [projected, to_end, dx, db, dc, fed, grown, weights, other, *far],
        6 * rows * STATE * WIDTH,
    )
    input_grad = lax.psum_scatter(
        mm(gathered, proj_grad, NT).astype(BF16), "fsdp", scatter_dimension=0, tiled=True
    )
    (layer_out,) = call(
        output_kernel,
        [state((rows, WIDTH), F32)],
        [projected, entering, growth, y],
        2 * rows * STATE * WIDTH,
    )

    if square:
        chips = [0, 2, 4, 6]
        to_near = jnp.concatenate([token_columns(bit ^ 1) for bit in chips], axis=1)
        to_keep = jnp.concatenate([token_columns(bit) for bit in chips], axis=1)
        received = swap(mm(to_near, proj_grad, TN).astype(BF16), size, 1)
        kept = (mm(to_keep, proj_grad, TN) + received.astype(F32)).astype(BF16)
        own, for_x, for_y, for_corner = kept.reshape(4, part, columns)
        corner_x, corner_y = swap(for_corner[:half], size, 2), swap(for_corner[half:], size, 4)
        top, low = swap(for_x[:half], size, 2), swap(for_y[half:], size, 4)
        low_x = swap((for_x[half:].astype(F32) + corner_y.astype(F32)).astype(BF16), size, 2)
        top_y = swap((for_y[:half].astype(F32) + corner_x.astype(F32)).astype(BF16), size, 4)
        w_in_grad = jnp.concatenate(
            [
                own[:half].astype(F32) + top.astype(F32) + top_y.astype(F32),
                own[half:].astype(F32) + low.astype(F32) + low_x.astype(F32),
            ]
        )
    else:
        w_in_grad = lax.psum_scatter(
            mm(tokens, proj_grad, TN).astype(BF16), "seq", scatter_dimension=0, tiled=True
        ).astype(F32)
    return (layer_out, input_grad, w_in_grad)


def solution(mesh):
    across = P("seq", "fsdp")
    return jax.shard_map(
        shards,
        mesh=mesh,
        in_specs=(P("seq", None), across, across, across, across),
        out_specs=(across, P("fsdp", "seq"), across),
        check_vma=False,
    )
```

time: 337 us -> 171 us (0.51)
  waiting for transfers between devices: 162 us -> 66.4 us
  other arithmetic: 42.5 us -> 3.64 us
  matrix products: 57.6 us -> 25.6 us
  local copies, waits for them, and re-layouts: 47.7 us -> 18.7 us
  starting transfers between devices: 0.38 us -> 19.1 us
  blocking collectives: 10.2 us -> 17.2 us
  Pallas kernels: 0 us -> 5.48 us
    reduce_scatter x2 -> x1, waiting for transfers between devices: 129 us -> 31.7 us  [shards(): lax.psum_scatter(mm(gathered, proj_grad, NT).astype(BF16), 'fsdp', scatte...]
    ppermute x0 -> x20, waiting for transfers between devices: none -> 34.7 us  [swap(): return lax.ppermute(value, 'seq', [(i, i ^ bit) for i in range(size)])]
    all_gather x3 -> x0, waiting for transfers between devices: 31.7 us -> none  [the longest x1 31.6 us: shards(): gathered = lax.all_gather(w_in, 'seq', axis=0, tiled=True)]
    dot_general x53 -> x14, matrix products: 56.1 us -> 25.6 us  [the longest x13 24.5 us: mm(): return lax.dot_general(a, b, dims, preferred_element_type=F32)]
    ppermute x0 -> x20, starting transfers between devices: none -> 19.1 us  [swap(): return lax.ppermute(value, 'seq', [(i, i ^ bit) for i in range(size)])]
    select_n x17 -> x2, other arithmetic: 16.2 us -> 0.03 us  [the longest x1 0.02 us: shards(): for_y = jnp.where(chip < 2, forward, backward)]
    dynamic_update_slice x16 -> x0, other arithmetic: 12.7 us -> none  [run_blocks(): lax.scan(block_step, empty_state, (values, in_map, out_map, steps_blocked...]
    dynamic_slice x20 -> x2, local copies, waits for them, and re-layouts: 11.9 us -> 3.55 us  [the longest x1 3.55 us: token_columns(): return lax.dynamic_slice_in_dim(tokens, (me ^ bit) * part, part, axis=1)]
  transfers between devices with their start and end apart: 5 -> 21, of which waited for: 3 -> 10; matrix products, arithmetic and copies ran while one was open for 33% -> 22% of each run, Pallas kernels for 0% -> 2%
where the time goes in v1:
time: 171 us
  waiting for transfers between devices  66.4 us (39%)
  matrix products  25.6 us (15%)
  starting transfers between devices  19.1 us (11%)
  local copies, waits for them, and re-layouts  18.7 us (11%)
  blocking collectives  17.2 us (10%)
  between operations  14.5 us (8%)
  Pallas kernels  5.48 us (3%)
  other arithmetic  3.64 us (2%)
    ppermute x20, waiting for transfers between devices, swap(): return lax.ppermute(value, 'seq', [(i, i ^ bit) for i in range(size)])  34.7 us
    reduce_scatter x1, waiting for transfers between devices, shards(): lax.psum_scatter(mm(gathered, proj_grad, NT).astype(BF16), 'fsdp', scatte...  31.7 us
    dot_general x13, matrix products, mm(): return lax.dot_general(a, b, dims, preferred_element_type=F32)  24.5 us
    ppermute x20, starting transfers between devices, swap(): return lax.ppermute(value, 'seq', [(i, i ^ bit) for i in range(size)])  19.1 us
    all_gather x1, blocking collectives, shards(): totals = lax.all_gather(log_total, 'seq')  17.2 us
    dynamic_update_slice x10, local copies, waits for them, and re-layouts, shards(): lax.dynamic_update_slice_in_dim(gathered, piece, (me ^ bit) * part + firs...  9.88 us
    pallas_call x4, Pallas kernels, call(): pl.pallas_call(kernel, out_shape=outs, in_specs=[pl.BlockSpec(memory_spac...  5.48 us
    dynamic_slice x1, local copies, waits for them, and re-layouts, token_columns(): return lax.dynamic_slice_in_dim(tokens, (me ^ bit) * part, part, axis=1)  3.55 us
  transfers between devices with their start and end apart: 21, of which 10 were waited for; matrix products, arithmetic and copies ran while one was open for 22% of the time, Pallas kernels for 2%

profile of v1, /device:TPU:0, one launch (start us, length us, event | category | flops | bytes accessed | tf_op | source)
XLA Modules:
  0.0 170.6 jit_solution(12737245394707285417)
XLA Ops:
  7.2 3.0 %collective-permute-start.1 = (bf16[512,768]{1,0:T(8,128)(2,1)}, bf16[512,768]{1,0:T(8,128)(2,1)S(1)}, u32[]{:S(2)}, u32[]{:S(2)}) collective-permute-start(bf16[512,768]{1,0:T(8,128)(2,1)} %param.6), channel_id=1, source_target_pairs={{0,8},{4,12},{8,0},{12,4},{16,24},{20,28},{24,16},{28,20},{1,9},{5... | collective-permute-start | bytes 2359304 | tf_op jit(solution)/shard_map/ppermute | solution.py:116
  15.1 17.2 %all-gather = f32[8,1,4]{2,1,0:T(1,128)S(1)} all-gather(f32[1,1,4]{2,1,0:T(1,128)S(1)} %bitcast.57), channel_id=1, replica_groups=mesh['seq'=8,'fsdp'=4] {'seq'}, dimensions={0}, use_global_device_ids=true | all-gather | bytes 144 | tf_op jit(solution)/shard_map/all_gather | solution.py:166
  33.5 3.0 %broadcast_in_dim.51 = bf16[4096,768]{1,0:T(8,128)(2,1)} broadcast(bf16[]{:T(256)} %constant.68.clone.1), dimensions={} | broadcast | bytes 6291458 | tf_op jit(solution)/shard_map/broadcast_in_dim | solution.py:149
  37.8 3.5 %constant_dynamic-slice_fusion.10 = (bf16[512,512]{1,0:T(8,128)(2,1)}, bf16[512,512]{1,0:T(8,128)(2,1)S(1)}, bf16[512,512]{1,0:T(8,128)(2,1)S(1)}, bf16[512,512]...) fusion(bf16[512,4096]{1,0:T(8,128)(2,1)} %param.5, ...), kind=kLoop, calls=%fused_computation.75 | loop fusion | bytes 8388640 | tf_op jit(solution)/shard_map/dynamic_slice | solution.py:134
  42.0 1.7 %collective-permute-start.5 = (bf16[256,768]{1,0:T(8,128)(2,1)S(1)}, bf16[256,768]{1,0:T(8,128)(2,1)S(1)}, u32[]{:S(2)}, u32[]{:S(2)}) collective-permute-start(bf16[256,768]{1,0:T(8,128)(2,1)S(1)} %slice.116), channel_id=1, source_target_pairs={{0,16},{4,20},{8,24},{12,28},{16,0},{20,4},{24,8},{28,12},{1,17},{... | collective-permute-start | bytes 1179656 | tf_op jit(solution)/shard_map/ppermute | solution.py:116
  43.8 1.6 collective-permute-start.6
  46.5 1.7 fusion.68
  48.2 2.1 %constant_dynamic-update-slice_fusion.8 = bf16[4096,768]{1,0:T(8,128)(2,1)} fusion(bf16[4096,768]{1,0:T(8,128)(2,1)} %constant_dynamic-update-slice_fusion.9, bf16[512,768]{1,0:T(8,128)(2,1)} %collective-permute-done, s32[]{:T(128)S(6)} %select_n.242), kind=kLoop, calls=%fused_computation.63 | loop fusion | bytes 1572868 | tf_op jit(solution)/shard_map/dynamic_update_slice | solution.py:151
  60.1 1.8 %add_convert_fusion.1.proj = bf16[512,768]{1,0:T(8,128)(2,1)S(1)} fusion(f32[512,768]{1,0:T(8,128)S(1)} %fusion.21, f32[512,768]{1,0:T(8,128)S(1)} %fusion.23, f32[512,768]{1,0:T(8,128)S(1)} %fusion.25, f32[512,768]{1,0:T(8,128)S(1)} %fusion.72, f32[512,768]{1,0:T(8,128)S(1)} %fusion.71, f32[512,768]{1,0:T(8,128)S(1)} %fusion.70, ...), kind=kOutput, calls=%fused_computation.18 | convolution fusion | flops 205258752 | bytes 15597572 | tf_op jit(solution)/shard_map/dot_general | solution.py:24
  68.5 2.6 %collective-permute-start.12 = (bf16[128,512]{1,0:T(8,128)(2,1)S(1)}, bf16[128,512]{1,0:T(8,128)(2,1)S(1)}, u32[]{:S(2)}, u32[]{:S(2)}) collective-permute-start(bf16[128,512]{1,0:T(8,128)(2,1)S(1)} %get-tuple-element.41), channel_id=1, source_target_pairs={{0,24},{4,28},{8,16},{12,20},{16,8},{20,12},{24,0},{28,4},{1,25},{... | collective-permute-start | bytes 393224 | tf_op jit(solution)/shard_map/ppermute | solution.py:116
  71.5 2.5 %shard_map.76 = (f32[512,512]{1,0:T(8,128)S(1)}, f32[512,512]{1,0:T(8,128)S(1)}, f32[512,128]{1,0:T(8,128)S(1)}, f32[512,128]{1,0:T(8,128)S(1)}, bf16[512,512]{1...) custom-call(bf16[512,768]{1,0:T(8,128)(2,1)S(1)} %add_convert_fusion.1.proj, bf16[512,512]{1,0:T(8,128)(2,1)S(1)} %copy-done, ...), custom_call_target="tpu_custom_call" | custom-call | flops 671088640 | bytes 5021696 | tf_op jit(solution)/shard_map/pallas_call | solution.py:29
  74.8 2.7 %collective-permute-done.10.rest_0_ = bf16[128,512]{1,0:T(8,128)(2,1)S(1)} collective-permute-done((bf16[128,512]{1,0:T(8,128)(2,1)S(1)}, bf16[128,512]{1,0:T(8,128)(2,1)S(1)}, u32[]{:S(2)}, u32[]{:S(2)}) %collective-permute-start.10) | collective-permute-done | bytes 131104 | tf_op jit(solution)/shard_map/ppermute | solution.py:116
  78.2 8.1 %convolution_convert_fusion = bf16[4096,512]{1,0:T(8,128)(2,1)} fusion(bf16[4096,768]{1,0:T(8,128)(2,1)} %constant_dynamic-update-slice_fusion, bf16[512,768]{1,0:T(8,128)(2,1)S(1)} %get-tuple-element.18), kind=kOutput, calls=%fused_computation.1 | convolution fusion | flops 3223322624 | bytes 11272192 | tf_op jit(solution)/shard_map/dot_general | solution.py:24
  86.4 3.5 %convolution_convert_fusion.1 = bf16[2048,768]{1,0:T(8,128)(2,1)S(1)} fusion(bf16[512,768]{1,0:T(8,128)(2,1)S(1)} %get-tuple-element.18, bf16[512,512]{1,0:T(8,128)(2,1)} %get-tuple-element.31, bf16[512,512]{1,0:T(8,128)(2,1)} %copy-done.8, bf16[512,512]{1,0:T(8,128)(2,1)} %copy-done.9, bf16[512,512]{1,0:T(8,128)(2,1)} %copy-done.10), kind=kOutput, calls=%fused_computation.2 | convolution fusion | flops 1620574208 | bytes 6029312 | tf_op jit(solution)/shard_map/dot_general | solution.py:24
  90.0 5.6 %collective-permute-done.13 = bf16[2048,768]{1,0:T(8,128)(2,1)S(1)} collective-permute-done((bf16[2048,768]{1,0:T(8,128)(2,1)S(1)}, bf16[2048,768]{1,0:T(8,128)(2,1)S(1)}, u32[]{:S(2)}, u32[]{:S(2)}) %collective-permute-start.13) | collective-permute-done | bytes 3145760 | tf_op jit(solution)/shard_map/ppermute | solution.py:116
  95.7 2.5 %add_convert_fusion = bf16[2048,768]{1,0:T(8,128)(2,1)S(1)} fusion(bf16[2048,768]{1,0:T(8,128)(2,1)S(1)} %collective-permute-done.13, bf16[512,768]{1,0:T(8,128)(2,1)S(1)} %get-tuple-element.18, bf16[512,512]{1,0:T(8,128)(2,1)S(1)} %copy-done.12, bf16[512,512]{1,0:T(8,128)(2,1)S(1)} %copy-done.3, bf16[512,512]{1,0:T(8,128)(2,1)S(1)} %copy-done.5, ...), kind=kOutput, calls=%fused_computation | convolution fusion | flops 1623719936 | bytes 9175040 | tf_op jit(solution)/shard_map/dot_general | solution.py:24
  98.3 1.6 collective-permute-start.15
  101.1 9.2 %collective-permute-done.15 = bf16[256,768]{1,0:T(8,128)(2,1)S(1)} collective-permute-done((bf16[256,768]{1,0:T(8,128)(2,1)S(1)}, bf16[256,768]{1,0:T(8,128)(2,1)S(1)}, u32[]{:S(2)}, u32[]{:S(2)}) %collective-permute-start.15) | collective-permute-done | bytes 393248 | tf_op jit(solution)/shard_map/ppermute | solution.py:116
  112.5 5.4 %collective-permute-done.14 = bf16[256,768]{1,0:T(8,128)(2,1)S(1)} collective-permute-done((bf16[256,768]{1,0:T(8,128)(2,1)S(1)}, bf16[256,768]{1,0:T(8,128)(2,1)S(1)}, u32[]{:S(2)}, u32[]{:S(2)}) %collective-permute-start.14) | collective-permute-done | bytes 393248 | tf_op jit(solution)/shard_map/ppermute | solution.py:116
  118.0 4.6 %collective-permute-done.16 = bf16[256,768]{1,0:T(8,128)(2,1)S(1)} collective-permute-done((bf16[256,768]{1,0:T(8,128)(2,1)S(1)}, bf16[256,768]{1,0:T(8,128)(2,1)S(1)}, u32[]{:S(2)}, u32[]{:S(2)}) %collective-permute-start.16) | collective-permute-done | bytes 393248 | tf_op jit(solution)/shard_map/ppermute | solution.py:116
  122.8 1.6 collective-permute-start.19
  125.8 2.8 %collective-permute-done.17 = bf16[256,768]{1,0:T(8,128)(2,1)S(1)} collective-permute-done((bf16[256,768]{1,0:T(8,128)(2,1)S(1)}, bf16[256,768]{1,0:T(8,128)(2,1)S(1)}, u32[]{:S(2)}, u32[]{:S(2)}) %collective-permute-start.17) | collective-permute-done | bytes 393248 | tf_op jit(solution)/shard_map/ppermute | solution.py:116
  128.6 2.1 %collective-permute-done.19 = bf16[256,768]{1,0:T(8,128)(2,1)S(1)} collective-permute-done((bf16[256,768]{1,0:T(8,128)(2,1)S(1)}, bf16[256,768]{1,0:T(8,128)(2,1)S(1)}, u32[]{:S(2)}, u32[]{:S(2)}) %collective-permute-start.19) | collective-permute-done | bytes 393248 | tf_op jit(solution)/shard_map/ppermute | solution.py:116
  132.0 31.7 %reduce-scatter.2.cloned.1.call-done = bf16[1024,512]{1,0:T(8,128)(2,1)} async-done(((bf16[4096,512]{1,0:T(8,128)(2,1)}), bf16[1024,512]{1,0:T(8,128)(2,1)}) %reduce-scatter.2.cloned.1.call-update) | async-done | bytes 1048592 | tf_op jit(solution)/shard_map/reduce_scatter | solution.py:243
  (112 shorter events, 33.7 us)
Async XLA Ops:
  7.2 156.5 %reduce-scatter.2.cloned.1.call-start = ((), (), s32[]{:S(2)}) async-start(), calls=%async_computation.1 | async-start | bytes 5242880 | tf_op jit(solution)/shard_map/reduce_scatter | solution.py:243
  7.2 34.8 %collective-permute-start.1 = (bf16[512,768]{1,0:T(8,128)(2,1)}, bf16[512,768]{1,0:T(8,128)(2,1)S(1)}, u32[]{:S(2)}, u32[]{:S(2)}) collective-permute-start(bf16[512,768]{1,0:T(8,128)(2,1)} %param.6), channel_id=1, source_target_pairs={{0,8},{4,12},{8,0},{12,4},{16,24},{20,28},{24,16},{28,20},{1,9},{5... | collective-permute-start | bytes 2359304 | tf_op jit(solution)/shard_map/ppermute | solution.py:116
  10.2 33.6 %collective-permute-start.2 = (bf16[512,768]{1,0:T(8,128)(2,1)}, bf16[512,768]{1,0:T(8,128)(2,1)S(1)}, u32[]{:S(2)}, u32[]{:S(2)}) collective-permute-start(bf16[512,768]{1,0:T(8,128)(2,1)} %param.6), channel_id=1, source_target_pairs={{0,16},{4,20},{8,24},{12,28},{16,0},{20,4},{24,8},{28,12},{1,17},{... | collective-permute-start | bytes 2359304 | tf_op jit(solution)/shard_map/ppermute | solution.py:116
  11.7 34.8 %collective-permute-start = (bf16[512,768]{1,0:T(8,128)(2,1)}, bf16[512,768]{1,0:T(8,128)(2,1)}, u32[]{:S(2)}, u32[]{:S(2)}) collective-permute-start(bf16[512,768]{1,0:T(8,128)(2,1)} %param.6), channel_id=1, source_target_pairs={{0,4},{4,0},{8,12},{12,8},{16,20},{20,16},{24,28},{28,24},{1,5},{5... | collective-permute-start | bytes 2359304 | tf_op jit(solution)/shard_map/ppermute | solution.py:116
  12.8 23.8 %copy-start.1 = (bf16[512,768]{1,0:T(8,128)(2,1)S(1)}, bf16[512,768]{1,0:T(8,128)(2,1)}, u32[]{:S(2)}) copy-start(bf16[512,768]{1,0:T(8,128)(2,1)} %param.6) | copy-start | bytes 2359300
  41.4 16.8 %copy-start.9 = (bf16[512,512]{1,0:T(8,128)(2,1)}, bf16[512,512]{1,0:T(8,128)(2,1)S(1)}, u32[]{:S(2)}) copy-start(bf16[512,512]{1,0:T(8,128)(2,1)S(1)} %get-tuple-element.26) | copy-start | bytes 1572868
  41.4 18.1 %copy-start.8 = (bf16[512,512]{1,0:T(8,128)(2,1)}, bf16[512,512]{1,0:T(8,128)(2,1)S(1)}, u32[]{:S(2)}) copy-start(bf16[512,512]{1,0:T(8,128)(2,1)S(1)} %get-tuple-element.25) | copy-start | bytes 1572868
  42.0 11.4 %collective-permute-start.5 = (bf16[256,768]{1,0:T(8,128)(2,1)S(1)}, bf16[256,768]{1,0:T(8,128)(2,1)S(1)}, u32[]{:S(2)}, u32[]{:S(2)}) collective-permute-start(bf16[256,768]{1,0:T(8,128)(2,1)S(1)} %slice.116), channel_id=1, source_target_pairs={{0,16},{4,20},{8,24},{12,28},{16,0},{20,4},{24,8},{28,12},{1,17},{... | collective-permute-start | bytes 1179656 | tf_op jit(solution)/shard_map/ppermute | solution.py:116
  43.8 11.1 %collective-permute-start.6 = (bf16[256,768]{1,0:T(8,128)(2,1)S(1)}, bf16[256,768]{1,0:T(8,128)(2,1)S(1)}, u32[]{:S(2)}, u32[]{:S(2)}) collective-permute-start(bf16[256,768]{1,0:T(8,128)(2,1)S(1)} %slice.117), channel_id=1, source_target_pairs={{0,8},{4,12},{8,0},{12,4},{16,24},{20,28},{24,16},{28,20},{1,9},{5... | collective-permute-start | bytes 1179656 | tf_op jit(solution)/shard_map/ppermute | solution.py:116
  45.4 12.2 %collective-permute-start.3 = (bf16[512,768]{1,0:T(8,128)(2,1)S(1)}, bf16[512,768]{1,0:T(8,128)(2,1)S(1)}, u32[]{:S(2)}, u32[]{:S(2)}) collective-permute-start(bf16[512,768]{1,0:T(8,128)(2,1)S(1)} %collective-permute-done.1), channel_id=1, source_target_pairs={{0,4},{4,0},{8,12},{12,8},{16,20},{20,16},{24,28},{28,24},{1,5},{5... | collective-permute-start | bytes 2359304 | tf_op jit(solution)/shard_map/ppermute | solution.py:116
  45.4 14.1 %collective-permute-start.4 = (bf16[512,768]{1,0:T(8,128)(2,1)S(1)}, bf16[512,768]{1,0:T(8,128)(2,1)S(1)}, u32[]{:S(2)}, u32[]{:S(2)}) collective-permute-start(bf16[512,768]{1,0:T(8,128)(2,1)S(1)} %collective-permute-done.2), channel_id=1, source_target_pairs={{0,4},{4,0},{8,12},{12,8},{16,20},{20,16},{24,28},{28,24},{1,5},{5... | collective-permute-start | bytes 2359304 | tf_op jit(solution)/shard_map/ppermute | solution.py:116
  53.5 4.7 %collective-permute-start.7 = (bf16[256,768]{1,0:T(8,128)(2,1)S(1)}, bf16[256,768]{1,0:T(8,128)(2,1)S(1)}, u32[]{:S(2)}, u32[]{:S(2)}) collective-permute-start(bf16[256,768]{1,0:T(8,128)(2,1)S(1)} %collective-permute-done.5), channel_id=1, source_target_pairs={{0,4},{4,0},{8,12},{12,8},{16,20},{20,16},{24,28},{28,24},{1,5},{5... | collective-permute-start | bytes 1179656 | tf_op jit(solution)/shard_map/ppermute | solution.py:116
  54.9 5.2 %collective-permute-start.8 = (bf16[256,768]{1,0:T(8,128)(2,1)S(1)}, bf16[256,768]{1,0:T(8,128)(2,1)S(1)}, u32[]{:S(2)}, u32[]{:S(2)}) collective-permute-start(bf16[256,768]{1,0:T(8,128)(2,1)S(1)} %collective-permute-done.6), channel_id=1, source_target_pairs={{0,4},{4,0},{8,12},{12,8},{16,20},{20,16},{24,28},{28,24},{1,5},{5... | collective-permute-start | bytes 1179656 | tf_op jit(solution)/shard_map/ppermute | solution.py:116
  62.9 4.8 %collective-permute-start.9 = (bf16[256,512]{1,0:T(8,128)(2,1)S(1)}, bf16[256,512]{1,0:T(8,128)(2,1)S(1)}, u32[]{:S(2)}, u32[]{:S(2)}) collective-permute-start(bf16[256,512]{1,0:T(8,128)(2,1)S(1)} %shard_map.77), channel_id=1, source_target_pairs={{0,4},{4,0},{8,12},{12,8},{16,20},{20,16},{24,28},{28,24},{1,5},{5... | collective-permute-start | bytes 786440 | tf_op jit(solution)/shard_map/ppermute | solution.py:116
  67.9 9.5 %collective-permute-start.11 = (bf16[128,512]{1,0:T(8,128)(2,1)S(1)}, bf16[128,512]{1,0:T(8,128)(2,1)S(1)}, u32[]{:S(2)}, u32[]{:S(2)}) collective-permute-start(bf16[128,512]{1,0:T(8,128)(2,1)S(1)} %get-tuple-element.41), channel_id=1, source_target_pairs={{0,16},{4,20},{8,24},{12,28},{16,0},{20,4},{24,8},{28,12},{1,17},{... | collective-permute-start | bytes 393224 | tf_op jit(solution)/shard_map/ppermute | solution.py:116
  68.5 9.0 %collective-permute-start.12 = (bf16[128,512]{1,0:T(8,128)(2,1)S(1)}, bf16[128,512]{1,0:T(8,128)(2,1)S(1)}, u32[]{:S(2)}, u32[]{:S(2)}) collective-permute-start(bf16[128,512]{1,0:T(8,128)(2,1)S(1)} %get-tuple-element.41), channel_id=1, source_target_pairs={{0,24},{4,28},{8,16},{12,20},{16,8},{20,12},{24,0},{28,4},{1,25},{... | collective-permute-start | bytes 393224 | tf_op jit(solution)/shard_map/ppermute | solution.py:116
  71.0 6.4 %collective-permute-start.10 = (bf16[128,512]{1,0:T(8,128)(2,1)S(1)}, bf16[128,512]{1,0:T(8,128)(2,1)S(1)}, u32[]{:S(2)}, u32[]{:S(2)}) collective-permute-start(bf16[128,512]{1,0:T(8,128)(2,1)S(1)} %get-tuple-element.42), channel_id=1, source_target_pairs={{0,8},{4,12},{8,0},{12,4},{16,24},{20,28},{24,16},{28,20},{1,9},{5... | collective-permute-start | bytes 393224 | tf_op jit(solution)/shard_map/ppermute | solution.py:116
  89.9 5.7 %collective-permute-start.13 = (bf16[2048,768]{1,0:T(8,128)(2,1)S(1)}, bf16[2048,768]{1,0:T(8,128)(2,1)S(1)}, u32[]{:S(2)}, u32[]{:S(2)}) collective-permute-start(bf16[2048,768]{1,0:T(8,128)(2,1)S(1)} %convolution_convert_fusion.1), channel_id=1, source_target_pairs={{0,4},{4,0},{8,12},{12,8},{16,20},{20,16},{24,28},{28,24},{1,5},{5... | collective-permute-start | bytes 9437192 | tf_op jit(solution)/shard_map/ppermute | solution.py:116
  98.3 12.0 %collective-permute-start.15 = (bf16[256,768]{1,0:T(8,128)(2,1)S(1)}, bf16[256,768]{1,0:T(8,128)(2,1)S(1)}, u32[]{:S(2)}, u32[]{:S(2)}) collective-permute-start(bf16[256,768]{1,0:T(8,128)(2,1)S(1)} %get-tuple-element.37), channel_id=1, source_target_pairs={{0,8},{4,12},{8,0},{12,4},{16,24},{20,28},{24,16},{28,20},{1,9},{5... | collective-permute-start | bytes 1179656 | tf_op jit(solution)/shard_map/ppermute | solution.py:116
  99.9 18.0 %collective-permute-start.14 = (bf16[256,768]{1,0:T(8,128)(2,1)S(1)}, bf16[256,768]{1,0:T(8,128)(2,1)S(1)}, u32[]{:S(2)}, u32[]{:S(2)}) collective-permute-start(bf16[256,768]{1,0:T(8,128)(2,1)S(1)} %get-tuple-element.34), channel_id=1, source_target_pairs={{0,8},{4,12},{8,0},{12,4},{16,24},{20,28},{24,16},{28,20},{1,9},{5... | collective-permute-start | bytes 1179656 | tf_op jit(solution)/shard_map/ppermute | solution.py:116
  100.4 17.6 %collective-permute-start.18 = (bf16[256,768]{1,0:T(8,128)(2,1)S(1)}, bf16[256,768]{1,0:T(8,128)(2,1)S(1)}, u32[]{:S(2)}, u32[]{:S(2)}) collective-permute-start(bf16[256,768]{1,0:T(8,128)(2,1)S(1)} %get-tuple-element.35), channel_id=1, source_target_pairs={{0,16},{4,20},{8,24},{12,28},{16,0},{20,4},{24,8},{28,12},{1,17},{... | collective-permute-start | bytes 1179656 | tf_op jit(solution)/shard_map/ppermute | solution.py:116
  110.4 12.1 %collective-permute-start.16 = (bf16[256,768]{1,0:T(8,128)(2,1)S(1)}, bf16[256,768]{1,0:T(8,128)(2,1)S(1)}, u32[]{:S(2)}, u32[]{:S(2)}) collective-permute-start(bf16[256,768]{1,0:T(8,128)(2,1)S(1)} %add_convert_fusion.3), channel_id=1, source_target_pairs={{0,16},{4,20},{8,24},{12,28},{16,0},{20,4},{24,8},{28,12},{1,17},{... | collective-permute-start | bytes 1179656 | tf_op jit(solution)/shard_map/ppermute | solution.py:116
  111.2 17.3 %collective-permute-start.17 = (bf16[256,768]{1,0:T(8,128)(2,1)S(1)}, bf16[256,768]{1,0:T(8,128)(2,1)S(1)}, u32[]{:S(2)}, u32[]{:S(2)}) collective-permute-start(bf16[256,768]{1,0:T(8,128)(2,1)S(1)} %get-tuple-element.36), channel_id=1, source_target_pairs={{0,16},{4,20},{8,24},{12,28},{16,0},{20,4},{24,8},{28,12},{1,17},{... | collective-permute-start | bytes 1179656 | tf_op jit(solution)/shard_map/ppermute | solution.py:116
  122.8 7.8 %collective-permute-start.19 = (bf16[256,768]{1,0:T(8,128)(2,1)S(1)}, bf16[256,768]{1,0:T(8,128)(2,1)S(1)}, u32[]{:S(2)}, u32[]{:S(2)}) collective-permute-start(bf16[256,768]{1,0:T(8,128)(2,1)S(1)} %get-tuple-element.33), channel_id=1, source_target_pairs={{0,8},{4,12},{8,0},{12,4},{16,24},{20,28},{24,16},{28,20},{1,9},{5... | collective-permute-start | bytes 1179656 | tf_op jit(solution)/shard_map/ppermute | solution.py:116
  (10 other events, 81.8 us)
Sparse Core Ops, SparseCore 0:
  86.5 77.1 reduce-scatter.1

commit v2 on v1

v2 whole, which is shorter than its diff:
```python
import functools

import jax
import jax.numpy as jnp
from jax import lax
from jax.experimental import pallas as pl
from jax.experimental.pallas import tpu as pltpu
from jax.sharding import PartitionSpec as P

HEAD_DIM = 128
STATE = 128
HEADS = 4
WIDTH = HEADS * HEAD_DIM
STRIP = 128
EXTRA = 16

F32 = jnp.float32
BF16 = jnp.bfloat16
NN = (((1,), (0,)), ((), ()))
NT = (((1,), (1,)), ((), ()))
TN = (((0,), (0,)), ((), ()))


def mm(a, b, dims=NN):
    return lax.dot_general(a, b, dims, preferred_element_type=F32)


def call(kernel, outs, args, flops, place=None):
    scalars = [] if place is None else [place]
    moved = sum(a.size * a.dtype.itemsize for a in (*args, *outs))
    return pl.pallas_call(
        kernel,
        out_shape=outs,
        in_specs=[pl.BlockSpec(memory_space=pltpu.SMEM)] * len(scalars)
        + [pl.BlockSpec(memory_space=pltpu.VMEM)] * len(args),
        out_specs=[pl.BlockSpec(memory_space=pltpu.VMEM)] * len(outs),
        compiler_params=pltpu.CompilerParams(vmem_limit_bytes=40 * 2**20),
        cost_estimate=pl.CostEstimate(flops=flops, bytes_accessed=moved, transcendentals=0),
    )(*scalars, *args)


def head(h):
    return slice(h * HEAD_DIM, (h + 1) * HEAD_DIM)


def split(row, at, ref):
    rest = row
    for k in range(3):
        piece = rest.astype(BF16)
        ref[at + k : at + k + 1, :] = piece
        rest = rest - piece.astype(F32)


def whole(ref, at):
    return sum(ref[at + k : at + k + 1, :].astype(F32) for k in range(3))


def ends_kernel(proj, cot, to_end, growth, total, ends):
    in_map = proj[:, WIDTH : WIDTH + STATE]
    out_map = proj[:, WIDTH + STATE :]
    fed = [
        (proj[:, head(h)].astype(F32) * to_end[:, h : h + 1]).astype(BF16) for h in range(HEADS)
    ]
    grown = [
        (cot[:, head(h)].astype(F32) * growth[:, h : h + 1]).astype(BF16) for h in range(HEADS)
    ]
    ends[:STATE, :] = mm(in_map, jnp.concatenate(fed, axis=1), TN).astype(BF16)
    ends[STATE : 2 * STATE, :] = mm(out_map, jnp.concatenate(grown, axis=1), TN).astype(BF16)
    ends[2 * STATE :, :] = jnp.zeros((EXTRA, WIDTH), BF16)
    split(total[...], 2 * STATE, ends)


def pair_kernel(place, ends, near, for_x, for_y):
    own_total, near_total = whole(ends, 2 * STATE), whole(near, 2 * STATE)
    is_first = place[0] == 0
    one = jnp.ones_like(own_total)
    decay_own, decay_near = jnp.exp(own_total), jnp.exp(near_total)
    forward = ends[:STATE, :].astype(F32) * jnp.where(is_first, decay_near, one) + near[
        :STATE, :
    ].astype(F32) * jnp.where(is_first, one, decay_own)
    backward = ends[STATE : 2 * STATE, :].astype(F32) * jnp.where(is_first, one, decay_near) + near[
        STATE : 2 * STATE, :
    ].astype(F32) * jnp.where(is_first, decay_own, one)
    for out, low in ((for_x, place[1] % 2 == 0), (for_y, place[1] < 2)):
        out[:STATE, :] = jnp.where(low, forward, backward).astype(BF16)
        out[STATE:, :] = jnp.zeros((EXTRA, WIDTH), BF16)
        split(own_total + near_total, STATE, out)


def local_kernel(
    proj, cot, cum, cum_rows, step_rows, to_end, growth, y, dx, db, dc, fed, grown
):
    rows = proj.shape[0]
    for h in range(HEADS):
        fed[:, head(h)] = (proj[:, head(h)].astype(F32) * to_end[:, h : h + 1]).astype(BF16)
        grown[:, head(h)] = (cot[:, head(h)].astype(F32) * growth[:, h : h + 1]).astype(BF16)
    dx[...] = jnp.zeros_like(dx)
    db[...] = jnp.zeros_like(db)
    for at in range(0, rows, STRIP):
        upto = at + STRIP
        here = slice(at, upto)
        in_map = proj[:upto, WIDTH : WIDTH + STATE]
        out_map = proj[here, WIDTH + STATE :]
        scores = mm(out_map, in_map, NT)
        t = lax.broadcasted_iota(jnp.int32, (STRIP, upto), 0) + at
        s = lax.broadcasted_iota(jnp.int32, (STRIP, upto), 1)
        causal = t >= s
        dscores = jnp.zeros_like(scores)
        for h in range(HEADS):
            span = cum[here, h : h + 1] - cum_rows[h : h + 1, :upto]
            factor = jnp.exp(jnp.where(causal, span, -1e30)) * step_rows[h : h + 1, :upto]
            mixing = (scores * factor).astype(BF16)
            values = proj[:upto, head(h)]
            grad = cot[here, head(h)]
            y[here, head(h)] = mm(mixing, values)
            dx[:upto, head(h)] += mm(mixing, grad, TN)
            dscores = dscores + mm(grad, values, NT) * factor
        dscores = dscores.astype(BF16)
        dc[here, :] = mm(dscores, in_map)
        db[:upto, :] += mm(dscores, out_map, TN)


def enter(place, ends, near, far):
    core, chip = place[0], place[1]
    own_total, near_total = whole(ends, 2 * STATE), whole(near, 2 * STATE)
    sums = [own_total + near_total] + [whole(part, STATE) for part in far]
    of_chip = [
        sum(jnp.where((chip ^ bit) == j, sums[bit], 0.0) for bit in range(4)) for j in range(4)
    ]
    decay = jnp.exp(near_total)
    before = jnp.zeros((STATE, WIDTH), F32)
    after = jnp.zeros((STATE, WIDTH), F32)
    for bit in (1, 2, 3):
        there = chip ^ bit
        low, high = jnp.minimum(chip, there), jnp.maximum(chip, there)
        between = sum(jnp.where((j > low) & (j < high), of_chip[j], 0.0) for j in range(4))
        weight = jnp.exp(between)
        value = far[bit - 1][:STATE, :].astype(F32) * weight
        before = before + jnp.where(there < chip, value, 0.0)
        after = after + jnp.where(there > chip, value, 0.0)
    before = jnp.where(core == 1, before * decay + near[:STATE, :].astype(F32), before)
    after = jnp.where(core == 0, after * decay + near[STATE : 2 * STATE, :].astype(F32), after)
    return before.astype(BF16), after.astype(BF16)


def join_kernel(square, place, proj, to_end, dx, db, dc, fed, grown, *rest):
    ends, (proj_grad, turned, entering) = rest[:-3], rest[-3:]
    if square:
        before, after = enter(place, ends[0], ends[1], ends[2:])
    else:
        before, after = ends[0][:STATE, :], ends[0][STATE:, :]
    entering[...] = before
    carried = mm(proj[:, WIDTH : WIDTH + STATE], after)
    for h in range(HEADS):
        proj_grad[:, head(h)] = (dx[:, head(h)] + carried[:, head(h)] * to_end[:, h : h + 1]).astype(BF16)
    proj_grad[:, WIDTH : WIDTH + STATE] = (db[...] + mm(fed[...], after, NT)).astype(BF16)
    proj_grad[:, WIDTH + STATE :] = (dc[...] + mm(grown[...], before, NT)).astype(BF16)
    turned[...] = proj_grad[...].T


def output_kernel(proj, entering, growth, y, out):
    carried = mm(proj[:, WIDTH + STATE :], entering[...])
    for h in range(HEADS):
        out[:, head(h)] = y[:, head(h)] + carried[:, head(h)] * growth[:, h : h + 1]


def swap(value, size, bit):
    return lax.ppermute(value, "seq", [(i, i ^ bit) for i in range(size)])


def once(value, *others):
    return lax.optimization_barrier((value, *others))[0]


def reduce_on_line(weights, grad, group, beside):
    weights = weights.reshape(4, -1, weights.shape[-1])
    low = group < 2

    def product(at):
        return mm(lax.dynamic_index_in_dim(weights, at, 0, keepdims=False), grad)

    def send(value, pairs):
        return lax.ppermute(value.astype(BF16), "fsdp", pairs)

    inward, across, outward = [(0, 1), (3, 2)], [(1, 2), (2, 1)], [(1, 0), (2, 3)]
    far = product(jnp.where(low, 3, 0)).astype(BF16)
    middle = product(jnp.where(low, 2, 1)).astype(BF16)
    near = product(group ^ 1).astype(BF16)
    far_in, middle_in, near_in = send(far, inward), send(middle, inward), send(near, inward)
    beside[0]((far, middle, near))
    far_in = once(far_in, *beside[1]())
    far_across = send(far.astype(F32) + far_in.astype(F32), across)
    middle_in = once(middle_in, *beside[2]())
    middle_across = send(middle.astype(F32) + middle_in.astype(F32), across)
    far_out = send(near.astype(F32) + far_across.astype(F32), outward)
    own = once(product(group), *beside[3]())
    own = own + near_in.astype(F32) + middle_across.astype(F32) + far_out.astype(F32)
    return own.astype(BF16)


def spread(row):
    return jnp.repeat(row, HEAD_DIM, axis=-1)


def shards(tokens, w_in, step_logit, decay_logit, cotangent):
    size = lax.axis_size("seq")
    me = lax.axis_index("seq")
    core, chip = me % 2, me // 2
    square = size == 8
    rows, columns = tokens.shape[0], w_in.shape[1]
    part = w_in.shape[0]
    half = part // 2
    state = jax.ShapeDtypeStruct

    place = jnp.stack([core, chip]).astype(jnp.int32)

    if square:
        from_x, from_y = swap(w_in, size, 2), swap(w_in, size, 4)
        near = swap(w_in, size, 1)
        corner0 = swap(from_x[:half], size, 4)
        corner1 = swap(from_y[half:], size, 2)
        near_x, near_y = swap(from_x, size, 1), swap(from_y, size, 1)
        near0, near1 = swap(corner0, size, 1), swap(corner1, size, 1)
        pieces = [(0, 0, w_in), (1, 0, near), (2, 0, from_x), (4, 0, from_y), (3, 0, near_x), (5, 0, near_y)]
        pieces += [(6, 0, corner0), (6, half, corner1), (7, 0, near0), (7, half, near1)]
        ordered = jnp.concatenate(
            [
                lax.dynamic_slice_in_dim(tokens, (me ^ bit) * part, part, axis=1)
                for bit in (1, 3, 5, 7, 0, 2, 4, 6)
            ],
            axis=1,
        )
        to_near, to_keep = ordered[:, : 4 * part], ordered[:, 4 * part :]
        total = 0.0
        for bit, first, piece in pieces:
            at = (bit // 2 + (0 if bit % 2 else 4)) * part + first
            total = total + mm(ordered[:, at : at + piece.shape[0]], piece)
        projected = total.astype(BF16)
        gathered = jnp.zeros((size, part, columns), BF16)
        for bit, first, piece in pieces:
            gathered = lax.dynamic_update_slice(gathered, piece[None], (me ^ bit, first, 0))
    else:
        gathered = lax.all_gather(w_in, "seq", axis=0, tiled=True)
        projected = mm(tokens, gathered).astype(BF16)
        gathered = gathered.reshape(size, part, columns)

    step_size = jax.nn.softplus(step_logit)
    log_decay = -jax.nn.softplus(decay_logit)
    lower = (
        lax.broadcasted_iota(jnp.int32, (rows, rows), 0) >= lax.broadcasted_iota(jnp.int32, (rows, rows), 1)
    ).astype(F32)
    cum = lax.dot_general(lower, log_decay, NN, precision=lax.Precision.HIGHEST, preferred_element_type=F32)
    log_total = cum[-1]
    growth = jnp.exp(cum)
    to_end = jnp.exp(log_total[None] - cum) * step_size
    cum_rows, step_rows = cum.T, step_size.T
    (ends,) = call(
        ends_kernel,
        [state((2 * STATE + EXTRA, WIDTH), BF16)],
        [projected, cotangent, to_end, growth, spread(log_total)[None]],
        4 * rows * STATE * WIDTH,
    )
    if square:
        near = swap(ends, size, 1)
        for_x, for_y = call(
            pair_kernel, [state((STATE + EXTRA, WIDTH), BF16)] * 2, [ends, near], 0, place
        )
        ends = [ends, near, swap(for_x, size, 2), swap(for_y, size, 4), swap(for_y, size, 6)]
    else:
        everything = lax.all_gather(ends[: 2 * STATE], "seq")
        totals = lax.all_gather(log_total, "seq")
        places = jnp.arange(size)
        until = jnp.stack([jnp.sum(jnp.where((places < k)[:, None], totals, 0.0), axis=0) for k in range(size + 1)])
        reach = jnp.where((places < me)[:, None], until[me][None] - until[1:], -1e30)
        before = jnp.einsum("jnk,jk->nk", everything[:, :STATE].astype(F32), spread(jnp.exp(reach)))
        reach = jnp.where((places > me)[:, None], until[:-1] - until[me + 1][None], -1e30)
        after = jnp.einsum("jnk,jk->nk", everything[:, STATE:].astype(F32), spread(jnp.exp(reach)))
        ends = [jnp.concatenate([before, after]).astype(BF16)]

    y, dx, db, dc, fed, grown = call(
        local_kernel,
        [
            state((rows, WIDTH), F32),
            state((rows, WIDTH), F32),
            state((rows, STATE), F32),
            state((rows, STATE), F32),
            state((rows, WIDTH), BF16),
            state((rows, WIDTH), BF16),
        ],
        [projected, cotangent, cum, cum_rows, step_rows, to_end, growth],
        20 * rows * rows * STATE,
    )
    dx, gathered = lax.optimization_barrier((dx, gathered))
    proj_grad, turned, entering = call(
        functools.partial(join_kernel, square),
        [state((rows, columns), BF16), state((columns, rows), BF16), state((STATE, WIDTH), BF16)],
        [projected, to_end, dx, db, dc, fed, grown, *ends],
        6 * rows * STATE * WIDTH,
        place,
    )
    groups, group = lax.axis_size("fsdp"), lax.axis_index("fsdp")
    kept, sent, out = [], [], []

    def near_products(last):
        products = mm(to_near, once(proj_grad, *last), TN).astype(BF16)
        kept.append(swap(products, size, 1))

    def kept_products():
        kept[0] = (mm(to_keep, proj_grad, TN) + kept[0].astype(F32)).astype(BF16)
        own, for_x, for_y, for_corner = kept[0].reshape(4, part, columns)
        sent.extend((own, for_x, for_y, swap(for_corner[:half], size, 2), swap(for_corner[half:], size, 4)))
        sent.extend((swap(for_x[:half], size, 2), swap(for_y[half:], size, 4)))
        return (kept[0],)

    def corner_sums():
        own, for_x, for_y, corner_x, corner_y, top, low = sent
        last_x = (for_x[half:].astype(F32) + corner_y.astype(F32)).astype(BF16)
        last_y = (for_y[:half].astype(F32) + corner_x.astype(F32)).astype(BF16)
        sent.extend((swap(last_x, size, 2), swap(last_y, size, 4)))
        return last_x, last_y

    def outputs():
        out.extend(
            call(
                output_kernel,
                [state((rows, WIDTH), F32)],
                [projected, entering, growth, y],
                2 * rows * STATE * WIDTH,
            )
        )
        return tuple(out)

    if square and groups == 4:
        input_grad = reduce_on_line(gathered, turned, group, (near_products, kept_products, corner_sums, outputs))
    else:
        input_grad = lax.psum_scatter(
            mm(gathered.reshape(part * size, columns), turned).astype(BF16), "fsdp", scatter_dimension=0, tiled=True
        )
        outputs()
    (layer_out,) = out

    if square and groups == 4:
        own, for_x, for_y, corner_x, corner_y, top, low, low_x, top_y = sent
        w_in_grad = jnp.concatenate(
            [
                own[:half].astype(F32) + top.astype(F32) + top_y.astype(F32),
                own[half:].astype(F32) + low.astype(F32) + low_x.astype(F32),
            ]
        )
    else:
        w_in_grad = lax.psum_scatter(
            mm(tokens, proj_grad, TN).astype(BF16), "seq", scatter_dimension=0, tiled=True
        ).astype(F32)
    return (layer_out, input_grad, w_in_grad)


def solution(mesh):
    across = P("seq", "fsdp")
    return jax.shard_map(
        shards,
        mesh=mesh,
        in_specs=(P("seq", None), across, across, across, across),
        out_specs=(across, P("fsdp", "seq"), across),
        check_vma=False,
    )
```

time: 171 us -> 151 us (0.88)
  blocking collectives: 17.2 us -> 0 us
  starting transfers between devices: 19.1 us -> 35.5 us
  between operations: 14.5 us -> 1.29 us
  local copies, waits for them, and re-layouts: 18.7 us -> 8.88 us
  other arithmetic: 3.64 us -> 13.4 us
  matrix products: 25.6 us -> 21.3 us
  waiting for transfers between devices: 66.4 us -> 62.7 us
    ppermute x0 -> x6, waiting for transfers between devices: none -> 38.5 us  [send(): return lax.ppermute(value.astype(BF16), 'fsdp', pairs)]
    reduce_scatter x1 -> x0, waiting for transfers between devices: 31.7 us -> none  [shards(): lax.psum_scatter(mm(gathered, proj_grad, NT).astype(BF16), 'fsdp', scatte...]
    all_gather x1 -> x0, blocking collectives: 17.2 us -> none  [shards(): totals = lax.all_gather(log_total, 'seq')]
    ppermute x0 -> x6, starting transfers between devices: none -> 16.7 us  [send(): return lax.ppermute(value.astype(BF16), 'fsdp', pairs)]
    ppermute x20, waiting for transfers between devices: 34.7 us -> 24.3 us  [swap(): return lax.ppermute(value, 'seq', [(i, i ^ bit) for i in range(size)])]
    dynamic_update_slice x10, local copies, waits for them, and re-layouts: 9.88 us -> 0.49 us  [shards(): lax.dynamic_update_slice(gathered, piece[None], (me ^ bit, first, 0))]
    convert_element_type x2 -> x5, other arithmetic: 0.25 us -> 8.49 us  [the longest x3 4.03 us: send(): return lax.ppermute(value.astype(BF16), 'fsdp', pairs)]
    dot_general x13 -> x16, matrix products: 24.5 us -> 20.2 us  [mm(): return lax.dot_general(a, b, dims, preferred_element_type=F32)]
  transfers between devices with their start and end apart: 21 -> 26, of which waited for: 10 -> 13; matrix products, arithmetic and copies ran while one was open for 22% -> 20% of each run, Pallas kernels for 2% -> 3%
where the time goes in v2:
time: 151 us; the launch traced here: 150 us
  waiting for transfers between devices  62.7 us (42%)
  starting transfers between devices  35.5 us (24%)
  matrix products  21.3 us (14%)
  other arithmetic  13.4 us (9%)
  local copies, waits for them, and re-layouts  8.88 us (6%)
  Pallas kernels  7.05 us (5%)
    ppermute x6, waiting for transfers between devices, send(): return lax.ppermute(value.astype(BF16), 'fsdp', pairs)  38.5 us
    ppermute x20, waiting for transfers between devices, swap(): return lax.ppermute(value, 'seq', [(i, i ^ bit) for i in range(size)])  24.3 us
    dot_general x16, matrix products, mm(): return lax.dot_general(a, b, dims, preferred_element_type=F32)  20.2 us
    ppermute x20, starting transfers between devices, swap(): return lax.ppermute(value, 'seq', [(i, i ^ bit) for i in range(size)])  18.9 us
    ppermute x6, starting transfers between devices, send(): return lax.ppermute(value.astype(BF16), 'fsdp', pairs)  16.7 us
    pallas_call x5, Pallas kernels, call(): pl.pallas_call(kernel, out_shape=outs, in_specs=[pl.BlockSpec(memory_spac...  7.05 us
    convert_element_type x3, other arithmetic, send(): return lax.ppermute(value.astype(BF16), 'fsdp', pairs)  4.03 us
    dynamic_slice x1, local copies, waits for them, and re-layouts, shards(): lax.dynamic_slice_in_dim(tokens, (me ^ bit) * part, part, axis=1)  3.63 us
  transfers between devices with their start and end apart: 26, of which 13 were waited for; matrix products, arithmetic and copies ran while one was open for 20% of the time, Pallas kernels for 3%

profile of v2, /device:TPU:0, one launch (start us, length us, event | category | flops | bytes accessed | tf_op | source)
XLA Modules:
  0.0 150.1 jit_solution(15748634220946267837)
XLA Ops:
  1.1 2.6 %collective-permute-start.1 = (bf16[512,768]{1,0:T(8,128)(2,1)}, bf16[512,768]{1,0:T(8,128)(2,1)S(1)}, u32[]{:S(2)}, u32[]{:S(2)}) collective-permute-start(bf16[512,768]{1,0:T(8,128)(2,1)} %param.6), channel_id=1, source_target_pairs={{0,8},{4,12},{8,0},{12,4},{16,24},{20,28},{24,16},{28,20},{1,9},{5... | collective-permute-start | bytes 2359304 | tf_op jit(solution)/shard_map/ppermute | solution.py:168
  6.7 1.6 %copy.37 = f32[512,4]{1,0:T(8,128)} copy(f32[512,4]{0,1:T(4,128)} %param.7) | data formatting | bytes 16384 | tf_op args[2]
  10.7 3.6 %constant_dynamic-slice_fusion.1 = (bf16[512,512]{1,0:T(8,128)(2,1)}, bf16[512,512]{1,0:T(8,128)(2,1)S(1)}, bf16[512,512]{1,0:T(8,128)(2,1)S(1)}, bf16[512,512]{...) fusion(bf16[512,4096]{1,0:T(8,128)(2,1)} %param.5, ...), kind=kLoop, calls=%fused_computation.81 | loop fusion | bytes 8388640 | tf_op jit(solution)/shard_map/dynamic_slice | solution.py:228
  15.5 6.6 %collective-permute-done.1 = bf16[512,768]{1,0:T(8,128)(2,1)S(1)} collective-permute-done((bf16[512,768]{1,0:T(8,128)(2,1)}, bf16[512,768]{1,0:T(8,128)(2,1)S(1)}, u32[]{:S(2)}, u32[]{:S(2)}) %collective-permute-start.1) | collective-permute-done | bytes 786464 | tf_op jit(solution)/shard_map/ppermute | solution.py:168
  22.1 1.9 %collective-permute-start.5 = (bf16[256,768]{1,0:T(8,128)(2,1)S(1)}, bf16[256,768]{1,0:T(8,128)(2,1)S(1)}, u32[]{:S(2)}, u32[]{:S(2)}) collective-permute-start(bf16[256,768]{1,0:T(8,128)(2,1)S(1)} %slice.80), channel_id=1, source_target_pairs={{0,16},{4,20},{8,24},{12,28},{16,0},{20,4},{24,8},{28,12},{1,17},{... | collective-permute-start | bytes 1179656 | tf_op jit(solution)/shard_map/ppermute | solution.py:168
  28.0 5.0 %collective-permute-done.5 = bf16[256,768]{1,0:T(8,128)(2,1)S(1)} collective-permute-done((bf16[256,768]{1,0:T(8,128)(2,1)S(1)}, bf16[256,768]{1,0:T(8,128)(2,1)S(1)}, u32[]{:S(2)}, u32[]{:S(2)}) %collective-permute-start.5) | collective-permute-done | bytes 393248 | tf_op jit(solution)/shard_map/ppermute | solution.py:168
  39.8 1.8 %add_convert_fusion.5.proj = bf16[512,768]{1,0:T(8,128)(2,1)S(1)} fusion(f32[512,768]{1,0:T(8,128)S(1)} %fusion.40, f32[512,768]{1,0:T(8,128)S(1)} %fusion.42, f32[512,768]{1,0:T(8,128)S(1)} %fusion.44, f32[512,768]{1,0:T(8,128)S(1)} %fusion.73, f32[512,768]{1,0:T(8,128)S(1)} %fusion.72, f32[512,768]{1,0:T(8,128)S(1)} %fusion.71, ...), kind=kOutput, calls=%fused_computation.33 | convolution fusion | flops 205258752 | bytes 15597572 | tf_op jit(solution)/shard_map/dot_general | solution.py:25
  46.2 1.9 %collective-permute-start.12 = (bf16[144,512]{1,0:T(8,128)(2,1)S(1)}, bf16[144,512]{1,0:T(8,128)(2,1)S(1)}, u32[]{:S(2)}, u32[]{:S(2)}) collective-permute-start(bf16[144,512]{1,0:T(8,128)(2,1)S(1)} %get-tuple-element.27), channel_id=1, source_target_pairs={{0,24},{4,28},{8,16},{12,20},{16,8},{20,12},{24,0},{28,4},{1,25},{... | collective-permute-start | bytes 442376 | tf_op jit(solution)/shard_map/ppermute | solution.py:168
  48.6 2.5 %shard_map.76 = (f32[512,512]{1,0:T(8,128)S(1)}, f32[512,512]{1,0:T(8,128)S(1)}, f32[512,128]{1,0:T(8,128)S(1)}, f32[512,128]{1,0:T(8,128)S(1)}, bf16[512,512]{1...) custom-call(bf16[512,768]{1,0:T(8,128)(2,1)S(1)} %add_convert_fusion.5.proj, bf16[512,512]{1,0:T(8,128)(2,1)S(1)} %copy-done, ...), custom_call_target="tpu_custom_call" | custom-call | flops 671088640 | bytes 5021696 | tf_op jit(solution)/shard_map/pallas_call | solution.py:31
  51.2 4.4 %collective-permute-done.10.rest_2_ = bf16[144,512]{1,0:T(8,128)(2,1)S(1)} collective-permute-done((bf16[144,512]{1,0:T(8,128)(2,1)S(1)}, bf16[144,512]{1,0:T(8,128)(2,1)S(1)}, u32[]{:S(2)}, u32[]{:S(2)}) %collective-permute-start.10) | collective-permute-done | bytes 147488 | tf_op jit(solution)/shard_map/ppermute | solution.py:168
  57.1 2.0 %fusion.26 = bf16[1024,512]{1,0:T(8,128)(2,1)} fusion(bf16[768,512]{1,0:T(8,128)(2,1)S(1)} %get-tuple-element.31, bf16[4,1024,768]{2,1,0:T(8,128)(2,1)S(1)} %bitcast.69, s32[]{:T(128)S(6)} %select_n.106), kind=kOutput, calls=%fused_computation.34 | convolution fusion | flops 805830656 | bytes 3407876 | tf_op jit(solution)/shard_map/dot_general | solution.py:25
  61.8 1.9 %convolution_convert_fusion = bf16[2048,768]{1,0:T(8,128)(2,1)S(1)} fusion(bf16[512,768]{1,0:T(8,128)(2,1)S(1)} %get-tuple-element.34, bf16[512,512]{1,0:T(8,128)(2,1)S(1)} %copy-done.23, bf16[512,512]{1,0:T(8,128)(2,1)S(1)} %copy-done.13, bf16[512,512]{1,0:T(8,128)(2,1)S(1)} %copy-done.15, bf16[512,512]{1,0:T(8,128)(2,1)S(1)} %copy-done.17), kind=kOutput, calls=%fused_computation.1 | convolution fusion | flops 1620574208 | bytes 6029312 | tf_op jit(solution)/shard_map/dot_general | solution.py:25
  63.7 3.6 %collective-permute-start.19 = (bf16[1024,512]{1,0:T(8,128)(2,1)S(1)}, bf16[1024,512]{1,0:T(8,128)(2,1)S(1)}, u32[]{:S(2)}, u32[]{:S(2)}) collective-permute-start(bf16[1024,512]{1,0:T(8,128)(2,1)S(1)} %fusion.32), channel_id=1, source_target_pairs={{0,1},{3,2},{4,5},{7,6},{8,9},{11,10},{12,13},{15,14},{16,17},{19,... | collective-permute-start | bytes 3145736 | tf_op jit(solution)/shard_map/ppermute | solution.py:183
  69.4 2.5 %add_convert_fusion = bf16[2048,768]{1,0:T(8,128)(2,1)S(1)} fusion(bf16[2048,768]{1,0:T(8,128)(2,1)S(1)} %collective-permute-done.15, bf16[512,768]{1,0:T(8,128)(2,1)S(1)} %get-tuple-element.34, bf16[512,512]{1,0:T(8,128)(2,1)S(1)} %copy-done.22, bf16[512,512]{1,0:T(8,128)(2,1)S(1)} %copy-done.7, bf16[512,512]{1,0:T(8,128)(2,1)S(1)} %copy-done.9, ...), kind=kOutput, calls=%fused_computation | convolution fusion | flops 1623719936 | bytes 9175040 | tf_op jit(solution)/shard_map/dot_general | solution.py:25
  71.9 18.7 %collective-permute-done.19 = bf16[1024,512]{1,0:T(8,128)(2,1)S(1)} collective-permute-done((bf16[1024,512]{1,0:T(8,128)(2,1)S(1)}, bf16[1024,512]{1,0:T(8,128)(2,1)S(1)}, u32[]{:S(2)}, u32[]{:S(2)}) %collective-permute-start.19) | collective-permute-done | bytes 1048608 | tf_op jit(solution)/shard_map/ppermute | solution.py:183
  93.8 8.1 %collective-permute-start.13 = (bf16[1024,512]{1,0:T(8,128)(2,1)}, bf16[1024,512]{1,0:T(8,128)(2,1)}, u32[]{:S(2)}, u32[]{:S(2)}) collective-permute-start(bf16[1024,512]{1,0:T(8,128)(2,1)} %fusion.26), channel_id=1, source_target_pairs={{0,1},{3,2},{4,5},{7,6},{8,9},{11,10},{12,13},{15,14},{16,17},{19,... | collective-permute-start | bytes 3145736 | tf_op jit(solution)/shard_map/ppermute | solution.py:183
  105.2 7.9 %collective-permute-done.14 = bf16[1024,512]{1,0:T(8,128)(2,1)S(1)} collective-permute-done((bf16[1024,512]{1,0:T(8,128)(2,1)S(1)}, bf16[1024,512]{1,0:T(8,128)(2,1)S(1)}, u32[]{:S(2)}, u32[]{:S(2)}) %collective-permute-start.14) | collective-permute-done | bytes 1048608 | tf_op jit(solution)/shard_map/ppermute | solution.py:183
  114.4 1.6 %collective-permute-start.18 = (bf16[1024,512]{1,0:T(8,128)(2,1)}, bf16[1024,512]{1,0:T(8,128)(2,1)}, u32[]{:S(2)}, u32[]{:S(2)}) collective-permute-start(bf16[1024,512]{1,0:T(8,128)(2,1)} %add_convert_fusion.4), channel_id=1, source_target_pairs={{1,2},{2,1},{5,6},{6,5},{9,10},{10,9},{13,14},{14,13},{17,18},{18,... | collective-permute-start | bytes 3145736 | tf_op jit(solution)/shard_map/ppermute | solution.py:183
  116.1 2.5 %add_convert_fusion.2 = bf16[1024,512]{1,0:T(8,128)(2,1)} fusion(bf16[1024,512]{1,0:T(8,128)(2,1)S(1)} %collective-permute-done.20, bf16[1024,512]{1,0:T(8,128)(2,1)} %fusion.26), kind=kLoop, calls=%fused_computation.17 | loop fusion | flops 2097152 | bytes 3145728 | tf_op jit(solution)/shard_map/convert_element_type | solution.py:183
  124.1 2.4 %fusion.20 = f32[1024,512]{1,0:T(8,128)S(1)} fusion(bf16[768,512]{1,0:T(8,128)(2,1)S(1)} %get-tuple-element.31, bf16[4,1024,768]{2,1,0:T(8,128)(2,1)} %bitcast.72, s32[]{:T(128)S(6)} %select_n.105), kind=kOutput, calls=%fused_computation.27 | convolution fusion | flops 805306368 | bytes 4456452 | tf_op jit(solution)/shard_map/dot_general | solution.py:25
  126.6 3.9 %collective-permute-done.23 = bf16[256,768]{1,0:T(8,128)(2,1)} collective-permute-done((bf16[256,768]{1,0:T(8,128)(2,1)}, bf16[256,768]{1,0:T(8,128)(2,1)}, u32[]{:S(2)}, u32[]{:S(2)}) %collective-permute-start.23) | collective-permute-done | bytes 393248 | tf_op jit(solution)/shard_map/ppermute | solution.py:168
  132.1 1.6 %convert_add_fusion.1 = (f32[256,768]{1,0:T(8,128)S(1)}, f32[256,768]{1,0:T(8,128)S(1)}) fusion(bf16[256,768]{1,0:T(8,128)(2,1)} %collective-permute-done.23, bf16[256,768]{1,0:T(8,128)(2,1)S(1)} %copy-done.25, bf16[2048,768]{1,0:T(8,128)(2,1)} %copy-done.5, bf16[256,768]{1,0:T(8,128)(2,1)} %collective-permute-done.25, bf16[256,768]{1,0:T(8,128)(2,1)S(1)} %copy-done.27), kind=kLoop, calls=%fused_computation.46 | loop fusion | flops 1966080 | bytes 3932160 | tf_op jit(solution)/shard_map/add | solution.py:346
  135.3 11.5 %collective-permute-done.21 = bf16[1024,512]{1,0:T(8,128)(2,1)} collective-permute-done((bf16[1024,512]{1,0:T(8,128)(2,1)}, bf16[1024,512]{1,0:T(8,128)(2,1)}, u32[]{:S(2)}, u32[]{:S(2)}) %collective-permute-start.21) | collective-permute-done | bytes 1048608 | tf_op jit(solution)/shard_map/ppermute | solution.py:183
  146.8 3.4 %add_convert_fusion.1 = bf16[1024,512]{1,0:T(8,128)(2,1)} fusion(bf16[1024,512]{1,0:T(8,128)(2,1)} %collective-permute-done.21, bf16[1024,512]{1,0:T(8,128)(2,1)} %collective-permute-done.18, f32[1024,512]{1,0:T(8,128)S(1)} %fusion.20, bf16[1024,512]{1,0:T(8,128)(2,1)} %collective-permute-done.13), kind=kLoop, calls=%fused_computation.16 | loop fusion | flops 3670016 | bytes 6291456 | tf_op jit(solution)/shard_map/convert_element_type | solution.py:198
  (137 shorter events, 45.5 us)
Async XLA Ops:
  0.6 26.6 %collective-permute-start = (bf16[512,768]{1,0:T(8,128)(2,1)}, bf16[512,768]{1,0:T(8,128)(2,1)S(1)}, u32[]{:S(2)}, u32[]{:S(2)}) collective-permute-start(bf16[512,768]{1,0:T(8,128)(2,1)} %param.6), channel_id=1, source_target_pairs={{0,4},{4,0},{8,12},{12,8},{16,20},{20,16},{24,28},{28,24},{1,5},{5... | collective-permute-start | bytes 2359304 | tf_op jit(solution)/shard_map/ppermute | solution.py:168
  1.1 20.9 %collective-permute-start.1 = (bf16[512,768]{1,0:T(8,128)(2,1)}, bf16[512,768]{1,0:T(8,128)(2,1)S(1)}, u32[]{:S(2)}, u32[]{:S(2)}) collective-permute-start(bf16[512,768]{1,0:T(8,128)(2,1)} %param.6), channel_id=1, source_target_pairs={{0,8},{4,12},{8,0},{12,4},{16,24},{20,28},{24,16},{28,20},{1,9},{5... | collective-permute-start | bytes 2359304 | tf_op jit(solution)/shard_map/ppermute | solution.py:168
  3.7 20.2 %collective-permute-start.2 = (bf16[512,768]{1,0:T(8,128)(2,1)}, bf16[512,768]{1,0:T(8,128)(2,1)S(1)}, u32[]{:S(2)}, u32[]{:S(2)}) collective-permute-start(bf16[512,768]{1,0:T(8,128)(2,1)} %param.6), channel_id=1, source_target_pairs={{0,16},{4,20},{8,24},{12,28},{16,0},{20,4},{24,8},{28,12},{1,17},{... | collective-permute-start | bytes 2359304 | tf_op jit(solution)/shard_map/ppermute | solution.py:168
  22.1 10.9 %collective-permute-start.5 = (bf16[256,768]{1,0:T(8,128)(2,1)S(1)}, bf16[256,768]{1,0:T(8,128)(2,1)S(1)}, u32[]{:S(2)}, u32[]{:S(2)}) collective-permute-start(bf16[256,768]{1,0:T(8,128)(2,1)S(1)} %slice.80), channel_id=1, source_target_pairs={{0,16},{4,20},{8,24},{12,28},{16,0},{20,4},{24,8},{28,12},{1,17},{... | collective-permute-start | bytes 1179656 | tf_op jit(solution)/shard_map/ppermute | solution.py:168
  24.0 10.5 %collective-permute-start.6 = (bf16[256,768]{1,0:T(8,128)(2,1)S(1)}, bf16[256,768]{1,0:T(8,128)(2,1)S(1)}, u32[]{:S(2)}, u32[]{:S(2)}) collective-permute-start(bf16[256,768]{1,0:T(8,128)(2,1)S(1)} %slice.81), channel_id=1, source_target_pairs={{0,8},{4,12},{8,0},{12,4},{16,24},{20,28},{24,16},{28,20},{1,9},{5... | collective-permute-start | bytes 1179656 | tf_op jit(solution)/shard_map/ppermute | solution.py:168
  25.5 11.7 %collective-permute-start.3 = (bf16[512,768]{1,0:T(8,128)(2,1)S(1)}, bf16[512,768]{1,0:T(8,128)(2,1)S(1)}, u32[]{:S(2)}, u32[]{:S(2)}) collective-permute-start(bf16[512,768]{1,0:T(8,128)(2,1)S(1)} %collective-permute-done.1), channel_id=1, source_target_pairs={{0,4},{4,0},{8,12},{12,8},{16,20},{20,16},{24,28},{28,24},{1,5},{5... | collective-permute-start | bytes 2359304 | tf_op jit(solution)/shard_map/ppermute | solution.py:168
  25.5 13.7 %collective-permute-start.4 = (bf16[512,768]{1,0:T(8,128)(2,1)S(1)}, bf16[512,768]{1,0:T(8,128)(2,1)S(1)}, u32[]{:S(2)}, u32[]{:S(2)}) collective-permute-start(bf16[512,768]{1,0:T(8,128)(2,1)S(1)} %collective-permute-done.2), channel_id=1, source_target_pairs={{0,4},{4,0},{8,12},{12,8},{16,20},{20,16},{24,28},{28,24},{1,5},{5... | collective-permute-start | bytes 2359304 | tf_op jit(solution)/shard_map/ppermute | solution.py:168
  34.4 5.4 %collective-permute-start.8 = (bf16[256,768]{1,0:T(8,128)(2,1)S(1)}, bf16[256,768]{1,0:T(8,128)(2,1)S(1)}, u32[]{:S(2)}, u32[]{:S(2)}) collective-permute-start(bf16[256,768]{1,0:T(8,128)(2,1)S(1)} %collective-permute-done.6), channel_id=1, source_target_pairs={{0,4},{4,0},{8,12},{12,8},{16,20},{20,16},{24,28},{28,24},{1,5},{5... | collective-permute-start | bytes 1179656 | tf_op jit(solution)/shard_map/ppermute | solution.py:168
  45.0 10.6 %collective-permute-start.11 = (bf16[144,512]{1,0:T(8,128)(2,1)S(1)}, bf16[144,512]{1,0:T(8,128)(2,1)S(1)}, u32[]{:S(2)}, u32[]{:S(2)}) collective-permute-start(bf16[144,512]{1,0:T(8,128)(2,1)S(1)} %get-tuple-element.27), channel_id=1, source_target_pairs={{0,16},{4,20},{8,24},{12,28},{16,0},{20,4},{24,8},{28,12},{1,17},{... | collective-permute-start | bytes 442376 | tf_op jit(solution)/shard_map/ppermute | solution.py:168
  46.2 9.4 %collective-permute-start.12 = (bf16[144,512]{1,0:T(8,128)(2,1)S(1)}, bf16[144,512]{1,0:T(8,128)(2,1)S(1)}, u32[]{:S(2)}, u32[]{:S(2)}) collective-permute-start(bf16[144,512]{1,0:T(8,128)(2,1)S(1)} %get-tuple-element.27), channel_id=1, source_target_pairs={{0,24},{4,28},{8,16},{12,20},{16,8},{20,12},{24,0},{28,4},{1,25},{... | collective-permute-start | bytes 442376 | tf_op jit(solution)/shard_map/ppermute | solution.py:168
  48.1 7.5 %collective-permute-start.10 = (bf16[144,512]{1,0:T(8,128)(2,1)S(1)}, bf16[144,512]{1,0:T(8,128)(2,1)S(1)}, u32[]{:S(2)}, u32[]{:S(2)}) collective-permute-start(bf16[144,512]{1,0:T(8,128)(2,1)S(1)} %get-tuple-element.26), channel_id=1, source_target_pairs={{0,8},{4,12},{8,0},{12,4},{16,24},{20,28},{24,16},{28,20},{1,9},{5... | collective-permute-start | bytes 442376 | tf_op jit(solution)/shard_map/ppermute | solution.py:168
  63.6 5.7 %collective-permute-start.15 = (bf16[2048,768]{1,0:T(8,128)(2,1)S(1)}, bf16[2048,768]{1,0:T(8,128)(2,1)S(1)}, u32[]{:S(2)}, u32[]{:S(2)}) collective-permute-start(bf16[2048,768]{1,0:T(8,128)(2,1)S(1)} %convolution_convert_fusion), channel_id=1, source_target_pairs={{0,4},{4,0},{8,12},{12,8},{16,20},{20,16},{24,28},{28,24},{1,5},{5... | collective-permute-start | bytes 9437192 | tf_op jit(solution)/shard_map/ppermute | solution.py:168
  63.7 27.0 %collective-permute-start.19 = (bf16[1024,512]{1,0:T(8,128)(2,1)S(1)}, bf16[1024,512]{1,0:T(8,128)(2,1)S(1)}, u32[]{:S(2)}, u32[]{:S(2)}) collective-permute-start(bf16[1024,512]{1,0:T(8,128)(2,1)S(1)} %fusion.32), channel_id=1, source_target_pairs={{0,1},{3,2},{4,5},{7,6},{8,9},{11,10},{12,13},{15,14},{16,17},{19,... | collective-permute-start | bytes 3145736 | tf_op jit(solution)/shard_map/ppermute | solution.py:183
  67.3 45.9 %collective-permute-start.14 = (bf16[1024,512]{1,0:T(8,128)(2,1)S(1)}, bf16[1024,512]{1,0:T(8,128)(2,1)S(1)}, u32[]{:S(2)}, u32[]{:S(2)}) collective-permute-start(bf16[1024,512]{1,0:T(8,128)(2,1)S(1)} %fusion.29), channel_id=1, source_target_pairs={{0,1},{3,2},{4,5},{7,6},{8,9},{11,10},{12,13},{15,14},{16,17},{19,... | collective-permute-start | bytes 3145736 | tf_op jit(solution)/shard_map/ppermute | solution.py:183
  90.9 25.1 %collective-permute-start.20 = (bf16[1024,512]{1,0:T(8,128)(2,1)S(1)}, bf16[1024,512]{1,0:T(8,128)(2,1)S(1)}, u32[]{:S(2)}, u32[]{:S(2)}) collective-permute-start(bf16[1024,512]{1,0:T(8,128)(2,1)S(1)} %add_convert_fusion.3), channel_id=1, source_target_pairs={{1,2},{2,1},{5,6},{6,5},{9,10},{10,9},{13,14},{14,13},{17,18},{18,... | collective-permute-start | bytes 3145736 | tf_op jit(solution)/shard_map/ppermute | solution.py:183
  91.8 10.4 %collective-permute-start.16 = (bf16[256,768]{1,0:T(8,128)(2,1)S(1)}, bf16[256,768]{1,0:T(8,128)(2,1)S(1)}, u32[]{:S(2)}, u32[]{:S(2)}) collective-permute-start(bf16[256,768]{1,0:T(8,128)(2,1)S(1)} %get-tuple-element.50), channel_id=1, source_target_pairs={{0,16},{4,20},{8,24},{12,28},{16,0},{20,4},{24,8},{28,12},{1,17},{... | collective-permute-start | bytes 1179656 | tf_op jit(solution)/shard_map/ppermute | solution.py:168
  92.9 10.7 %collective-permute-start.17 = (bf16[256,768]{1,0:T(8,128)(2,1)S(1)}, bf16[256,768]{1,0:T(8,128)(2,1)S(1)}, u32[]{:S(2)}, u32[]{:S(2)}) collective-permute-start(bf16[256,768]{1,0:T(8,128)(2,1)S(1)} %get-tuple-element.49), channel_id=1, source_target_pairs={{0,8},{4,12},{8,0},{12,4},{16,24},{20,28},{24,16},{28,20},{1,9},{5... | collective-permute-start | bytes 1179656 | tf_op jit(solution)/shard_map/ppermute | solution.py:168
  93.8 41.4 %collective-permute-start.13 = (bf16[1024,512]{1,0:T(8,128)(2,1)}, bf16[1024,512]{1,0:T(8,128)(2,1)}, u32[]{:S(2)}, u32[]{:S(2)}) collective-permute-start(bf16[1024,512]{1,0:T(8,128)(2,1)} %fusion.26), channel_id=1, source_target_pairs={{0,1},{3,2},{4,5},{7,6},{8,9},{11,10},{12,13},{15,14},{16,17},{19,... | collective-permute-start | bytes 3145736 | tf_op jit(solution)/shard_map/ppermute | solution.py:183
  102.2 17.6 %collective-permute-start.22 = (bf16[256,768]{1,0:T(8,128)(2,1)S(1)}, bf16[256,768]{1,0:T(8,128)(2,1)S(1)}, u32[]{:S(2)}, u32[]{:S(2)}) collective-permute-start(bf16[256,768]{1,0:T(8,128)(2,1)S(1)} %get-tuple-element.47), channel_id=1, source_target_pairs={{0,8},{4,12},{8,0},{12,4},{16,24},{20,28},{24,16},{28,20},{1,9},{5... | collective-permute-start | bytes 1179656 | tf_op jit(solution)/shard_map/ppermute | solution.py:168
  103.7 17.3 %collective-permute-start.24 = (bf16[256,768]{1,0:T(8,128)(2,1)S(1)}, bf16[256,768]{1,0:T(8,128)(2,1)S(1)}, u32[]{:S(2)}, u32[]{:S(2)}) collective-permute-start(bf16[256,768]{1,0:T(8,128)(2,1)S(1)} %get-tuple-element.48), channel_id=1, source_target_pairs={{0,16},{4,20},{8,24},{12,28},{16,0},{20,4},{24,8},{28,12},{1,17},{... | collective-permute-start | bytes 1179656 | tf_op jit(solution)/shard_map/ppermute | solution.py:168
  114.4 20.9 %collective-permute-start.18 = (bf16[1024,512]{1,0:T(8,128)(2,1)}, bf16[1024,512]{1,0:T(8,128)(2,1)}, u32[]{:S(2)}, u32[]{:S(2)}) collective-permute-start(bf16[1024,512]{1,0:T(8,128)(2,1)} %add_convert_fusion.4), channel_id=1, source_target_pairs={{1,2},{2,1},{5,6},{6,5},{9,10},{10,9},{13,14},{14,13},{17,18},{18,... | collective-permute-start | bytes 3145736 | tf_op jit(solution)/shard_map/ppermute | solution.py:183
  118.5 28.3 %collective-permute-start.21 = (bf16[1024,512]{1,0:T(8,128)(2,1)}, bf16[1024,512]{1,0:T(8,128)(2,1)}, u32[]{:S(2)}, u32[]{:S(2)}) collective-permute-start(bf16[1024,512]{1,0:T(8,128)(2,1)} %add_convert_fusion.2), channel_id=1, source_target_pairs={{1,0},{2,3},{5,4},{6,7},{9,8},{10,11},{13,12},{14,15},{17,16},{18,... | collective-permute-start | bytes 3145736 | tf_op jit(solution)/shard_map/ppermute | solution.py:183
  119.8 10.7 %collective-permute-start.23 = (bf16[256,768]{1,0:T(8,128)(2,1)}, bf16[256,768]{1,0:T(8,128)(2,1)}, u32[]{:S(2)}, u32[]{:S(2)}) collective-permute-start(bf16[256,768]{1,0:T(8,128)(2,1)} %get-tuple-element.51), channel_id=1, source_target_pairs={{0,16},{4,20},{8,24},{12,28},{16,0},{20,4},{24,8},{28,12},{1,17},{... | collective-permute-start | bytes 1179656 | tf_op jit(solution)/shard_map/ppermute | solution.py:168
  121.7 10.4 %collective-permute-start.25 = (bf16[256,768]{1,0:T(8,128)(2,1)}, bf16[256,768]{1,0:T(8,128)(2,1)}, u32[]{:S(2)}, u32[]{:S(2)}) collective-permute-start(bf16[256,768]{1,0:T(8,128)(2,1)} %get-tuple-element.52), channel_id=1, source_target_pairs={{0,8},{4,12},{8,0},{12,4},{16,24},{20,28},{24,16},{28,20},{1,9},{5... | collective-permute-start | bytes 1179656 | tf_op jit(solution)/shard_map/ppermute | solution.py:168
  (30 other events, 207.8 us)

commit v3 on v2

--- a/solution.py
+++ b/solution.py
@@ -194,8 +194,8 @@
     middle_across = send(middle.astype(F32) + middle_in.astype(F32), across)
     far_out = send(near.astype(F32) + far_across.astype(F32), outward)
     own = once(product(group), *beside[3]())
-    own = own + near_in.astype(F32) + middle_across.astype(F32) + far_out.astype(F32)
-    return own.astype(BF16)
+    own, near_in, middle_across, far_out = lax.optimization_barrier((own, near_in, middle_across, far_out))
+    return (own + near_in.astype(F32) + middle_across.astype(F32) + far_out.astype(F32)).astype(BF16)
 
 
 def spread(row):
@@ -217,12 +217,10 @@
     if square:
         from_x, from_y = swap(w_in, size, 2), swap(w_in, size, 4)
         near = swap(w_in, size, 1)
-        corner0 = swap(from_x[:half], size, 4)
-        corner1 = swap(from_y[half:], size, 2)
-        near_x, near_y = swap(from_x, size, 1), swap(from_y, size, 1)
-        near0, near1 = swap(corner0, size, 1), swap(corner1, size, 1)
-        pieces = [(0, 0, w_in), (1, 0, near), (2, 0, from_x), (4, 0, from_y), (3, 0, near_x), (5, 0, near_y)]
-        pieces += [(6, 0, corner0), (6, half, corner1), (7, 0, near0), (7, half, near1)]
+        corner = jnp.concatenate([swap(from_x[:half], size, 4), swap(from_y[half:], size, 2)])
+        near_x, near_y, near_corner = swap(from_x, size, 1), swap(from_y, size, 1), swap(corner, size, 1)
+        pieces = [(0, w_in), (1, near), (2, from_x), (4, from_y), (3, near_x), (5, near_y)]
+        pieces += [(6, corner), (7, near_corner)]
         ordered = jnp.concatenate(
             [
                 lax.dynamic_slice_in_dim(tokens, (me ^ bit) * part, part, axis=1)
@@ -232,13 +230,13 @@
         )
         to_near, to_keep = ordered[:, : 4 * part], ordered[:, 4 * part :]
         total = 0.0
-        for bit, first, piece in pieces:
-            at = (bit // 2 + (0 if bit % 2 else 4)) * part + first
-            total = total + mm(ordered[:, at : at + piece.shape[0]], piece)
+        for bit, piece in pieces:
+            at = (bit // 2 + (0 if bit % 2 else 4)) * part
+            total = total + mm(ordered[:, at : at + part], piece)
         projected = total.astype(BF16)
         gathered = jnp.zeros((size, part, columns), BF16)
-        for bit, first, piece in pieces:
-            gathered = lax.dynamic_update_slice(gathered, piece[None], (me ^ bit, first, 0))
+        for bit, piece in pieces:
+            gathered = lax.dynamic_update_slice(gathered, piece[None], (me ^ bit, 0, 0))
     else:
         gathered = lax.all_gather(w_in, "seq", axis=0, tiled=True)
         projected = mm(tokens, gathered).astype(BF16)

time: 151 us -> 147 us (0.974)
  matrix products: 21.3 us -> 17 us
  waiting for transfers between devices: 62.7 us -> 65.4 us
  local copies, waits for them, and re-layouts: 8.88 us -> 6.76 us
    dot_general x16 -> x14, matrix products: 20.2 us -> 15.9 us  [mm(): return lax.dot_general(a, b, dims, preferred_element_type=F32)]
    ppermute x20 -> x19, waiting for transfers between devices: 24.3 us -> 27 us  [swap(): return lax.ppermute(value, 'seq', [(i, i ^ bit) for i in range(size)])]
    unnamed x57 -> x18, local copies, waits for them, and re-layouts: 3.43 us -> 2.38 us
    ppermute x20 -> x19, starting transfers between devices: 18.9 us -> 18.7 us  [swap(): return lax.ppermute(value, 'seq', [(i, i ^ bit) for i in range(size)])]
  transfers between devices with their start and end apart: 26 -> 25, of which waited for: 13 -> 15; matrix products, arithmetic and copies ran while one was open for 20% -> 18% of each run, Pallas kernels for 3% -> 3%
where the time goes in v3:
time: 147 us; the launch traced here: 146 us
  waiting for transfers between devices  65.4 us (44%)
  starting transfers between devices  35.4 us (24%)
  matrix products  17 us (12%)
  other arithmetic  13.5 us (9%)
  Pallas kernels  7.07 us (5%)
  local copies, waits for them, and re-layouts  6.76 us (5%)
    ppermute x6, waiting for transfers between devices, send(): return lax.ppermute(value.astype(BF16), 'fsdp', pairs)  38.4 us
    ppermute x19, waiting for transfers between devices, swap(): return lax.ppermute(value, 'seq', [(i, i ^ bit) for i in range(size)])  27 us
    ppermute x19, starting transfers between devices, swap(): return lax.ppermute(value, 'seq', [(i, i ^ bit) for i in range(size)])  18.7 us
    ppermute x6, starting transfers between devices, send(): return lax.ppermute(value.astype(BF16), 'fsdp', pairs)  16.7 us
    dot_general x14, matrix products, mm(): return lax.dot_general(a, b, dims, preferred_element_type=F32)  15.9 us
    pallas_call x5, Pallas kernels, call(): pl.pallas_call(kernel, out_shape=outs, in_specs=[pl.BlockSpec(memory_spac...  7.07 us
    convert_element_type x3, other arithmetic, send(): return lax.ppermute(value.astype(BF16), 'fsdp', pairs)  4.18 us
    convert_element_type x1, other arithmetic, reduce_on_line(): (own + near_in.astype(F32) + middle_across.astype(F32) + far_out.astype(F...  3.38 us
  transfers between devices with their start and end apart: 25, of which 15 were waited for; matrix products, arithmetic and copies ran while one was open for 18% of the time, Pallas kernels for 3%

profile of v3, /device:TPU:0, one launch (start us, length us, event | category | flops | bytes accessed | tf_op | source)
XLA Modules:
  0.0 146.2 jit_solution(9592532556721975828)
XLA Ops:
  1.1 2.6 %collective-permute-start.1 = (bf16[512,768]{1,0:T(8,128)(2,1)}, bf16[512,768]{1,0:T(8,128)(2,1)S(1)}, u32[]{:S(2)}, u32[]{:S(2)}) collective-permute-start(bf16[512,768]{1,0:T(8,128)(2,1)} %param.6), channel_id=1, source_target_pairs={{0,8},{4,12},{8,0},{12,4},{16,24},{20,28},{24,16},{28,20},{1,9},{5... | collective-permute-start | bytes 2359304 | tf_op jit(solution)/shard_map/ppermute | solution.py:168
  6.7 1.6 %copy.37 = f32[512,4]{1,0:T(8,128)} copy(f32[512,4]{0,1:T(4,128)} %param.7) | data formatting | bytes 16384 | tf_op args[2]
  10.7 2.5 %constant_dynamic-slice_fusion.6 = (bf16[512,512]{1,0:T(8,128)(2,1)S(1)}, bf16[512,512]{1,0:T(8,128)(2,1)S(1)}, bf16[512,512]{1,0:T(8,128)(2,1)S(1)}, bf16[512,5...) fusion(bf16[512,4096]{1,0:T(8,128)(2,1)} %param.5, ...), kind=kLoop, calls=%fused_computation.74 | loop fusion | bytes 8388640 | tf_op jit(solution)/shard_map/dynamic_slice | solution.py:226
  14.3 7.7 %collective-permute-done.1 = bf16[512,768]{1,0:T(8,128)(2,1)S(1)} collective-permute-done((bf16[512,768]{1,0:T(8,128)(2,1)}, bf16[512,768]{1,0:T(8,128)(2,1)S(1)}, u32[]{:S(2)}, u32[]{:S(2)}) %collective-permute-start.1) | collective-permute-done | bytes 786464 | tf_op jit(solution)/shard_map/ppermute | solution.py:168
  22.1 1.9 %collective-permute-start.5 = (bf16[256,768]{1,0:T(8,128)(2,1)S(1)}, bf16[256,768]{1,0:T(8,128)(2,1)S(1)}, u32[]{:S(2)}, u32[]{:S(2)}) collective-permute-start(bf16[256,768]{1,0:T(8,128)(2,1)S(1)} %slice.64), channel_id=1, source_target_pairs={{0,16},{4,20},{8,24},{12,28},{16,0},{20,4},{24,8},{28,12},{1,17},{... | collective-permute-start | bytes 1179656 | tf_op jit(solution)/shard_map/ppermute | solution.py:168
  28.0 5.0 %collective-permute-done.5 = bf16[256,768]{1,0:T(8,128)(2,1)S(1)} collective-permute-done((bf16[256,768]{1,0:T(8,128)(2,1)S(1)}, bf16[256,768]{1,0:T(8,128)(2,1)S(1)}, u32[]{:S(2)}, u32[]{:S(2)}) %collective-permute-start.5) | collective-permute-done | bytes 393248 | tf_op jit(solution)/shard_map/ppermute | solution.py:168
  42.9 1.9 %collective-permute-start.11 = (bf16[144,512]{1,0:T(8,128)(2,1)S(1)}, bf16[144,512]{1,0:T(8,128)(2,1)S(1)}, u32[]{:S(2)}, u32[]{:S(2)}) collective-permute-start(bf16[144,512]{1,0:T(8,128)(2,1)S(1)} %get-tuple-element.31), channel_id=1, source_target_pairs={{0,24},{4,28},{8,16},{12,20},{16,8},{20,12},{24,0},{28,4},{1,25},{... | collective-permute-start | bytes 442376 | tf_op jit(solution)/shard_map/ppermute | solution.py:168
  45.4 2.6 %shard_map.76 = (f32[512,512]{1,0:T(8,128)S(1)}, f32[512,512]{1,0:T(8,128)S(1)}, f32[512,128]{1,0:T(8,128)S(1)}, f32[512,128]{1,0:T(8,128)S(1)}, bf16[512,512]{1...) custom-call(bf16[512,768]{1,0:T(8,128)(2,1)S(1)} %add_convert_fusion.5.proj, bf16[512,512]{1,0:T(8,128)(2,1)S(1)} %copy-done, ...), custom_call_target="tpu_custom_call" | custom-call | flops 671088640 | bytes 5021696 | tf_op jit(solution)/shard_map/pallas_call | solution.py:31
  48.0 2.9 %collective-permute-done.10.rest_3_ = bf16[144,512]{1,0:T(8,128)(2,1)S(1)} collective-permute-done((bf16[144,512]{1,0:T(8,128)(2,1)S(1)}, bf16[144,512]{1,0:T(8,128)(2,1)S(1)}, u32[]{:S(2)}, u32[]{:S(2)}) %collective-permute-start.10) | collective-permute-done | bytes 147488 | tf_op jit(solution)/shard_map/ppermute | solution.py:168
  55.6 2.1 %fusion.26 = bf16[1024,512]{1,0:T(8,128)(2,1)} fusion(bf16[768,512]{1,0:T(8,128)(2,1)S(1)} %get-tuple-element.35, bf16[4,1024,768]{2,1,0:T(8,128)(2,1)S(1)} %bitcast.67, s32[]{:T(128)S(6)} %select_n.104), kind=kOutput, calls=%fused_computation.34 | convolution fusion | flops 805830656 | bytes 3407876 | tf_op jit(solution)/shard_map/dot_general | solution.py:25
  57.7 1.9 %convolution_convert_fusion = bf16[2048,768]{1,0:T(8,128)(2,1)S(1)} fusion(bf16[512,768]{1,0:T(8,128)(2,1)S(1)} %get-tuple-element.38, bf16[512,512]{1,0:T(8,128)(2,1)S(1)} %get-tuple-element.51, bf16[512,512]{1,0:T(8,128)(2,1)S(1)} %get-tuple-element.46, bf16[512,512]{1,0:T(8,128)(2,1)S(1)} %get-tuple-element.47, bf16[512,512]{1,0:T(8,128)(2,1)S(1)} %get-tuple-element.45), kind=kOutput, calls=%fused_computation.1 | convolution fusion | flops 1620574208 | bytes 6029312 | tf_op jit(solution)/shard_map/dot_general | solution.py:25
  59.7 3.5 %collective-permute-start.18 = (bf16[1024,512]{1,0:T(8,128)(2,1)S(1)}, bf16[1024,512]{1,0:T(8,128)(2,1)S(1)}, u32[]{:S(2)}, u32[]{:S(2)}) collective-permute-start(bf16[1024,512]{1,0:T(8,128)(2,1)S(1)} %fusion.32), channel_id=1, source_target_pairs={{0,1},{3,2},{4,5},{7,6},{8,9},{11,10},{12,13},{15,14},{16,17},{19,... | collective-permute-start | bytes 3145736 | tf_op jit(solution)/shard_map/ppermute | solution.py:183
  65.3 2.5 %add_convert_fusion = bf16[2048,768]{1,0:T(8,128)(2,1)S(1)} fusion(bf16[2048,768]{1,0:T(8,128)(2,1)S(1)} %collective-permute-done.14, bf16[512,768]{1,0:T(8,128)(2,1)S(1)} %get-tuple-element.38, bf16[512,512]{1,0:T(8,128)(2,1)S(1)} %get-tuple-element.52, bf16[512,512]{1,0:T(8,128)(2,1)S(1)} %get-tuple-element.48, bf16[512,512]{1,0:T(8,128)(2,1)S(1)} %get-tuple-element.49, ...), kind=kOutput, calls=%fused_computation | convolution fusion | flops 1623719936 | bytes 9175040 | tf_op jit(solution)/shard_map/dot_general | solution.py:25
  67.8 18.8 %collective-permute-done.18 = bf16[1024,512]{1,0:T(8,128)(2,1)S(1)} collective-permute-done((bf16[1024,512]{1,0:T(8,128)(2,1)S(1)}, bf16[1024,512]{1,0:T(8,128)(2,1)S(1)}, u32[]{:S(2)}, u32[]{:S(2)}) %collective-permute-start.18) | collective-permute-done | bytes 1048608 | tf_op jit(solution)/shard_map/ppermute | solution.py:183
  89.9 8.1 %collective-permute-start.12 = (bf16[1024,512]{1,0:T(8,128)(2,1)}, bf16[1024,512]{1,0:T(8,128)(2,1)}, u32[]{:S(2)}, u32[]{:S(2)}) collective-permute-start(bf16[1024,512]{1,0:T(8,128)(2,1)} %fusion.26), channel_id=1, source_target_pairs={{0,1},{3,2},{4,5},{7,6},{8,9},{11,10},{12,13},{15,14},{16,17},{19,... | collective-permute-start | bytes 3145736 | tf_op jit(solution)/shard_map/ppermute | solution.py:183
  101.3 7.8 %collective-permute-done.13 = bf16[1024,512]{1,0:T(8,128)(2,1)S(1)} collective-permute-done((bf16[1024,512]{1,0:T(8,128)(2,1)S(1)}, bf16[1024,512]{1,0:T(8,128)(2,1)S(1)}, u32[]{:S(2)}, u32[]{:S(2)}) %collective-permute-start.13) | collective-permute-done | bytes 1048608 | tf_op jit(solution)/shard_map/ppermute | solution.py:183
  110.4 1.6 %collective-permute-start.17 = (bf16[1024,512]{1,0:T(8,128)(2,1)}, bf16[1024,512]{1,0:T(8,128)(2,1)}, u32[]{:S(2)}, u32[]{:S(2)}) collective-permute-start(bf16[1024,512]{1,0:T(8,128)(2,1)} %add_convert_fusion.4), channel_id=1, source_target_pairs={{1,2},{2,1},{5,6},{6,5},{9,10},{10,9},{13,14},{14,13},{17,18},{18,... | collective-permute-start | bytes 3145736 | tf_op jit(solution)/shard_map/ppermute | solution.py:183
  112.0 2.6 %add_convert_fusion.2 = bf16[1024,512]{1,0:T(8,128)(2,1)} fusion(bf16[1024,512]{1,0:T(8,128)(2,1)S(1)} %collective-permute-done.19, bf16[1024,512]{1,0:T(8,128)(2,1)} %fusion.26), kind=kLoop, calls=%fused_computation.17 | loop fusion | flops 2097152 | bytes 3145728 | tf_op jit(solution)/shard_map/convert_element_type | solution.py:183
  120.3 2.4 %fusion.20 = f32[1024,512]{1,0:T(8,128)S(1)} fusion(bf16[768,512]{1,0:T(8,128)(2,1)S(1)} %get-tuple-element.35, bf16[4,1024,768]{2,1,0:T(8,128)(2,1)} %bitcast.68, s32[]{:T(128)S(6)} %select_n.103), kind=kOutput, calls=%fused_computation.27 | convolution fusion | flops 805306368 | bytes 4456452 | tf_op jit(solution)/shard_map/dot_general | solution.py:25
  122.7 3.9 %collective-permute-done.22 = bf16[256,768]{1,0:T(8,128)(2,1)} collective-permute-done((bf16[256,768]{1,0:T(8,128)(2,1)}, bf16[256,768]{1,0:T(8,128)(2,1)}, u32[]{:S(2)}, u32[]{:S(2)}) %collective-permute-start.22) | collective-permute-done | bytes 393248 | tf_op jit(solution)/shard_map/ppermute | solution.py:168
  126.6 1.6 %collective-permute-done.24 = bf16[256,768]{1,0:T(8,128)(2,1)} collective-permute-done((bf16[256,768]{1,0:T(8,128)(2,1)}, bf16[256,768]{1,0:T(8,128)(2,1)}, u32[]{:S(2)}, u32[]{:S(2)}) %collective-permute-start.24) | collective-permute-done | bytes 393248 | tf_op jit(solution)/shard_map/ppermute | solution.py:168
  128.2 1.6 %convert_add_fusion.1 = (f32[256,768]{1,0:T(8,128)S(1)}, f32[256,768]{1,0:T(8,128)S(1)}) fusion(bf16[256,768]{1,0:T(8,128)(2,1)} %collective-permute-done.22, bf16[256,768]{1,0:T(8,128)(2,1)S(1)} %copy-done.5, bf16[2048,768]{1,0:T(8,128)(2,1)} %copy-done.3, bf16[256,768]{1,0:T(8,128)(2,1)} %collective-permute-done.24, bf16[256,768]{1,0:T(8,128)(2,1)S(1)} %copy-done.7), kind=kLoop, calls=%fused_computation.48 | loop fusion | flops 1966080 | bytes 3932160 | tf_op jit(solution)/shard_map/add | solution.py:344
  131.3 11.6 %collective-permute-done.20 = bf16[1024,512]{1,0:T(8,128)(2,1)} collective-permute-done((bf16[1024,512]{1,0:T(8,128)(2,1)}, bf16[1024,512]{1,0:T(8,128)(2,1)}, u32[]{:S(2)}, u32[]{:S(2)}) %collective-permute-start.20) | collective-permute-done | bytes 1048608 | tf_op jit(solution)/shard_map/ppermute | solution.py:183
  142.9 3.4 %add_convert_fusion.1 = bf16[1024,512]{1,0:T(8,128)(2,1)} fusion(bf16[1024,512]{1,0:T(8,128)(2,1)} %collective-permute-done.20, bf16[1024,512]{1,0:T(8,128)(2,1)} %collective-permute-done.17, f32[1024,512]{1,0:T(8,128)S(1)} %fusion.20, bf16[1024,512]{1,0:T(8,128)(2,1)} %collective-permute-done.12), kind=kLoop, calls=%fused_computation.16 | loop fusion | flops 3670016 | bytes 6291456 | tf_op jit(solution)/shard_map/convert_element_type | solution.py:198
  (93 shorter events, 43.1 us)
Async XLA Ops:
  0.6 26.6 %collective-permute-start = (bf16[512,768]{1,0:T(8,128)(2,1)}, bf16[512,768]{1,0:T(8,128)(2,1)S(1)}, u32[]{:S(2)}, u32[]{:S(2)}) collective-permute-start(bf16[512,768]{1,0:T(8,128)(2,1)} %param.6), channel_id=1, source_target_pairs={{0,4},{4,0},{8,12},{12,8},{16,20},{20,16},{24,28},{28,24},{1,5},{5... | collective-permute-start | bytes 2359304 | tf_op jit(solution)/shard_map/ppermute | solution.py:168
  1.1 20.9 %collective-permute-start.1 = (bf16[512,768]{1,0:T(8,128)(2,1)}, bf16[512,768]{1,0:T(8,128)(2,1)S(1)}, u32[]{:S(2)}, u32[]{:S(2)}) collective-permute-start(bf16[512,768]{1,0:T(8,128)(2,1)} %param.6), channel_id=1, source_target_pairs={{0,8},{4,12},{8,0},{12,4},{16,24},{20,28},{24,16},{28,20},{1,9},{5... | collective-permute-start | bytes 2359304 | tf_op jit(solution)/shard_map/ppermute | solution.py:168
  3.7 20.2 %collective-permute-start.2 = (bf16[512,768]{1,0:T(8,128)(2,1)}, bf16[512,768]{1,0:T(8,128)(2,1)S(1)}, u32[]{:S(2)}, u32[]{:S(2)}) collective-permute-start(bf16[512,768]{1,0:T(8,128)(2,1)} %param.6), channel_id=1, source_target_pairs={{0,16},{4,20},{8,24},{12,28},{16,0},{20,4},{24,8},{28,12},{1,17},{... | collective-permute-start | bytes 2359304 | tf_op jit(solution)/shard_map/ppermute | solution.py:168
  22.1 10.9 %collective-permute-start.5 = (bf16[256,768]{1,0:T(8,128)(2,1)S(1)}, bf16[256,768]{1,0:T(8,128)(2,1)S(1)}, u32[]{:S(2)}, u32[]{:S(2)}) collective-permute-start(bf16[256,768]{1,0:T(8,128)(2,1)S(1)} %slice.64), channel_id=1, source_target_pairs={{0,16},{4,20},{8,24},{12,28},{16,0},{20,4},{24,8},{28,12},{1,17},{... | collective-permute-start | bytes 1179656 | tf_op jit(solution)/shard_map/ppermute | solution.py:168
  24.0 10.5 %collective-permute-start.6 = (bf16[256,768]{1,0:T(8,128)(2,1)S(1)}, bf16[256,768]{1,0:T(8,128)(2,1)S(1)}, u32[]{:S(2)}, u32[]{:S(2)}) collective-permute-start(bf16[256,768]{1,0:T(8,128)(2,1)S(1)} %slice.65), channel_id=1, source_target_pairs={{0,8},{4,12},{8,0},{12,4},{16,24},{20,28},{24,16},{28,20},{1,9},{5... | collective-permute-start | bytes 1179656 | tf_op jit(solution)/shard_map/ppermute | solution.py:168
  25.5 9.6 %collective-permute-start.3 = (bf16[512,768]{1,0:T(8,128)(2,1)S(1)}, bf16[512,768]{1,0:T(8,128)(2,1)S(1)}, u32[]{:S(2)}, u32[]{:S(2)}) collective-permute-start(bf16[512,768]{1,0:T(8,128)(2,1)S(1)} %collective-permute-done.1), channel_id=1, source_target_pairs={{0,4},{4,0},{8,12},{12,8},{16,20},{20,16},{24,28},{28,24},{1,5},{5... | collective-permute-start | bytes 2359304 | tf_op jit(solution)/shard_map/ppermute | solution.py:168
  25.5 11.9 %collective-permute-start.4 = (bf16[512,768]{1,0:T(8,128)(2,1)S(1)}, bf16[512,768]{1,0:T(8,128)(2,1)S(1)}, u32[]{:S(2)}, u32[]{:S(2)}) collective-permute-start(bf16[512,768]{1,0:T(8,128)(2,1)S(1)} %collective-permute-done.2), channel_id=1, source_target_pairs={{0,4},{4,0},{8,12},{12,8},{16,20},{20,16},{24,28},{28,24},{1,5},{5... | collective-permute-start | bytes 2359304 | tf_op jit(solution)/shard_map/ppermute | solution.py:168
  34.5 2.4 %collective-permute-start.7 = (bf16[512,768]{1,0:T(8,128)(2,1)S(1)}, bf16[512,768]{1,0:T(8,128)(2,1)S(1)}, u32[]{:S(2)}, u32[]{:S(2)}) collective-permute-start(bf16[512,768]{1,0:T(8,128)(2,1)S(1)} %constant_dynamic-update-slice_fusion), channel_id=1, source_target_pairs={{0,4},{4,0},{8,12},{12,8},{16,20},{20,16},{24,28},{28,24},{1,5},{5... | collective-permute-start | bytes 2359304 | tf_op jit(solution)/shard_map/ppermute | solution.py:168
  41.8 9.1 %collective-permute-start.10 = (bf16[144,512]{1,0:T(8,128)(2,1)S(1)}, bf16[144,512]{1,0:T(8,128)(2,1)S(1)}, u32[]{:S(2)}, u32[]{:S(2)}) collective-permute-start(bf16[144,512]{1,0:T(8,128)(2,1)S(1)} %get-tuple-element.31), channel_id=1, source_target_pairs={{0,16},{4,20},{8,24},{12,28},{16,0},{20,4},{24,8},{28,12},{1,17},{... | collective-permute-start | bytes 442376 | tf_op jit(solution)/shard_map/ppermute | solution.py:168
  42.9 8.0 %collective-permute-start.11 = (bf16[144,512]{1,0:T(8,128)(2,1)S(1)}, bf16[144,512]{1,0:T(8,128)(2,1)S(1)}, u32[]{:S(2)}, u32[]{:S(2)}) collective-permute-start(bf16[144,512]{1,0:T(8,128)(2,1)S(1)} %get-tuple-element.31), channel_id=1, source_target_pairs={{0,24},{4,28},{8,16},{12,20},{16,8},{20,12},{24,0},{28,4},{1,25},{... | collective-permute-start | bytes 442376 | tf_op jit(solution)/shard_map/ppermute | solution.py:168
  44.8 7.3 %collective-permute-start.9 = (bf16[144,512]{1,0:T(8,128)(2,1)S(1)}, bf16[144,512]{1,0:T(8,128)(2,1)S(1)}, u32[]{:S(2)}, u32[]{:S(2)}) collective-permute-start(bf16[144,512]{1,0:T(8,128)(2,1)S(1)} %get-tuple-element.30), channel_id=1, source_target_pairs={{0,8},{4,12},{8,0},{12,4},{16,24},{20,28},{24,16},{28,20},{1,9},{5... | collective-permute-start | bytes 442376 | tf_op jit(solution)/shard_map/ppermute | solution.py:168
  59.6 5.7 %collective-permute-start.14 = (bf16[2048,768]{1,0:T(8,128)(2,1)S(1)}, bf16[2048,768]{1,0:T(8,128)(2,1)S(1)}, u32[]{:S(2)}, u32[]{:S(2)}) collective-permute-start(bf16[2048,768]{1,0:T(8,128)(2,1)S(1)} %convolution_convert_fusion), channel_id=1, source_target_pairs={{0,4},{4,0},{8,12},{12,8},{16,20},{20,16},{24,28},{28,24},{1,5},{5... | collective-permute-start | bytes 9437192 | tf_op jit(solution)/shard_map/ppermute | solution.py:168
  59.7 26.9 %collective-permute-start.18 = (bf16[1024,512]{1,0:T(8,128)(2,1)S(1)}, bf16[1024,512]{1,0:T(8,128)(2,1)S(1)}, u32[]{:S(2)}, u32[]{:S(2)}) collective-permute-start(bf16[1024,512]{1,0:T(8,128)(2,1)S(1)} %fusion.32), channel_id=1, source_target_pairs={{0,1},{3,2},{4,5},{7,6},{8,9},{11,10},{12,13},{15,14},{16,17},{19,... | collective-permute-start | bytes 3145736 | tf_op jit(solution)/shard_map/ppermute | solution.py:183
  63.2 45.9 %collective-permute-start.13 = (bf16[1024,512]{1,0:T(8,128)(2,1)S(1)}, bf16[1024,512]{1,0:T(8,128)(2,1)S(1)}, u32[]{:S(2)}, u32[]{:S(2)}) collective-permute-start(bf16[1024,512]{1,0:T(8,128)(2,1)S(1)} %fusion.29), channel_id=1, source_target_pairs={{0,1},{3,2},{4,5},{7,6},{8,9},{11,10},{12,13},{15,14},{16,17},{19,... | collective-permute-start | bytes 3145736 | tf_op jit(solution)/shard_map/ppermute | solution.py:183
  87.0 25.1 %collective-permute-start.19 = (bf16[1024,512]{1,0:T(8,128)(2,1)S(1)}, bf16[1024,512]{1,0:T(8,128)(2,1)S(1)}, u32[]{:S(2)}, u32[]{:S(2)}) collective-permute-start(bf16[1024,512]{1,0:T(8,128)(2,1)S(1)} %add_convert_fusion.3), channel_id=1, source_target_pairs={{1,2},{2,1},{5,6},{6,5},{9,10},{10,9},{13,14},{14,13},{17,18},{18,... | collective-permute-start | bytes 3145736 | tf_op jit(solution)/shard_map/ppermute | solution.py:183
  87.8 10.4 %collective-permute-start.15 = (bf16[256,768]{1,0:T(8,128)(2,1)S(1)}, bf16[256,768]{1,0:T(8,128)(2,1)S(1)}, u32[]{:S(2)}, u32[]{:S(2)}) collective-permute-start(bf16[256,768]{1,0:T(8,128)(2,1)S(1)} %get-tuple-element.58), channel_id=1, source_target_pairs={{0,16},{4,20},{8,24},{12,28},{16,0},{20,4},{24,8},{28,12},{1,17},{... | collective-permute-start | bytes 1179656 | tf_op jit(solution)/shard_map/ppermute | solution.py:168
  88.9 10.7 %collective-permute-start.16 = (bf16[256,768]{1,0:T(8,128)(2,1)S(1)}, bf16[256,768]{1,0:T(8,128)(2,1)S(1)}, u32[]{:S(2)}, u32[]{:S(2)}) collective-permute-start(bf16[256,768]{1,0:T(8,128)(2,1)S(1)} %get-tuple-element.57), channel_id=1, source_target_pairs={{0,8},{4,12},{8,0},{12,4},{16,24},{20,28},{24,16},{28,20},{1,9},{5... | collective-permute-start | bytes 1179656 | tf_op jit(solution)/shard_map/ppermute | solution.py:168
  89.9 41.4 %collective-permute-start.12 = (bf16[1024,512]{1,0:T(8,128)(2,1)}, bf16[1024,512]{1,0:T(8,128)(2,1)}, u32[]{:S(2)}, u32[]{:S(2)}) collective-permute-start(bf16[1024,512]{1,0:T(8,128)(2,1)} %fusion.26), channel_id=1, source_target_pairs={{0,1},{3,2},{4,5},{7,6},{8,9},{11,10},{12,13},{15,14},{16,17},{19,... | collective-permute-start | bytes 3145736 | tf_op jit(solution)/shard_map/ppermute | solution.py:183
  98.2 17.7 %collective-permute-start.21 = (bf16[256,768]{1,0:T(8,128)(2,1)S(1)}, bf16[256,768]{1,0:T(8,128)(2,1)S(1)}, u32[]{:S(2)}, u32[]{:S(2)}) collective-permute-start(bf16[256,768]{1,0:T(8,128)(2,1)S(1)} %get-tuple-element.55), channel_id=1, source_target_pairs={{0,8},{4,12},{8,0},{12,4},{16,24},{20,28},{24,16},{28,20},{1,9},{5... | collective-permute-start | bytes 1179656 | tf_op jit(solution)/shard_map/ppermute | solution.py:168
  99.7 17.4 %collective-permute-start.23 = (bf16[256,768]{1,0:T(8,128)(2,1)S(1)}, bf16[256,768]{1,0:T(8,128)(2,1)S(1)}, u32[]{:S(2)}, u32[]{:S(2)}) collective-permute-start(bf16[256,768]{1,0:T(8,128)(2,1)S(1)} %get-tuple-element.56), channel_id=1, source_target_pairs={{0,16},{4,20},{8,24},{12,28},{16,0},{20,4},{24,8},{28,12},{1,17},{... | collective-permute-start | bytes 1179656 | tf_op jit(solution)/shard_map/ppermute | solution.py:168
  110.4 20.9 %collective-permute-start.17 = (bf16[1024,512]{1,0:T(8,128)(2,1)}, bf16[1024,512]{1,0:T(8,128)(2,1)}, u32[]{:S(2)}, u32[]{:S(2)}) collective-permute-start(bf16[1024,512]{1,0:T(8,128)(2,1)} %add_convert_fusion.4), channel_id=1, source_target_pairs={{1,2},{2,1},{5,6},{6,5},{9,10},{10,9},{13,14},{14,13},{17,18},{18,... | collective-permute-start | bytes 3145736 | tf_op jit(solution)/shard_map/ppermute | solution.py:183
  114.6 28.3 %collective-permute-start.20 = (bf16[1024,512]{1,0:T(8,128)(2,1)}, bf16[1024,512]{1,0:T(8,128)(2,1)}, u32[]{:S(2)}, u32[]{:S(2)}) collective-permute-start(bf16[1024,512]{1,0:T(8,128)(2,1)} %add_convert_fusion.2), channel_id=1, source_target_pairs={{1,0},{2,3},{5,4},{6,7},{9,8},{10,11},{13,12},{14,15},{17,16},{18,... | collective-permute-start | bytes 3145736 | tf_op jit(solution)/shard_map/ppermute | solution.py:183
  115.9 10.7 %collective-permute-start.22 = (bf16[256,768]{1,0:T(8,128)(2,1)}, bf16[256,768]{1,0:T(8,128)(2,1)}, u32[]{:S(2)}, u32[]{:S(2)}) collective-permute-start(bf16[256,768]{1,0:T(8,128)(2,1)} %get-tuple-element.59), channel_id=1, source_target_pairs={{0,16},{4,20},{8,24},{12,28},{16,0},{20,4},{24,8},{28,12},{1,17},{... | collective-permute-start | bytes 1179656 | tf_op jit(solution)/shard_map/ppermute | solution.py:168
  117.8 10.4 %collective-permute-start.24 = (bf16[256,768]{1,0:T(8,128)(2,1)}, bf16[256,768]{1,0:T(8,128)(2,1)}, u32[]{:S(2)}, u32[]{:S(2)}) collective-permute-start(bf16[256,768]{1,0:T(8,128)(2,1)} %get-tuple-element.60), channel_id=1, source_target_pairs={{0,8},{4,12},{8,0},{12,4},{16,24},{20,28},{24,16},{28,20},{1,9},{5... | collective-permute-start | bytes 1179656 | tf_op jit(solution)/shard_map/ppermute | solution.py:168
  (9 other events, 65.5 us)

commit v4 on v3

--- a/solution.py
+++ b/solution.py
@@ -34,7 +34,7 @@
         in_specs=[pl.BlockSpec(memory_space=pltpu.SMEM)] * len(scalars)
         + [pl.BlockSpec(memory_space=pltpu.VMEM)] * len(args),
         out_specs=[pl.BlockSpec(memory_space=pltpu.VMEM)] * len(outs),
-        compiler_params=pltpu.CompilerParams(vmem_limit_bytes=40 * 2**20),
+        compiler_params=pltpu.CompilerParams(vmem_limit_bytes=14 * 2**20),
         cost_estimate=pl.CostEstimate(flops=flops, bytes_accessed=moved, transcendentals=0),
     )(*scalars, *args)
 
@@ -229,6 +229,7 @@
             axis=1,
         )
         to_near, to_keep = ordered[:, : 4 * part], ordered[:, 4 * part :]
+        chip_tokens = jnp.concatenate([to_keep, swap(to_near, size, 1)])
         total = 0.0
         for bit, piece in pieces:
             at = (bit // 2 + (0 if bit % 2 else 4)) * part
@@ -299,12 +300,11 @@
     groups, group = lax.axis_size("fsdp"), lax.axis_index("fsdp")
     kept, sent, out = [], [], []
 
-    def near_products(last):
-        products = mm(to_near, once(proj_grad, *last), TN).astype(BF16)
-        kept.append(swap(products, size, 1))
+    def near_gradient(last):
+        kept.append(swap(proj_grad, size, 1))
 
     def kept_products():
-        kept[0] = (mm(to_keep, proj_grad, TN) + kept[0].astype(F32)).astype(BF16)
+        kept[0] = mm(chip_tokens, jnp.concatenate([proj_grad, kept[0]]), TN).astype(BF16)
         own, for_x, for_y, for_corner = kept[0].reshape(4, part, columns)
         sent.extend((own, for_x, for_y, swap(for_corner[:half], size, 2), swap(for_corner[half:], size, 4)))
         sent.extend((swap(for_x[:half], size, 2), swap(for_y[half:], size, 4)))
@@ -329,7 +329,7 @@
         return tuple(out)
 
     if square and groups == 4:
-        input_grad = reduce_on_line(gathered, turned, group, (near_products, kept_products, corner_sums, outputs))
+        input_grad = reduce_on_line(gathered, turned, group, (near_gradient, kept_products, corner_sums, outputs))
     else:
         input_grad = lax.psum_scatter(
             mm(gathered.reshape(part * size, columns), turned).astype(BF16), "fsdp", scatter_dimension=0, tiled=True

time: 147 us -> 146 us (level)
  waiting for transfers between devices: 65.4 us -> 45.1 us
  matrix products: 17 us -> 23.7 us
  other arithmetic: 13.5 us -> 19.3 us
  local copies, waits for them, and re-layouts: 6.76 us -> 12.2 us
    ppermute x6, waiting for transfers between devices: 38.4 us -> 25.1 us  [send(): return lax.ppermute(value.astype(BF16), 'fsdp', pairs)]
    dot_general x14 -> x13, matrix products: 15.9 us -> 23.3 us  [mm(): return lax.dot_general(a, b, dims, preferred_element_type=F32)]
    ppermute x19 -> x20, waiting for transfers between devices: 27 us -> 20 us  [swap(): return lax.ppermute(value, 'seq', [(i, i ^ bit) for i in range(size)])]
    convert_element_type x3, other arithmetic: 4.18 us -> 6.87 us  [send(): return lax.ppermute(value.astype(BF16), 'fsdp', pairs)]
    concatenate x0 -> x1, other arithmetic: none -> 1.63 us  [shards(): jnp.concatenate([lax.dynamic_slice_in_dim(tokens, (me ^ bit) * part, part...]
    unnamed x18 -> x50, local copies, waits for them, and re-layouts: 2.38 us -> 3.35 us
    ppermute x19 -> x20, starting transfers between devices: 18.7 us -> 18.6 us  [swap(): return lax.ppermute(value, 'seq', [(i, i ^ bit) for i in range(size)])]
  transfers between devices with their start and end apart: 25 -> 26, of which waited for: 15 -> 12; matrix products, arithmetic and copies ran while one was open for 18% -> 34% of each run, Pallas kernels for 3% -> 5%
where the time goes in v4:
time: 146 us
  waiting for transfers between devices  45.1 us (31%)
  starting transfers between devices  36.6 us (25%)
  matrix products  23.7 us (16%)
  other arithmetic  19.3 us (13%)
  local copies, waits for them, and re-layouts  12.2 us (8%)
  Pallas kernels  7.73 us (5%)
    ppermute x6, waiting for transfers between devices, send(): return lax.ppermute(value.astype(BF16), 'fsdp', pairs)  25.1 us
    dot_general x13, matrix products, mm(): return lax.dot_general(a, b, dims, preferred_element_type=F32)  23.3 us
    ppermute x20, waiting for transfers between devices, swap(): return lax.ppermute(value, 'seq', [(i, i ^ bit) for i in range(size)])  20 us
    ppermute x20, starting transfers between devices, swap(): return lax.ppermute(value, 'seq', [(i, i ^ bit) for i in range(size)])  18.6 us
    ppermute x6, starting transfers between devices, send(): return lax.ppermute(value.astype(BF16), 'fsdp', pairs)  18 us
    pallas_call x5, Pallas kernels, call(): pl.pallas_call(kernel, out_shape=outs, in_specs=[pl.BlockSpec(memory_spac...  7.73 us
    convert_element_type x3, other arithmetic, send(): return lax.ppermute(value.astype(BF16), 'fsdp', pairs)  6.87 us
    dynamic_slice x1, local copies, waits for them, and re-layouts, shards(): lax.dynamic_slice_in_dim(tokens, (me ^ bit) * part, part, axis=1)  3.8 us
  transfers between devices with their start and end apart: 26, of which 12 were waited for; matrix products, arithmetic and copies ran while one was open for 34% of the time, Pallas kernels for 5%

profile of v4, /device:TPU:0, one launch (start us, length us, event | category | flops | bytes accessed | tf_op | source)
XLA Modules:
  0.0 145.6 jit_solution(13493307475827021816)
XLA Ops:
  1.1 2.6 %collective-permute-start.1 = (bf16[512,768]{1,0:T(8,128)(2,1)}, bf16[512,768]{1,0:T(8,128)(2,1)S(1)}, u32[]{:S(2)}, u32[]{:S(2)}) collective-permute-start(bf16[512,768]{1,0:T(8,128)(2,1)} %param.6), channel_id=1, source_target_pairs={{0,8},{4,12},{8,0},{12,4},{16,24},{20,28},{24,16},{28,20},{1,9},{5... | collective-permute-start | bytes 2359304 | tf_op jit(solution)/shard_map/ppermute | solution.py:168
  5.2 3.8 %constant_dynamic-slice_fusion.6 = (bf16[512,512]{1,0:T(8,128)(2,1)S(1)}, bf16[512,512]{1,0:T(8,128)(2,1)S(1)}, bf16[512,512]{1,0:T(8,128)(2,1)S(1)}, bf16[512,5...) fusion(bf16[512,4096]{1,0:T(8,128)(2,1)} %param.5, ...), kind=kLoop, calls=%fused_computation.73 | loop fusion | bytes 8388640 | tf_op jit(solution)/shard_map/dynamic_slice | solution.py:226
  12.6 1.9 %fusion.38 = (f32[4,512]{0,1:T(8,128)}, f32[512,4]{1,0:T(8,128)S(1)}, f32[512,4]{1,0:T(8,128)S(1)}) fusion(pred[512,4]{1,0:T(8,128)(4,1)S(1)} %copy.36, f32[512,4]{1,0:T(8,128)} %copy.37, f32[512,4]{1,0:T(8,128)S(1)} %copy.32.cum, f32[4]{0:T(128)S(1)} %slice_reduce_fusion), kind=kLoop, calls=%fused_computation.52 | loop fusion | flops 14336 | bytes 43024 | tf_op jit(solution)/shard_map/transpose | solution.py:255
  17.5 4.6 %collective-permute-done.1 = bf16[512,768]{1,0:T(8,128)(2,1)S(1)} collective-permute-done((bf16[512,768]{1,0:T(8,128)(2,1)}, bf16[512,768]{1,0:T(8,128)(2,1)S(1)}, u32[]{:S(2)}, u32[]{:S(2)}) %collective-permute-start.1) | collective-permute-done | bytes 786464 | tf_op jit(solution)/shard_map/ppermute | solution.py:168
  30.7 2.3 %collective-permute-done.5 = bf16[256,768]{1,0:T(8,128)(2,1)S(1)} collective-permute-done((bf16[256,768]{1,0:T(8,128)(2,1)S(1)}, bf16[256,768]{1,0:T(8,128)(2,1)S(1)}, u32[]{:S(2)}, u32[]{:S(2)}) %collective-permute-start.5) | collective-permute-done | bytes 393248 | tf_op jit(solution)/shard_map/ppermute | solution.py:168
  42.9 1.9 %collective-permute-start.11 = (bf16[144,512]{1,0:T(8,128)(2,1)S(1)}, bf16[144,512]{1,0:T(8,128)(2,1)S(1)}, u32[]{:S(2)}, u32[]{:S(2)}) collective-permute-start(bf16[144,512]{1,0:T(8,128)(2,1)S(1)} %get-tuple-element.30), channel_id=1, source_target_pairs={{0,24},{4,28},{8,16},{12,20},{16,8},{20,12},{24,0},{28,4},{1,25},{... | collective-permute-start | bytes 442376 | tf_op jit(solution)/shard_map/ppermute | solution.py:168
  45.4 2.4 %shard_map.76 = (f32[512,512]{1,0:T(8,128)S(1)}, f32[512,512]{1,0:T(8,128)S(1)}, f32[512,128]{1,0:T(8,128)S(1)}, f32[512,128]{1,0:T(8,128)S(1)}, bf16[512,512]{1...) custom-call(bf16[512,768]{1,0:T(8,128)(2,1)S(1)} %add_convert_fusion.4.proj, bf16[512,512]{1,0:T(8,128)(2,1)S(1)} %copy-done, ...), custom_call_target="tpu_custom_call" | custom-call | flops 671088640 | bytes 5021696 | tf_op jit(solution)/shard_map/pallas_call | solution.py:31
  47.9 3.0 %collective-permute-done.10.rest_3_ = bf16[144,512]{1,0:T(8,128)(2,1)S(1)} collective-permute-done((bf16[144,512]{1,0:T(8,128)(2,1)S(1)}, bf16[144,512]{1,0:T(8,128)(2,1)S(1)}, u32[]{:S(2)}, u32[]{:S(2)}) %collective-permute-start.10) | collective-permute-done | bytes 147488 | tf_op jit(solution)/shard_map/ppermute | solution.py:168
  52.1 2.3 %shard_map.79 = (bf16[512,768]{1,0:T(8,128)(2,1)}, bf16[768,512]{1,0:T(8,128)(2,1)S(1)}, bf16[128,512]{1,0:T(8,128)(2,1)S(1)}) custom-call(s32[2]{0:T(128)S(1)} %pad_add_fusion.place, bf16[512,768]{1,0:T(8,128)(2,1)S(1)} %add_convert_fusion.4.proj, f32[512,4]{1,0:T(8,128)S(1)} %get-tuple-element.60.to_end, f32[512,512]{1,0:T(8,128)S(1)} %get-tuple-element.24.dx, ...), custom_call_target="tpu_custom_call" | custom-call | flops 201326592 | bytes 6119424 | tf_op jit(solution)/shard_map/pallas_call | solution.py:31
  54.5 2.4 %fusion.34 = bf16[1024,512]{1,0:T(8,128)(2,1)S(1)} fusion(bf16[768,512]{1,0:T(8,128)(2,1)S(1)} %get-tuple-element.34, bf16[4,1024,768]{2,1,0:T(8,128)(2,1)} %bitcast.63, s32[]{:T(128)S(6)} %select_n.106), kind=kOutput, calls=%fused_computation.35 | convolution fusion | flops 805830656 | bytes 3407876 | tf_op jit(solution)/shard_map/dot_general | solution.py:25
  56.9 3.9 %collective-permute-start.19 = (bf16[1024,512]{1,0:T(8,128)(2,1)S(1)}, bf16[1024,512]{1,0:T(8,128)(2,1)S(1)}, u32[]{:S(2)}, u32[]{:S(2)}) collective-permute-start(bf16[1024,512]{1,0:T(8,128)(2,1)S(1)} %fusion.34), channel_id=1, source_target_pairs={{0,1},{3,2},{4,5},{7,6},{8,9},{11,10},{12,13},{15,14},{16,17},{19,... | collective-permute-start | bytes 3145736 | tf_op jit(solution)/shard_map/ppermute | solution.py:183
  60.8 3.4 %fusion.31 = bf16[1024,512]{1,0:T(8,128)(2,1)} fusion(bf16[768,512]{1,0:T(8,128)(2,1)S(1)} %get-tuple-element.34, bf16[4,1024,768]{2,1,0:T(8,128)(2,1)} %bitcast.64, s32[]{:T(128)S(6)} %select_n.105), kind=kOutput, calls=%fused_computation.34 | convolution fusion | flops 805830656 | bytes 3407876 | tf_op jit(solution)/shard_map/dot_general | solution.py:25
  64.1 2.3 %collective-permute-start.13 = (bf16[1024,512]{1,0:T(8,128)(2,1)}, bf16[1024,512]{1,0:T(8,128)(2,1)}, u32[]{:S(2)}, u32[]{:S(2)}) collective-permute-start(bf16[1024,512]{1,0:T(8,128)(2,1)} %fusion.31), channel_id=1, source_target_pairs={{0,1},{3,2},{4,5},{7,6},{8,9},{11,10},{12,13},{15,14},{16,17},{19,... | collective-permute-start | bytes 3145736 | tf_op jit(solution)/shard_map/ppermute | solution.py:183
  66.5 5.5 %fusion.10 = bf16[2048,768]{1,0:T(8,128)(2,1)S(1)} fusion(bf16[512,2048]{1,0:T(8,128)(2,1)} %collective-permute-done.14, bf16[512,512]{1,0:T(8,128)(2,1)S(1)} %copy-done.15, bf16[512,512]{1,0:T(8,128)(2,1)S(1)} %copy-done.9, bf16[512,512]{1,0:T(8,128)(2,1)S(1)} %copy-done.11, bf16[512,512]{1,0:T(8,128)(2,1)S(1)} %copy-done.13, ...), kind=kOutput, calls=%fused_computation.10 | convolution fusion | flops 3246915584 | bytes 8912896 | tf_op jit(solution)/shard_map/dot_general | solution.py:25
  72.0 11.9 %collective-permute-done.19 = bf16[1024,512]{1,0:T(8,128)(2,1)S(1)} collective-permute-done((bf16[1024,512]{1,0:T(8,128)(2,1)S(1)}, bf16[1024,512]{1,0:T(8,128)(2,1)S(1)}, u32[]{:S(2)}, u32[]{:S(2)}) %collective-permute-start.19) | collective-permute-done | bytes 1048608 | tf_op jit(solution)/shard_map/ppermute | solution.py:183
  90.1 3.4 %fusion.28 = bf16[1024,512]{1,0:T(8,128)(2,1)} fusion(bf16[768,512]{1,0:T(8,128)(2,1)S(1)} %get-tuple-element.34, bf16[4,1024,768]{2,1,0:T(8,128)(2,1)} %bitcast.65, s32[]{:T(128)S(6)} %select_n.104), kind=kOutput, calls=%fused_computation.33 | convolution fusion | flops 805830656 | bytes 3407876 | tf_op jit(solution)/shard_map/dot_general | solution.py:25
  93.5 7.2 %collective-permute-start.12 = (bf16[1024,512]{1,0:T(8,128)(2,1)}, bf16[1024,512]{1,0:T(8,128)(2,1)}, u32[]{:S(2)}, u32[]{:S(2)}) collective-permute-start(bf16[1024,512]{1,0:T(8,128)(2,1)} %fusion.28), channel_id=1, source_target_pairs={{0,1},{3,2},{4,5},{7,6},{8,9},{11,10},{12,13},{15,14},{16,17},{19,... | collective-permute-start | bytes 3145736 | tf_op jit(solution)/shard_map/ppermute | solution.py:183
  102.7 2.4 %add_convert_fusion.5 = (bf16[256,768]{1,0:T(8,128)(2,1)}, bf16[256,768]{1,0:T(8,128)(2,1)}) fusion(bf16[256,768]{1,0:T(8,128)(2,1)} %collective-permute-done.17, bf16[2048,768]{1,0:T(8,128)(2,1)} %copy-done.7, bf16[256,768]{1,0:T(8,128)(2,1)} %collective-permute-done.16), kind=kLoop, calls=%fused_computation.48 | loop fusion | flops 1572864 | bytes 2359296 | tf_op jit(solution)/shard_map/convert_element_type | solution.py:316
  106.5 2.8 %add_convert_fusion.3 = bf16[1024,512]{1,0:T(8,128)(2,1)} fusion(bf16[1024,512]{1,0:T(8,128)(2,1)} %collective-permute-done.13, bf16[1024,512]{1,0:T(8,128)(2,1)} %fusion.31), kind=kLoop, calls=%fused_computation.15 | loop fusion | flops 2097152 | bytes 3145728 | tf_op jit(solution)/shard_map/convert_element_type | solution.py:183
  111.0 2.8 %add_convert_fusion.1 = bf16[1024,512]{1,0:T(8,128)(2,1)} fusion(bf16[1024,512]{1,0:T(8,128)(2,1)} %collective-permute-done.20, bf16[1024,512]{1,0:T(8,128)(2,1)} %fusion.28), kind=kLoop, calls=%fused_computation.13 | loop fusion | flops 2097152 | bytes 3145728 | tf_op jit(solution)/shard_map/convert_element_type | solution.py:183
  119.5 2.4 %fusion.22 = f32[1024,512]{1,0:T(8,128)S(1)} fusion(bf16[768,512]{1,0:T(8,128)(2,1)S(1)} %get-tuple-element.34, bf16[4,1024,768]{2,1,0:T(8,128)(2,1)} %bitcast.66, s32[]{:T(128)S(6)} %select_n.103), kind=kOutput, calls=%fused_computation.26 | convolution fusion | flops 805306368 | bytes 4456452 | tf_op jit(solution)/shard_map/dot_general | solution.py:25
  121.9 4.0 %collective-permute-done.23 = bf16[256,768]{1,0:T(8,128)(2,1)} collective-permute-done((bf16[256,768]{1,0:T(8,128)(2,1)}, bf16[256,768]{1,0:T(8,128)(2,1)}, u32[]{:S(2)}, u32[]{:S(2)}) %collective-permute-start.23) | collective-permute-done | bytes 393248 | tf_op jit(solution)/shard_map/ppermute | solution.py:168
  130.3 11.8 %collective-permute-done.21 = bf16[1024,512]{1,0:T(8,128)(2,1)} collective-permute-done((bf16[1024,512]{1,0:T(8,128)(2,1)}, bf16[1024,512]{1,0:T(8,128)(2,1)}, u32[]{:S(2)}, u32[]{:S(2)}) %collective-permute-start.21) | collective-permute-done | bytes 1048608 | tf_op jit(solution)/shard_map/ppermute | solution.py:183
  142.1 3.5 %add_convert_fusion = bf16[1024,512]{1,0:T(8,128)(2,1)} fusion(bf16[1024,512]{1,0:T(8,128)(2,1)} %collective-permute-done.21, bf16[1024,512]{1,0:T(8,128)(2,1)} %collective-permute-done.18, f32[1024,512]{1,0:T(8,128)S(1)} %fusion.22, bf16[1024,512]{1,0:T(8,128)(2,1)} %collective-permute-done.12), kind=kLoop, calls=%fused_computation.12 | loop fusion | flops 3670016 | bytes 6291456 | tf_op jit(solution)/shard_map/convert_element_type | solution.py:198
  (127 shorter events, 50.0 us)
Async XLA Ops:
  0.6 24.9 %collective-permute-start = (bf16[512,768]{1,0:T(8,128)(2,1)}, bf16[512,768]{1,0:T(8,128)(2,1)}, u32[]{:S(2)}, u32[]{:S(2)}) collective-permute-start(bf16[512,768]{1,0:T(8,128)(2,1)} %param.6), channel_id=1, source_target_pairs={{0,4},{4,0},{8,12},{12,8},{16,20},{20,16},{24,28},{28,24},{1,5},{5... | collective-permute-start | bytes 2359304 | tf_op jit(solution)/shard_map/ppermute | solution.py:168
  1.1 20.9 %collective-permute-start.1 = (bf16[512,768]{1,0:T(8,128)(2,1)}, bf16[512,768]{1,0:T(8,128)(2,1)S(1)}, u32[]{:S(2)}, u32[]{:S(2)}) collective-permute-start(bf16[512,768]{1,0:T(8,128)(2,1)} %param.6), channel_id=1, source_target_pairs={{0,8},{4,12},{8,0},{12,4},{16,24},{20,28},{24,16},{28,20},{1,9},{5... | collective-permute-start | bytes 2359304 | tf_op jit(solution)/shard_map/ppermute | solution.py:168
  3.7 20.2 %collective-permute-start.2 = (bf16[512,768]{1,0:T(8,128)(2,1)}, bf16[512,768]{1,0:T(8,128)(2,1)S(1)}, u32[]{:S(2)}, u32[]{:S(2)}) collective-permute-start(bf16[512,768]{1,0:T(8,128)(2,1)} %param.6), channel_id=1, source_target_pairs={{0,16},{4,20},{8,24},{12,28},{16,0},{20,4},{24,8},{28,12},{1,17},{... | collective-permute-start | bytes 2359304 | tf_op jit(solution)/shard_map/ppermute | solution.py:168
  10.7 55.7 %collective-permute-start.14 = (bf16[512,2048]{1,0:T(8,128)(2,1)}, bf16[512,2048]{1,0:T(8,128)(2,1)}, u32[]{:S(2)}, u32[]{:S(2)}) collective-permute-start(bf16[512,2048]{1,0:T(8,128)(2,1)} %pad_maximum_fusion), channel_id=1, source_target_pairs={{0,4},{4,0},{8,12},{12,8},{16,20},{20,16},{24,28},{28,24},{1,5},{5... | collective-permute-start | bytes 6291464 | tf_op jit(solution)/shard_map/ppermute | solution.py:168
  22.1 10.9 %collective-permute-start.5 = (bf16[256,768]{1,0:T(8,128)(2,1)S(1)}, bf16[256,768]{1,0:T(8,128)(2,1)S(1)}, u32[]{:S(2)}, u32[]{:S(2)}) collective-permute-start(bf16[256,768]{1,0:T(8,128)(2,1)S(1)} %slice.64), channel_id=1, source_target_pairs={{0,16},{4,20},{8,24},{12,28},{16,0},{20,4},{24,8},{28,12},{1,17},{... | collective-permute-start | bytes 1179656 | tf_op jit(solution)/shard_map/ppermute | solution.py:168
  24.0 10.5 %collective-permute-start.6 = (bf16[256,768]{1,0:T(8,128)(2,1)S(1)}, bf16[256,768]{1,0:T(8,128)(2,1)S(1)}, u32[]{:S(2)}, u32[]{:S(2)}) collective-permute-start(bf16[256,768]{1,0:T(8,128)(2,1)S(1)} %slice.65), channel_id=1, source_target_pairs={{0,8},{4,12},{8,0},{12,4},{16,24},{20,28},{24,16},{28,20},{1,9},{5... | collective-permute-start | bytes 1179656 | tf_op jit(solution)/shard_map/ppermute | solution.py:168
  25.5 9.6 %collective-permute-start.3 = (bf16[512,768]{1,0:T(8,128)(2,1)S(1)}, bf16[512,768]{1,0:T(8,128)(2,1)S(1)}, u32[]{:S(2)}, u32[]{:S(2)}) collective-permute-start(bf16[512,768]{1,0:T(8,128)(2,1)S(1)} %collective-permute-done.1), channel_id=1, source_target_pairs={{0,4},{4,0},{8,12},{12,8},{16,20},{20,16},{24,28},{28,24},{1,5},{5... | collective-permute-start | bytes 2359304 | tf_op jit(solution)/shard_map/ppermute | solution.py:168
  25.5 11.9 %collective-permute-start.4 = (bf16[512,768]{1,0:T(8,128)(2,1)S(1)}, bf16[512,768]{1,0:T(8,128)(2,1)S(1)}, u32[]{:S(2)}, u32[]{:S(2)}) collective-permute-start(bf16[512,768]{1,0:T(8,128)(2,1)S(1)} %collective-permute-done.2), channel_id=1, source_target_pairs={{0,4},{4,0},{8,12},{12,8},{16,20},{20,16},{24,28},{28,24},{1,5},{5... | collective-permute-start | bytes 2359304 | tf_op jit(solution)/shard_map/ppermute | solution.py:168
  41.8 9.1 %collective-permute-start.10 = (bf16[144,512]{1,0:T(8,128)(2,1)S(1)}, bf16[144,512]{1,0:T(8,128)(2,1)S(1)}, u32[]{:S(2)}, u32[]{:S(2)}) collective-permute-start(bf16[144,512]{1,0:T(8,128)(2,1)S(1)} %get-tuple-element.30), channel_id=1, source_target_pairs={{0,16},{4,20},{8,24},{12,28},{16,0},{20,4},{24,8},{28,12},{1,17},{... | collective-permute-start | bytes 442376 | tf_op jit(solution)/shard_map/ppermute | solution.py:168
  42.9 8.0 %collective-permute-start.11 = (bf16[144,512]{1,0:T(8,128)(2,1)S(1)}, bf16[144,512]{1,0:T(8,128)(2,1)S(1)}, u32[]{:S(2)}, u32[]{:S(2)}) collective-permute-start(bf16[144,512]{1,0:T(8,128)(2,1)S(1)} %get-tuple-element.30), channel_id=1, source_target_pairs={{0,24},{4,28},{8,16},{12,20},{16,8},{20,12},{24,0},{28,4},{1,25},{... | collective-permute-start | bytes 442376 | tf_op jit(solution)/shard_map/ppermute | solution.py:168
  44.8 7.3 %collective-permute-start.9 = (bf16[144,512]{1,0:T(8,128)(2,1)S(1)}, bf16[144,512]{1,0:T(8,128)(2,1)S(1)}, u32[]{:S(2)}, u32[]{:S(2)}) collective-permute-start(bf16[144,512]{1,0:T(8,128)(2,1)S(1)} %get-tuple-element.29), channel_id=1, source_target_pairs={{0,8},{4,12},{8,0},{12,4},{16,24},{20,28},{24,16},{28,20},{1,9},{5... | collective-permute-start | bytes 442376 | tf_op jit(solution)/shard_map/ppermute | solution.py:168
  54.5 12.0 %collective-permute-start.15 = (bf16[512,768]{1,0:T(8,128)(2,1)}, bf16[512,768]{1,0:T(8,128)(2,1)}, u32[]{:S(2)}, u32[]{:S(2)}) collective-permute-start(bf16[512,768]{1,0:T(8,128)(2,1)} %get-tuple-element.36), channel_id=1, source_target_pairs={{0,4},{4,0},{8,12},{12,8},{16,20},{20,16},{24,28},{28,24},{1,5},{5... | collective-permute-start | bytes 2359304 | tf_op jit(solution)/shard_map/ppermute | solution.py:168
  56.9 27.1 %collective-permute-start.19 = (bf16[1024,512]{1,0:T(8,128)(2,1)S(1)}, bf16[1024,512]{1,0:T(8,128)(2,1)S(1)}, u32[]{:S(2)}, u32[]{:S(2)}) collective-permute-start(bf16[1024,512]{1,0:T(8,128)(2,1)S(1)} %fusion.34), channel_id=1, source_target_pairs={{0,1},{3,2},{4,5},{7,6},{8,9},{11,10},{12,13},{15,14},{16,17},{19,... | collective-permute-start | bytes 3145736 | tf_op jit(solution)/shard_map/ppermute | solution.py:183
  64.1 42.4 %collective-permute-start.13 = (bf16[1024,512]{1,0:T(8,128)(2,1)}, bf16[1024,512]{1,0:T(8,128)(2,1)}, u32[]{:S(2)}, u32[]{:S(2)}) collective-permute-start(bf16[1024,512]{1,0:T(8,128)(2,1)} %fusion.31), channel_id=1, source_target_pairs={{0,1},{3,2},{4,5},{7,6},{8,9},{11,10},{12,13},{15,14},{16,17},{19,... | collective-permute-start | bytes 3145736 | tf_op jit(solution)/shard_map/ppermute | solution.py:183
  85.2 25.8 %collective-permute-start.20 = (bf16[1024,512]{1,0:T(8,128)(2,1)}, bf16[1024,512]{1,0:T(8,128)(2,1)}, u32[]{:S(2)}, u32[]{:S(2)}) collective-permute-start(bf16[1024,512]{1,0:T(8,128)(2,1)} %add_convert_fusion.2), channel_id=1, source_target_pairs={{1,2},{2,1},{5,6},{6,5},{9,10},{10,9},{13,14},{14,13},{17,18},{18,... | collective-permute-start | bytes 3145736 | tf_op jit(solution)/shard_map/ppermute | solution.py:183
  88.1 12.6 %collective-permute-start.16 = (bf16[256,768]{1,0:T(8,128)(2,1)}, bf16[256,768]{1,0:T(8,128)(2,1)}, u32[]{:S(2)}, u32[]{:S(2)}) collective-permute-start(bf16[256,768]{1,0:T(8,128)(2,1)} %get-tuple-element.56), channel_id=1, source_target_pairs={{0,16},{4,20},{8,24},{12,28},{16,0},{20,4},{24,8},{28,12},{1,17},{... | collective-permute-start | bytes 1179656 | tf_op jit(solution)/shard_map/ppermute | solution.py:168
  89.1 12.6 %collective-permute-start.17 = (bf16[256,768]{1,0:T(8,128)(2,1)}, bf16[256,768]{1,0:T(8,128)(2,1)}, u32[]{:S(2)}, u32[]{:S(2)}) collective-permute-start(bf16[256,768]{1,0:T(8,128)(2,1)} %get-tuple-element.55), channel_id=1, source_target_pairs={{0,8},{4,12},{8,0},{12,4},{16,24},{20,28},{24,16},{28,20},{1,9},{5... | collective-permute-start | bytes 1179656 | tf_op jit(solution)/shard_map/ppermute | solution.py:168
  93.5 36.8 %collective-permute-start.12 = (bf16[1024,512]{1,0:T(8,128)(2,1)}, bf16[1024,512]{1,0:T(8,128)(2,1)}, u32[]{:S(2)}, u32[]{:S(2)}) collective-permute-start(bf16[1024,512]{1,0:T(8,128)(2,1)} %fusion.28), channel_id=1, source_target_pairs={{0,1},{3,2},{4,5},{7,6},{8,9},{11,10},{12,13},{15,14},{16,17},{19,... | collective-permute-start | bytes 3145736 | tf_op jit(solution)/shard_map/ppermute | solution.py:183
  100.7 14.4 %collective-permute-start.22 = (bf16[256,768]{1,0:T(8,128)(2,1)S(1)}, bf16[256,768]{1,0:T(8,128)(2,1)S(1)}, u32[]{:S(2)}, u32[]{:S(2)}) collective-permute-start(bf16[256,768]{1,0:T(8,128)(2,1)S(1)} %copy-done.17), channel_id=1, source_target_pairs={{0,8},{4,12},{8,0},{12,4},{16,24},{20,28},{24,16},{28,20},{1,9},{5... | collective-permute-start | bytes 1179656 | tf_op jit(solution)/shard_map/ppermute | solution.py:168
  101.8 14.5 %collective-permute-start.24 = (bf16[256,768]{1,0:T(8,128)(2,1)S(1)}, bf16[256,768]{1,0:T(8,128)(2,1)S(1)}, u32[]{:S(2)}, u32[]{:S(2)}) collective-permute-start(bf16[256,768]{1,0:T(8,128)(2,1)S(1)} %copy-done.16), channel_id=1, source_target_pairs={{0,16},{4,20},{8,24},{12,28},{16,0},{20,4},{24,8},{28,12},{1,17},{... | collective-permute-start | bytes 1179656 | tf_op jit(solution)/shard_map/ppermute | solution.py:168
  109.3 21.0 %collective-permute-start.18 = (bf16[1024,512]{1,0:T(8,128)(2,1)}, bf16[1024,512]{1,0:T(8,128)(2,1)}, u32[]{:S(2)}, u32[]{:S(2)}) collective-permute-start(bf16[1024,512]{1,0:T(8,128)(2,1)} %add_convert_fusion.3), channel_id=1, source_target_pairs={{1,2},{2,1},{5,6},{6,5},{9,10},{10,9},{13,14},{14,13},{17,18},{18,... | collective-permute-start | bytes 3145736 | tf_op jit(solution)/shard_map/ppermute | solution.py:183
  113.8 28.2 %collective-permute-start.21 = (bf16[1024,512]{1,0:T(8,128)(2,1)}, bf16[1024,512]{1,0:T(8,128)(2,1)}, u32[]{:S(2)}, u32[]{:S(2)}) collective-permute-start(bf16[1024,512]{1,0:T(8,128)(2,1)} %add_convert_fusion.1), channel_id=1, source_target_pairs={{1,0},{2,3},{5,4},{6,7},{9,8},{10,11},{13,12},{14,15},{17,16},{18,... | collective-permute-start | bytes 3145736 | tf_op jit(solution)/shard_map/ppermute | solution.py:183
  115.1 10.8 %collective-permute-start.23 = (bf16[256,768]{1,0:T(8,128)(2,1)}, bf16[256,768]{1,0:T(8,128)(2,1)}, u32[]{:S(2)}, u32[]{:S(2)}) collective-permute-start(bf16[256,768]{1,0:T(8,128)(2,1)} %get-tuple-element.57), channel_id=1, source_target_pairs={{0,16},{4,20},{8,24},{12,28},{16,0},{20,4},{24,8},{28,12},{1,17},{... | collective-permute-start | bytes 1179656 | tf_op jit(solution)/shard_map/ppermute | solution.py:168
  117.0 10.4 %collective-permute-start.25 = (bf16[256,768]{1,0:T(8,128)(2,1)}, bf16[256,768]{1,0:T(8,128)(2,1)}, u32[]{:S(2)}, u32[]{:S(2)}) collective-permute-start(bf16[256,768]{1,0:T(8,128)(2,1)} %get-tuple-element.58), channel_id=1, source_target_pairs={{0,8},{4,12},{8,0},{12,4},{16,24},{20,28},{24,16},{28,20},{1,9},{5... | collective-permute-start | bytes 1179656 | tf_op jit(solution)/shard_map/ppermute | solution.py:168
  (26 other events, 144.2 us)

commit v5 on v4

--- a/solution.py
+++ b/solution.py
@@ -34,7 +34,7 @@
         in_specs=[pl.BlockSpec(memory_space=pltpu.SMEM)] * len(scalars)
         + [pl.BlockSpec(memory_space=pltpu.VMEM)] * len(args),
         out_specs=[pl.BlockSpec(memory_space=pltpu.VMEM)] * len(outs),
-        compiler_params=pltpu.CompilerParams(vmem_limit_bytes=14 * 2**20),
+        compiler_params=pltpu.CompilerParams(vmem_limit_bytes=40 * 2**20),
         cost_estimate=pl.CostEstimate(flops=flops, bytes_accessed=moved, transcendentals=0),
     )(*scalars, *args)
 
@@ -229,7 +229,7 @@
             axis=1,
         )
         to_near, to_keep = ordered[:, : 4 * part], ordered[:, 4 * part :]
-        chip_tokens = jnp.concatenate([to_keep, swap(to_near, size, 1)])
+        near_tokens = swap(to_near, size, 1)
         total = 0.0
         for bit, piece in pieces:
             at = (bit // 2 + (0 if bit % 2 else 4)) * part
@@ -304,7 +304,7 @@
         kept.append(swap(proj_grad, size, 1))
 
     def kept_products():
-        kept[0] = mm(chip_tokens, jnp.concatenate([proj_grad, kept[0]]), TN).astype(BF16)
+        kept[0] = (mm(to_keep, proj_grad, TN) + mm(near_tokens, kept[0], TN)).astype(BF16)
         own, for_x, for_y, for_corner = kept[0].reshape(4, part, columns)
         sent.extend((own, for_x, for_y, swap(for_corner[:half], size, 2), swap(for_corner[half:], size, 4)))
         sent.extend((swap(for_x[:half], size, 2), swap(for_y[half:], size, 4)))

time: 146 us -> 146 us (level)
  waiting for transfers between devices: 45.1 us -> 40.3 us
  local copies, waits for them, and re-layouts: 12.2 us -> 14.9 us
  matrix products: 23.7 us -> 25.3 us
    unnamed x50, local copies, waits for them, and re-layouts: 3.35 us -> 6.13 us
    ppermute x20, waiting for transfers between devices: 20 us -> 17.2 us  [swap(): return lax.ppermute(value, 'seq', [(i, i ^ bit) for i in range(size)])]
    ppermute x6, waiting for transfers between devices: 25.1 us -> 23.1 us  [send(): return lax.ppermute(value.astype(BF16), 'fsdp', pairs)]
    dot_general x13 -> x14, matrix products: 23.3 us -> 24.9 us  [mm(): return lax.dot_general(a, b, dims, preferred_element_type=F32)]
  transfers between devices with their start and end apart: 26 -> 26, of which waited for: 12 -> 12; matrix products, arithmetic and copies ran while one was open for 34% -> 35% of each run, Pallas kernels for 5% -> 5%
where the time goes in v5:
time: 146 us; the launch traced here: 145 us
  waiting for transfers between devices  40.3 us (28%)
  starting transfers between devices  36.6 us (25%)
  matrix products  25.3 us (17%)
  other arithmetic  19.3 us (13%)
  local copies, waits for them, and re-layouts  14.9 us (10%)
  Pallas kernels  7.73 us (5%)
    dot_general x14, matrix products, mm(): return lax.dot_general(a, b, dims, preferred_element_type=F32)  24.9 us
    ppermute x6, waiting for transfers between devices, send(): return lax.ppermute(value.astype(BF16), 'fsdp', pairs)  23.1 us
    ppermute x20, starting transfers between devices, swap(): return lax.ppermute(value, 'seq', [(i, i ^ bit) for i in range(size)])  18.6 us
    ppermute x6, starting transfers between devices, send(): return lax.ppermute(value.astype(BF16), 'fsdp', pairs)  18 us
    ppermute x20, waiting for transfers between devices, swap(): return lax.ppermute(value, 'seq', [(i, i ^ bit) for i in range(size)])  17.2 us
    pallas_call x5, Pallas kernels, call(): pl.pallas_call(kernel, out_shape=outs, in_specs=[pl.BlockSpec(memory_spac...  7.73 us
    convert_element_type x3, other arithmetic, send(): return lax.ppermute(value.astype(BF16), 'fsdp', pairs)  6.83 us
    unnamed x50, local copies, waits for them, and re-layouts  6.13 us
  transfers between devices with their start and end apart: 26, of which 12 were waited for; matrix products, arithmetic and copies ran while one was open for 35% of the time, Pallas kernels for 5%

profile of v5, /device:TPU:0, one launch (start us, length us, event | category | flops | bytes accessed | tf_op | source)
XLA Modules:
  0.0 145.3 jit_solution(12603793301853932945)
XLA Ops:
  1.1 2.6 %collective-permute-start.1 = (bf16[512,768]{1,0:T(8,128)(2,1)}, bf16[512,768]{1,0:T(8,128)(2,1)S(1)}, u32[]{:S(2)}, u32[]{:S(2)}) collective-permute-start(bf16[512,768]{1,0:T(8,128)(2,1)} %param.6), channel_id=1, source_target_pairs={{0,8},{4,12},{8,0},{12,4},{16,24},{20,28},{24,16},{28,20},{1,9},{5... | collective-permute-start | bytes 2359304 | tf_op jit(solution)/shard_map/ppermute | solution.py:168
  5.2 3.8 %constant_dynamic-slice_fusion.6 = (bf16[512,512]{1,0:T(8,128)(2,1)S(1)}, bf16[512,512]{1,0:T(8,128)(2,1)S(1)}, bf16[512,512]{1,0:T(8,128)(2,1)S(1)}, bf16[512,5...) fusion(bf16[512,4096]{1,0:T(8,128)(2,1)} %param.5, ...), kind=kLoop, calls=%fused_computation.67 | loop fusion | bytes 8388640 | tf_op jit(solution)/shard_map/dynamic_slice | solution.py:226
  17.6 4.5 %collective-permute-done.1 = bf16[512,768]{1,0:T(8,128)(2,1)S(1)} collective-permute-done((bf16[512,768]{1,0:T(8,128)(2,1)}, bf16[512,768]{1,0:T(8,128)(2,1)S(1)}, u32[]{:S(2)}, u32[]{:S(2)}) %collective-permute-start.1) | collective-permute-done | bytes 786464 | tf_op jit(solution)/shard_map/ppermute | solution.py:168
  30.7 2.3 %collective-permute-done.5 = bf16[256,768]{1,0:T(8,128)(2,1)S(1)} collective-permute-done((bf16[256,768]{1,0:T(8,128)(2,1)S(1)}, bf16[256,768]{1,0:T(8,128)(2,1)S(1)}, u32[]{:S(2)}, u32[]{:S(2)}) %collective-permute-start.5) | collective-permute-done | bytes 393248 | tf_op jit(solution)/shard_map/ppermute | solution.py:168
  42.8 1.9 %collective-permute-start.11 = (bf16[144,512]{1,0:T(8,128)(2,1)S(1)}, bf16[144,512]{1,0:T(8,128)(2,1)S(1)}, u32[]{:S(2)}, u32[]{:S(2)}) collective-permute-start(bf16[144,512]{1,0:T(8,128)(2,1)S(1)} %get-tuple-element.30), channel_id=1, source_target_pairs={{0,24},{4,28},{8,16},{12,20},{16,8},{20,12},{24,0},{28,4},{1,25},{... | collective-permute-start | bytes 442376 | tf_op jit(solution)/shard_map/ppermute | solution.py:168
  45.3 2.7 %copy-done.1 = bf16[8,512,768]{2,1,0:T(8,128)(2,1)} copy-done((bf16[8,512,768]{2,1,0:T(8,128)(2,1)}, bf16[8,512,768]{2,1,0:T(8,128)(2,1)S(1)}, u32[]{:S(2)}) %copy-start.1) | copy-done | bytes 6291480
  48.0 2.4 %shard_map.76 = (f32[512,512]{1,0:T(8,128)S(1)}, f32[512,512]{1,0:T(8,128)S(1)}, f32[512,128]{1,0:T(8,128)S(1)}, f32[512,128]{1,0:T(8,128)S(1)}, bf16[512,512]{1...) custom-call(bf16[512,768]{1,0:T(8,128)(2,1)S(1)} %add_convert_fusion.5.proj, bf16[512,512]{1,0:T(8,128)(2,1)S(1)} %copy-done, ...), custom_call_target="tpu_custom_call" | custom-call | flops 671088640 | bytes 5021696 | tf_op jit(solution)/shard_map/pallas_call | solution.py:31
  52.0 2.3 %shard_map.79 = (bf16[512,768]{1,0:T(8,128)(2,1)}, bf16[768,512]{1,0:T(8,128)(2,1)S(1)}, bf16[128,512]{1,0:T(8,128)(2,1)S(1)}) custom-call(s32[2]{0:T(128)S(1)} %pad_add_fusion.place, bf16[512,768]{1,0:T(8,128)(2,1)S(1)} %add_convert_fusion.5.proj, f32[512,4]{1,0:T(8,128)S(1)} %get-tuple-element.60.to_end, f32[512,512]{1,0:T(8,128)S(1)} %get-tuple-element.24.dx, ...), custom_call_target="tpu_custom_call" | custom-call | flops 201326592 | bytes 6119424 | tf_op jit(solution)/shard_map/pallas_call | solution.py:31
  54.3 2.4 %fusion.25 = bf16[1024,512]{1,0:T(8,128)(2,1)S(1)} fusion(bf16[768,512]{1,0:T(8,128)(2,1)S(1)} %get-tuple-element.34, bf16[4,1024,768]{2,1,0:T(8,128)(2,1)} %bitcast.66, s32[]{:T(128)S(6)} %select_n.106), kind=kOutput, calls=%fused_computation.29 | convolution fusion | flops 805830656 | bytes 3407876 | tf_op jit(solution)/shard_map/dot_general | solution.py:25
  56.7 3.7 %collective-permute-start.19 = (bf16[1024,512]{1,0:T(8,128)(2,1)S(1)}, bf16[1024,512]{1,0:T(8,128)(2,1)S(1)}, u32[]{:S(2)}, u32[]{:S(2)}) collective-permute-start(bf16[1024,512]{1,0:T(8,128)(2,1)S(1)} %fusion.25), channel_id=1, source_target_pairs={{0,1},{3,2},{4,5},{7,6},{8,9},{11,10},{12,13},{15,14},{16,17},{19,... | collective-permute-start | bytes 3145736 | tf_op jit(solution)/shard_map/ppermute | solution.py:183
  60.5 3.4 %fusion.22 = bf16[1024,512]{1,0:T(8,128)(2,1)} fusion(bf16[768,512]{1,0:T(8,128)(2,1)S(1)} %get-tuple-element.34, bf16[4,1024,768]{2,1,0:T(8,128)(2,1)} %bitcast.67, s32[]{:T(128)S(6)} %select_n.105), kind=kOutput, calls=%fused_computation.28 | convolution fusion | flops 805830656 | bytes 3407876 | tf_op jit(solution)/shard_map/dot_general | solution.py:25
  63.8 2.5 %collective-permute-start.13 = (bf16[1024,512]{1,0:T(8,128)(2,1)}, bf16[1024,512]{1,0:T(8,128)(2,1)}, u32[]{:S(2)}, u32[]{:S(2)}) collective-permute-start(bf16[1024,512]{1,0:T(8,128)(2,1)} %fusion.22), channel_id=1, source_target_pairs={{0,1},{3,2},{4,5},{7,6},{8,9},{11,10},{12,13},{15,14},{16,17},{19,... | collective-permute-start | bytes 3145736 | tf_op jit(solution)/shard_map/ppermute | solution.py:183
  66.3 3.6 %fusion.53 = f32[2048,768]{1,0:T(8,128)S(1)} fusion(bf16[512,2048]{1,0:T(8,128)(2,1)} %collective-permute-done.14, bf16[512,768]{1,0:T(8,128)(2,1)} %collective-permute-done.15), kind=kOutput, calls=%fused_computation.82 | convolution fusion | flops 1610612736 | bytes 9175040 | tf_op jit(solution)/shard_map/dot_general | solution.py:25
  70.0 3.7 %add_convert_fusion = bf16[2048,768]{1,0:T(8,128)(2,1)S(1)} fusion(f32[2048,768]{1,0:T(8,128)S(1)} %fusion.53, bf16[512,768]{1,0:T(8,128)(2,1)} %get-tuple-element.36, bf16[512,512]{1,0:T(8,128)(2,1)S(1)} %copy-done.15, bf16[512,512]{1,0:T(8,128)(2,1)S(1)} %copy-done.9, bf16[512,512]{1,0:T(8,128)(2,1)S(1)} %copy-done.11, bf16[512,512]{1,0:T(8,128)(2,1)S(1)} %copy-done.13), kind=kOutput, calls=%fused_computation | convolution fusion | flops 1622147072 | bytes 12320768 | tf_op jit(solution)/shard_map/dot_general | solution.py:25
  73.7 9.9 %collective-permute-done.19 = bf16[1024,512]{1,0:T(8,128)(2,1)S(1)} collective-permute-done((bf16[1024,512]{1,0:T(8,128)(2,1)S(1)}, bf16[1024,512]{1,0:T(8,128)(2,1)S(1)}, u32[]{:S(2)}, u32[]{:S(2)}) %collective-permute-start.19) | collective-permute-done | bytes 1048608 | tf_op jit(solution)/shard_map/ppermute | solution.py:183
  89.7 3.4 %fusion.19 = bf16[1024,512]{1,0:T(8,128)(2,1)} fusion(bf16[768,512]{1,0:T(8,128)(2,1)S(1)} %get-tuple-element.34, bf16[4,1024,768]{2,1,0:T(8,128)(2,1)} %bitcast.68, s32[]{:T(128)S(6)} %select_n.104), kind=kOutput, calls=%fused_computation.27 | convolution fusion | flops 805830656 | bytes 3407876 | tf_op jit(solution)/shard_map/dot_general | solution.py:25
  93.1 7.2 %collective-permute-start.12 = (bf16[1024,512]{1,0:T(8,128)(2,1)}, bf16[1024,512]{1,0:T(8,128)(2,1)}, u32[]{:S(2)}, u32[]{:S(2)}) collective-permute-start(bf16[1024,512]{1,0:T(8,128)(2,1)} %fusion.19), channel_id=1, source_target_pairs={{0,1},{3,2},{4,5},{7,6},{8,9},{11,10},{12,13},{15,14},{16,17},{19,... | collective-permute-start | bytes 3145736 | tf_op jit(solution)/shard_map/ppermute | solution.py:183
  102.4 2.4 %add_convert_fusion.6 = (bf16[256,768]{1,0:T(8,128)(2,1)}, bf16[256,768]{1,0:T(8,128)(2,1)}) fusion(bf16[256,768]{1,0:T(8,128)(2,1)} %collective-permute-done.17, bf16[2048,768]{1,0:T(8,128)(2,1)} %copy-done.7, bf16[256,768]{1,0:T(8,128)(2,1)} %collective-permute-done.16), kind=kLoop, calls=%fused_computation.42 | loop fusion | flops 1572864 | bytes 2359296 | tf_op jit(solution)/shard_map/convert_element_type | solution.py:316
  106.2 2.8 %add_convert_fusion.4 = bf16[1024,512]{1,0:T(8,128)(2,1)} fusion(bf16[1024,512]{1,0:T(8,128)(2,1)} %collective-permute-done.13, bf16[1024,512]{1,0:T(8,128)(2,1)} %fusion.22), kind=kLoop, calls=%fused_computation.12 | loop fusion | flops 2097152 | bytes 3145728 | tf_op jit(solution)/shard_map/convert_element_type | solution.py:183
  110.7 2.8 %add_convert_fusion.2 = bf16[1024,512]{1,0:T(8,128)(2,1)} fusion(bf16[1024,512]{1,0:T(8,128)(2,1)} %collective-permute-done.20, bf16[1024,512]{1,0:T(8,128)(2,1)} %fusion.19), kind=kLoop, calls=%fused_computation.10 | loop fusion | flops 2097152 | bytes 3145728 | tf_op jit(solution)/shard_map/convert_element_type | solution.py:183
  119.2 2.5 %fusion.13 = f32[1024,512]{1,0:T(8,128)S(1)} fusion(bf16[768,512]{1,0:T(8,128)(2,1)S(1)} %get-tuple-element.34, bf16[4,1024,768]{2,1,0:T(8,128)(2,1)} %bitcast.69, s32[]{:T(128)S(6)} %select_n.103), kind=kOutput, calls=%fused_computation.20 | convolution fusion | flops 805306368 | bytes 4456452 | tf_op jit(solution)/shard_map/dot_general | solution.py:25
  121.6 4.0 %collective-permute-done.23 = bf16[256,768]{1,0:T(8,128)(2,1)} collective-permute-done((bf16[256,768]{1,0:T(8,128)(2,1)}, bf16[256,768]{1,0:T(8,128)(2,1)}, u32[]{:S(2)}, u32[]{:S(2)}) %collective-permute-start.23) | collective-permute-done | bytes 393248 | tf_op jit(solution)/shard_map/ppermute | solution.py:168
  130.0 11.7 %collective-permute-done.21 = bf16[1024,512]{1,0:T(8,128)(2,1)} collective-permute-done((bf16[1024,512]{1,0:T(8,128)(2,1)}, bf16[1024,512]{1,0:T(8,128)(2,1)}, u32[]{:S(2)}, u32[]{:S(2)}) %collective-permute-start.21) | collective-permute-done | bytes 1048608 | tf_op jit(solution)/shard_map/ppermute | solution.py:183
  141.8 3.5 %add_convert_fusion.1 = bf16[1024,512]{1,0:T(8,128)(2,1)} fusion(bf16[1024,512]{1,0:T(8,128)(2,1)} %collective-permute-done.21, bf16[1024,512]{1,0:T(8,128)(2,1)} %collective-permute-done.18, f32[1024,512]{1,0:T(8,128)S(1)} %fusion.13, bf16[1024,512]{1,0:T(8,128)(2,1)} %collective-permute-done.12), kind=kLoop, calls=%fused_computation.9 | loop fusion | flops 3670016 | bytes 6291456 | tf_op jit(solution)/shard_map/convert_element_type | solution.py:198
  (128 shorter events, 52.2 us)
Async XLA Ops:
  0.6 24.9 %collective-permute-start = (bf16[512,768]{1,0:T(8,128)(2,1)}, bf16[512,768]{1,0:T(8,128)(2,1)}, u32[]{:S(2)}, u32[]{:S(2)}) collective-permute-start(bf16[512,768]{1,0:T(8,128)(2,1)} %param.6), channel_id=1, source_target_pairs={{0,4},{4,0},{8,12},{12,8},{16,20},{20,16},{24,28},{28,24},{1,5},{5... | collective-permute-start | bytes 2359304 | tf_op jit(solution)/shard_map/ppermute | solution.py:168
  1.1 20.9 %collective-permute-start.1 = (bf16[512,768]{1,0:T(8,128)(2,1)}, bf16[512,768]{1,0:T(8,128)(2,1)S(1)}, u32[]{:S(2)}, u32[]{:S(2)}) collective-permute-start(bf16[512,768]{1,0:T(8,128)(2,1)} %param.6), channel_id=1, source_target_pairs={{0,8},{4,12},{8,0},{12,4},{16,24},{20,28},{24,16},{28,20},{1,9},{5... | collective-permute-start | bytes 2359304 | tf_op jit(solution)/shard_map/ppermute | solution.py:168
  3.7 20.2 %collective-permute-start.2 = (bf16[512,768]{1,0:T(8,128)(2,1)}, bf16[512,768]{1,0:T(8,128)(2,1)S(1)}, u32[]{:S(2)}, u32[]{:S(2)}) collective-permute-start(bf16[512,768]{1,0:T(8,128)(2,1)} %param.6), channel_id=1, source_target_pairs={{0,16},{4,20},{8,24},{12,28},{16,0},{20,4},{24,8},{28,12},{1,17},{... | collective-permute-start | bytes 2359304 | tf_op jit(solution)/shard_map/ppermute | solution.py:168
  10.8 55.5 %collective-permute-start.14 = (bf16[512,2048]{1,0:T(8,128)(2,1)}, bf16[512,2048]{1,0:T(8,128)(2,1)}, u32[]{:S(2)}, u32[]{:S(2)}) collective-permute-start(bf16[512,2048]{1,0:T(8,128)(2,1)} %pad_maximum_fusion), channel_id=1, source_target_pairs={{0,4},{4,0},{8,12},{12,8},{16,20},{20,16},{24,28},{28,24},{1,5},{5... | collective-permute-start | bytes 6291464 | tf_op jit(solution)/shard_map/ppermute | solution.py:168
  22.1 10.9 %collective-permute-start.5 = (bf16[256,768]{1,0:T(8,128)(2,1)S(1)}, bf16[256,768]{1,0:T(8,128)(2,1)S(1)}, u32[]{:S(2)}, u32[]{:S(2)}) collective-permute-start(bf16[256,768]{1,0:T(8,128)(2,1)S(1)} %slice.64), channel_id=1, source_target_pairs={{0,16},{4,20},{8,24},{12,28},{16,0},{20,4},{24,8},{28,12},{1,17},{... | collective-permute-start | bytes 1179656 | tf_op jit(solution)/shard_map/ppermute | solution.py:168
  24.0 10.5 %collective-permute-start.6 = (bf16[256,768]{1,0:T(8,128)(2,1)S(1)}, bf16[256,768]{1,0:T(8,128)(2,1)S(1)}, u32[]{:S(2)}, u32[]{:S(2)}) collective-permute-start(bf16[256,768]{1,0:T(8,128)(2,1)S(1)} %slice.65), channel_id=1, source_target_pairs={{0,8},{4,12},{8,0},{12,4},{16,24},{20,28},{24,16},{28,20},{1,9},{5... | collective-permute-start | bytes 1179656 | tf_op jit(solution)/shard_map/ppermute | solution.py:168
  25.5 9.6 %collective-permute-start.3 = (bf16[512,768]{1,0:T(8,128)(2,1)S(1)}, bf16[512,768]{1,0:T(8,128)(2,1)S(1)}, u32[]{:S(2)}, u32[]{:S(2)}) collective-permute-start(bf16[512,768]{1,0:T(8,128)(2,1)S(1)} %collective-permute-done.1), channel_id=1, source_target_pairs={{0,4},{4,0},{8,12},{12,8},{16,20},{20,16},{24,28},{28,24},{1,5},{5... | collective-permute-start | bytes 2359304 | tf_op jit(solution)/shard_map/ppermute | solution.py:168
  25.5 11.9 %collective-permute-start.4 = (bf16[512,768]{1,0:T(8,128)(2,1)S(1)}, bf16[512,768]{1,0:T(8,128)(2,1)S(1)}, u32[]{:S(2)}, u32[]{:S(2)}) collective-permute-start(bf16[512,768]{1,0:T(8,128)(2,1)S(1)} %collective-permute-done.2), channel_id=1, source_target_pairs={{0,4},{4,0},{8,12},{12,8},{16,20},{20,16},{24,28},{28,24},{1,5},{5... | collective-permute-start | bytes 2359304 | tf_op jit(solution)/shard_map/ppermute | solution.py:168
  41.7 9.1 %collective-permute-start.10 = (bf16[144,512]{1,0:T(8,128)(2,1)S(1)}, bf16[144,512]{1,0:T(8,128)(2,1)S(1)}, u32[]{:S(2)}, u32[]{:S(2)}) collective-permute-start(bf16[144,512]{1,0:T(8,128)(2,1)S(1)} %get-tuple-element.30), channel_id=1, source_target_pairs={{0,16},{4,20},{8,24},{12,28},{16,0},{20,4},{24,8},{28,12},{1,17},{... | collective-permute-start | bytes 442376 | tf_op jit(solution)/shard_map/ppermute | solution.py:168
  42.8 8.0 %collective-permute-start.11 = (bf16[144,512]{1,0:T(8,128)(2,1)S(1)}, bf16[144,512]{1,0:T(8,128)(2,1)S(1)}, u32[]{:S(2)}, u32[]{:S(2)}) collective-permute-start(bf16[144,512]{1,0:T(8,128)(2,1)S(1)} %get-tuple-element.30), channel_id=1, source_target_pairs={{0,24},{4,28},{8,16},{12,20},{16,8},{20,12},{24,0},{28,4},{1,25},{... | collective-permute-start | bytes 442376 | tf_op jit(solution)/shard_map/ppermute | solution.py:168
  44.7 7.3 %collective-permute-start.9 = (bf16[144,512]{1,0:T(8,128)(2,1)S(1)}, bf16[144,512]{1,0:T(8,128)(2,1)S(1)}, u32[]{:S(2)}, u32[]{:S(2)}) collective-permute-start(bf16[144,512]{1,0:T(8,128)(2,1)S(1)} %get-tuple-element.29), channel_id=1, source_target_pairs={{0,8},{4,12},{8,0},{12,4},{16,24},{20,28},{24,16},{28,20},{1,9},{5... | collective-permute-start | bytes 442376 | tf_op jit(solution)/shard_map/ppermute | solution.py:168
  54.3 12.0 %collective-permute-start.15 = (bf16[512,768]{1,0:T(8,128)(2,1)}, bf16[512,768]{1,0:T(8,128)(2,1)}, u32[]{:S(2)}, u32[]{:S(2)}) collective-permute-start(bf16[512,768]{1,0:T(8,128)(2,1)} %get-tuple-element.36), channel_id=1, source_target_pairs={{0,4},{4,0},{8,12},{12,8},{16,20},{20,16},{24,28},{28,24},{1,5},{5... | collective-permute-start | bytes 2359304 | tf_op jit(solution)/shard_map/ppermute | solution.py:168
  56.7 26.9 %collective-permute-start.19 = (bf16[1024,512]{1,0:T(8,128)(2,1)S(1)}, bf16[1024,512]{1,0:T(8,128)(2,1)S(1)}, u32[]{:S(2)}, u32[]{:S(2)}) collective-permute-start(bf16[1024,512]{1,0:T(8,128)(2,1)S(1)} %fusion.25), channel_id=1, source_target_pairs={{0,1},{3,2},{4,5},{7,6},{8,9},{11,10},{12,13},{15,14},{16,17},{19,... | collective-permute-start | bytes 3145736 | tf_op jit(solution)/shard_map/ppermute | solution.py:183
  63.8 42.4 %collective-permute-start.13 = (bf16[1024,512]{1,0:T(8,128)(2,1)}, bf16[1024,512]{1,0:T(8,128)(2,1)}, u32[]{:S(2)}, u32[]{:S(2)}) collective-permute-start(bf16[1024,512]{1,0:T(8,128)(2,1)} %fusion.22), channel_id=1, source_target_pairs={{0,1},{3,2},{4,5},{7,6},{8,9},{11,10},{12,13},{15,14},{16,17},{19,... | collective-permute-start | bytes 3145736 | tf_op jit(solution)/shard_map/ppermute | solution.py:183
  84.9 25.8 %collective-permute-start.20 = (bf16[1024,512]{1,0:T(8,128)(2,1)}, bf16[1024,512]{1,0:T(8,128)(2,1)}, u32[]{:S(2)}, u32[]{:S(2)}) collective-permute-start(bf16[1024,512]{1,0:T(8,128)(2,1)} %add_convert_fusion.3), channel_id=1, source_target_pairs={{1,2},{2,1},{5,6},{6,5},{9,10},{10,9},{13,14},{14,13},{17,18},{18,... | collective-permute-start | bytes 3145736 | tf_op jit(solution)/shard_map/ppermute | solution.py:183
  87.7 12.6 %collective-permute-start.16 = (bf16[256,768]{1,0:T(8,128)(2,1)}, bf16[256,768]{1,0:T(8,128)(2,1)}, u32[]{:S(2)}, u32[]{:S(2)}) collective-permute-start(bf16[256,768]{1,0:T(8,128)(2,1)} %get-tuple-element.56), channel_id=1, source_target_pairs={{0,16},{4,20},{8,24},{12,28},{16,0},{20,4},{24,8},{28,12},{1,17},{... | collective-permute-start | bytes 1179656 | tf_op jit(solution)/shard_map/ppermute | solution.py:168
  88.8 12.6 %collective-permute-start.17 = (bf16[256,768]{1,0:T(8,128)(2,1)}, bf16[256,768]{1,0:T(8,128)(2,1)}, u32[]{:S(2)}, u32[]{:S(2)}) collective-permute-start(bf16[256,768]{1,0:T(8,128)(2,1)} %get-tuple-element.55), channel_id=1, source_target_pairs={{0,8},{4,12},{8,0},{12,4},{16,24},{20,28},{24,16},{28,20},{1,9},{5... | collective-permute-start | bytes 1179656 | tf_op jit(solution)/shard_map/ppermute | solution.py:168
  93.1 36.9 %collective-permute-start.12 = (bf16[1024,512]{1,0:T(8,128)(2,1)}, bf16[1024,512]{1,0:T(8,128)(2,1)}, u32[]{:S(2)}, u32[]{:S(2)}) collective-permute-start(bf16[1024,512]{1,0:T(8,128)(2,1)} %fusion.19), channel_id=1, source_target_pairs={{0,1},{3,2},{4,5},{7,6},{8,9},{11,10},{12,13},{15,14},{16,17},{19,... | collective-permute-start | bytes 3145736 | tf_op jit(solution)/shard_map/ppermute | solution.py:183
  100.3 14.5 %collective-permute-start.22 = (bf16[256,768]{1,0:T(8,128)(2,1)S(1)}, bf16[256,768]{1,0:T(8,128)(2,1)S(1)}, u32[]{:S(2)}, u32[]{:S(2)}) collective-permute-start(bf16[256,768]{1,0:T(8,128)(2,1)S(1)} %copy-done.17), channel_id=1, source_target_pairs={{0,8},{4,12},{8,0},{12,4},{16,24},{20,28},{24,16},{28,20},{1,9},{5... | collective-permute-start | bytes 1179656 | tf_op jit(solution)/shard_map/ppermute | solution.py:168
  101.5 14.5 %collective-permute-start.24 = (bf16[256,768]{1,0:T(8,128)(2,1)S(1)}, bf16[256,768]{1,0:T(8,128)(2,1)S(1)}, u32[]{:S(2)}, u32[]{:S(2)}) collective-permute-start(bf16[256,768]{1,0:T(8,128)(2,1)S(1)} %copy-done.16), channel_id=1, source_target_pairs={{0,16},{4,20},{8,24},{12,28},{16,0},{20,4},{24,8},{28,12},{1,17},{... | collective-permute-start | bytes 1179656 | tf_op jit(solution)/shard_map/ppermute | solution.py:168
  109.0 21.0 %collective-permute-start.18 = (bf16[1024,512]{1,0:T(8,128)(2,1)}, bf16[1024,512]{1,0:T(8,128)(2,1)}, u32[]{:S(2)}, u32[]{:S(2)}) collective-permute-start(bf16[1024,512]{1,0:T(8,128)(2,1)} %add_convert_fusion.4), channel_id=1, source_target_pairs={{1,2},{2,1},{5,6},{6,5},{9,10},{10,9},{13,14},{14,13},{17,18},{18,... | collective-permute-start | bytes 3145736 | tf_op jit(solution)/shard_map/ppermute | solution.py:183
  113.5 28.2 %collective-permute-start.21 = (bf16[1024,512]{1,0:T(8,128)(2,1)}, bf16[1024,512]{1,0:T(8,128)(2,1)}, u32[]{:S(2)}, u32[]{:S(2)}) collective-permute-start(bf16[1024,512]{1,0:T(8,128)(2,1)} %add_convert_fusion.2), channel_id=1, source_target_pairs={{1,0},{2,3},{5,4},{6,7},{9,8},{10,11},{13,12},{14,15},{17,16},{18,... | collective-permute-start | bytes 3145736 | tf_op jit(solution)/shard_map/ppermute | solution.py:183
  114.8 10.8 %collective-permute-start.23 = (bf16[256,768]{1,0:T(8,128)(2,1)}, bf16[256,768]{1,0:T(8,128)(2,1)}, u32[]{:S(2)}, u32[]{:S(2)}) collective-permute-start(bf16[256,768]{1,0:T(8,128)(2,1)} %get-tuple-element.57), channel_id=1, source_target_pairs={{0,16},{4,20},{8,24},{12,28},{16,0},{20,4},{24,8},{28,12},{1,17},{... | collective-permute-start | bytes 1179656 | tf_op jit(solution)/shard_map/ppermute | solution.py:168
  116.7 10.4 %collective-permute-start.25 = (bf16[256,768]{1,0:T(8,128)(2,1)}, bf16[256,768]{1,0:T(8,128)(2,1)}, u32[]{:S(2)}, u32[]{:S(2)}) collective-permute-start(bf16[256,768]{1,0:T(8,128)(2,1)} %get-tuple-element.58), channel_id=1, source_target_pairs={{0,8},{4,12},{8,0},{12,4},{16,24},{20,28},{24,16},{28,20},{1,9},{5... | collective-permute-start | bytes 1179656 | tf_op jit(solution)/shard_map/ppermute | solution.py:168
  (26 other events, 121.9 us)
